TPU v7x, 128 devices: a whole 4x4x4 slice. The times are simulated.
128 devices in a mesh: seq: 16 (over y_lo, x, core), tp: 8 (over z, y_hi).
Axes of the slice: x: 4, y: 4 (y_hi: 2, y_lo: 2; y = y_hi * 2 + y_lo), z: 4, core: 2. Of those that a mesh axis runs over, the one named last changes fastest.
Arguments:
- inputs: bfloat16 [16384, 4096], P('seq'), may hold values from -6 to 6
- w_query: bfloat16 [4096, 512], P(None, 'tp'), may hold values from -0.09375 to 0.09375
- w_key: bfloat16 [4096, 512], P(None, 'tp'), may hold values from -0.09375 to 0.09375
- w_value: bfloat16 [4096, 4096], P(None, 'tp'), may hold values from -0.09375 to 0.09375
- taps_query: float32 [3, 512], P(None, 'tp'), may hold values from -3 to 3
- taps_key: float32 [3, 512], P(None, 'tp'), may hold values from -3 to 3
- taps_value: float32 [3, 4096], P(None, 'tp'), may hold values from -3 to 3
- out_gain: float32 [4096], P('tp'), may hold values from 0.1 to 1.9
- out_grad: float32 [16384, 4096], P('seq', 'tp'), may hold values from -6 to 6
Outputs:
- outputs: float32 [16384, 4096], P('seq', 'tp')
- input_grad: bfloat16 [16384, 4096], P('seq', 'tp')
- grad_query: float32 [4096, 512], P('seq', 'tp')
- grad_key: float32 [4096, 512], P('seq', 'tp')
- grad_value: float32 [4096, 4096], P('seq', 'tp')
All inputs are finite; a program needn't handle non-finite values.
Results may differ from a plain program's by a relative error of at most 0.0049.
Values may be sent and summed in bfloat16 or wider, within the bound.
No kernel may reach another device: no remote copies, remote signals or barrier semaphores. Data moves between devices by JAX's collectives and lax.ppermute only.
A program may use at most 192 MiB of HBM per device.

v0:
```python
import math

import jax
import jax.numpy as jnp
from jax import lax
from jax.sharding import PartitionSpec as P

FEAT = 16
HDIM = 128


HIGHEST = lax.Precision.HIGHEST
ROOT_HALF = 1.0 / math.sqrt(2.0)
epsilon = 1e-05


def passed_along(x, axis, by):
    length = lax.axis_size(axis)
    pairs = [(i, i + by) for i in range(length) if 0 <= i + by < length]
    return lax.ppermute(x, axis, pairs)


def carried_in(value, axis, join, neutral, backward):
    count, mine = (lax.axis_size(axis), lax.axis_index(axis))
    pieces = jax.tree.map(lambda part: lax.all_gather(part, axis), value)
    if backward:
        pieces = jax.tree.map(lambda part: part[::-1], pieces)
        mine = count - 1 - mine
    subtotal = jax.tree.map(
        lambda part, zero: jnp.full_like(part, 0) + jnp.asarray(zero, part.dtype), value, neutral
    )

    def step(position, subtotal):
        longer = join(subtotal, jax.tree.map(lambda part: part[position], pieces))
        return jax.tree.map(lambda new, old: jnp.where(position < mine, new, old), longer, subtotal)

    return lax.fori_loop(0, count - 1, step, subtotal)


def conv_taps(proj, tail, taps):
    length = proj.shape[0]
    extended = jnp.concatenate([tail, proj], axis=0)
    return taps[0] * extended[2:] + taps[1] * extended[1 : length + 1] + taps[2] * extended[:length]


def attend(query_one, query_two, key_one, values, state):
    state_zero, state_one, state_two = state
    length = query_one.shape[0]
    carried = state_zero[None] + jnp.einsum("thf,hfd->thd", query_one, state_one, precision=HIGHEST)
    carried = carried + jnp.einsum("the,hed->thd", query_two, state_two, precision=HIGHEST)
    score = jnp.einsum("thf,uhf->htu", query_one, key_one, precision=HIGHEST)
    kernel = 1.0 + score + 0.5 * score * score
    causal = jnp.tril(jnp.ones((length, length), dtype=bool))
    kernel = jnp.where(causal[None], kernel, 0.0)
    inner = jnp.einsum("htu,uhd->thd", kernel, values, precision=HIGHEST)
    return carried + inner


def contrib(key_one, key_two, values):
    return (
        jnp.sum(values, axis=0),
        jnp.einsum("uhf,uhd->hfd", key_one, values, precision=HIGHEST),
        jnp.einsum("uhe,uhd->hed", key_two, values, precision=HIGHEST),
    )


def add_states(earlier, later):
    return tuple((a + b for a, b in zip(earlier, later)))


def local(inputs, w_query, w_key, w_value, taps_query, taps_key, taps_value, out_gain, out_grad):
    heads = w_value.shape[1] // HDIM
    length = inputs.shape[0]
    proj_q = jnp.dot(inputs, w_query, preferred_element_type=jnp.float32)
    proj_k = jnp.dot(inputs, w_key, preferred_element_type=jnp.float32)
    proj_v = jnp.dot(inputs, w_value, preferred_element_type=jnp.float32)
    tail_q, tail_k, tail_v = passed_along((proj_q[-2:], proj_k[-2:], proj_v[-2:]), "seq", 1)

    def feature_maps(proj_q, proj_k, proj_v, tail_q, tail_k, tail_v):
        conv_q = conv_taps(proj_q, tail_q, taps_query)
        conv_k = conv_taps(proj_k, tail_k, taps_key)
        conv_v = conv_taps(proj_v, tail_v, taps_value)
        query_one = conv_q.reshape(length, heads, FEAT) * 0.5
        key_one = conv_k.reshape(length, heads, FEAT) * 0.5
        query_two = (query_one[:, :, :, None] * query_one[:, :, None, :]).reshape(
            length, heads, FEAT * FEAT
        ) * ROOT_HALF
        key_two = (key_one[:, :, :, None] * key_one[:, :, None, :]).reshape(
            length, heads, FEAT * FEAT
        ) * ROOT_HALF
        return (query_one, query_two, key_one, key_two, conv_v.reshape(length, heads, HDIM))

    mapped, pull_maps = jax.vjp(feature_maps, proj_q, proj_k, proj_v, tail_q, tail_k, tail_v)
    query_one, query_two, key_one, key_two, values = mapped
    own_state, pull_own = jax.vjp(contrib, key_one, key_two, values)
    zero_state = tuple((jnp.zeros_like(part) for part in own_state))
    earlier = carried_in(own_state, "seq", add_states, zero_state, False)

    def normed(query_one, query_two, key_one, key_two, values, state):
        numer = attend(query_one, query_two, key_one, values, state)
        meansq = jnp.mean(numer * numer, axis=-1, keepdims=True)
        scaled = numer * lax.rsqrt(meansq + epsilon) * out_gain.reshape(heads, HDIM)
        return scaled.reshape(length, heads * HDIM)

    outputs, pull_out = jax.vjp(normed, query_one, query_two, key_one, key_two, values, earlier)
    grad_q1, grad_q2, grad_k1, grad_k2, grad_val, grad_state = pull_out(out_grad)
    later = carried_in(grad_state, "seq", add_states, zero_state, True)
    extra_k1, extra_k2, extra_val = pull_own(later)
    grad_pq, grad_pk, grad_pv, grad_tq, grad_tk, grad_tv = pull_maps(
        (grad_q1, grad_q2, grad_k1 + extra_k1, grad_k2 + extra_k2, grad_val + extra_val)
    )
    back_q, back_k, back_v = passed_along((grad_tq, grad_tk, grad_tv), "seq", -1)
    round_q = grad_pq.at[-2:].add(back_q).astype(jnp.bfloat16)
    round_k = grad_pk.at[-2:].add(back_k).astype(jnp.bfloat16)
    round_v = grad_pv.at[-2:].add(back_v).astype(jnp.bfloat16)
    all_grads = jnp.concatenate([round_q, round_k, round_v], axis=1)
    input_term = jnp.einsum("tc,dc->td", round_q, w_query, preferred_element_type=jnp.float32)
    input_term = input_term + jnp.einsum(
        "tc,dc->td", round_k, w_key, preferred_element_type=jnp.float32
    )
    input_term = input_term + jnp.einsum(
        "tc,dc->td", round_v, w_value, preferred_element_type=jnp.float32
    )
    input_grad = lax.psum_scatter(input_term, "tp", scatter_dimension=1, tiled=True).astype(
        jnp.bfloat16
    )
    width_q = w_query.shape[1]
    width_k = w_key.shape[1]
    summed = lax.psum_scatter(
        jnp.einsum("td,tc->dc", inputs, all_grads, preferred_element_type=jnp.float32),
        "seq",
        scatter_dimension=0,
        tiled=True,
    )
    grad_query = summed[:, :width_q]
    grad_key = summed[:, width_q : width_q + width_k]
    grad_value = summed[:, width_q + width_k :]
    return (outputs, input_grad, grad_query, grad_key, grad_value)


def solution(mesh):
    return jax.shard_map(
        local,
        mesh=mesh,
        in_specs=(
            P("seq", None),
            P(None, "tp"),
            P(None, "tp"),
            P(None, "tp"),
            P(None, "tp"),
            P(None, "tp"),
            P(None, "tp"),
            P("tp"),
            P("seq", "tp"),
        ),
        out_specs=(P("seq", "tp"), P("seq", "tp"), P("seq", "tp"), P("seq", "tp"), P("seq", "tp")),
        check_vma=False,
    )
```

profile of v0, /device:TPU:2, one launch (start us, length us, event | category | flops | bytes accessed | tf_op | source)
XLA Modules:
  0.0 671.8 jit_solution(16436691748603267659)
XLA Ops:
  7.2 8.3 %fusion.101 = f32[1024,512]{1,0:T(8,128)S(1)} fusion(bf16[1024,4096]{1,0:T(8,128)(2,1)} %param.19, bf16[4096,512]{1,0:T(8,128)(2,1)} %param.22), kind=kOutput, calls=%fused_computation.147 | convolution fusion | flops 4294967296 | bytes 14680064 | tf_op jit(solution)/shard_map/dot_general | solution.py:76
  15.6 1.9 collective-permute-start
  17.5 2.7 fusion.102
  20.3 3.5 collective-permute-start.1
  23.8 1.6 collective-permute-done.1
  27.1 1.3 copy-done.5
  28.4 4.6 fusion.26
  33.1 6.0 fusion.103
  39.2 2.3 collective-permute-start.2
  41.5 1.3 iota_compare_fusion
  42.8 2.9 copy.113
  45.6 1.5 fusion.79
  47.1 2.6 multiply_multiply_fusion.1
  49.8 15.8 %fusion.106 = f32[4,1024,1024]{2,1,0:T(8,128)} fusion(f32[1024,4,16]{0,2,1:T(8,128)S(1)} %bitcast.215, f32[1024,4,16]{0,2,1:T(8,128)S(1)} %bitcast.209), kind=kOutput, calls=%fused_computation.152 | convolution fusion | flops 805306368 | bytes 17301504 | tf_op jit(solution)/shard_map/jvp(thf,uhf->htu)/dot_general | solution.py:51
  65.6 17.2 %all_gather.35 = f32[16,4,128]{2,1,0:T(4,128)S(1)} all-gather(f32[1,4,128]{2,1,0:T(4,128)S(1)} %bitcast.233), channel_id=1, replica_groups=mesh['seq'=16,'tp'=8] {'seq'}, dimensions={0}, use_global_device_ids=true | all-gather | bytes 34816 | tf_op jit(solution)/shard_map/all_gather | solution.py:25
  84.0 22.2 %all-gather = f32[64,16,128]{2,1,0:T(8,128)} all-gather(f32[4,16,128]{2,1,0:T(8,128)S(1)} %fusion.24), channel_id=2, replica_groups=mesh['seq'=16,'tp'=8] {'seq'}, dimensions={0}, use_global_device_ids=true | all-gather | bytes 557056 | tf_op jit(solution)/shard_map/all_gather | solution.py:25
  106.2 30.3 %while.39 = (s32[]{:T(128)}, f32[4,128]{1,0:T(4,128)S(1)}, f32[4,16,128]{2,1,0:T(8,128)S(1)}, f32[4,256,128]{2,1,0:T(8,128)S(1)}, s32[]{:T(128)}, /*index=5*/f32...) while((s32[]{:T(128)}, f32[4,128]{1,0:T(4,128)S(1)}, ...), condition=%wide.region_2.3_spmd.clone, body=%wide.region_1.2_spmd.clone.sunk | while | flops 419332 | bytes 1677449 | solution.py:37
  108.2 1.2 add_select_fusion.14
  110.3 1.2 add_select_fusion.14
  112.3 1.2 add_select_fusion.14
  114.3 1.2 add_select_fusion.14
  136.5 3.0 fusion.104
  139.6 4.7 fusion.105
  144.3 24.0 %fusion.40 = (f32[1024,4]{0,1:T(4,128)S(1)}, f32[1024,4]{0,1:T(4,128)S(1)}, f32[4,128,1024]{2,1,0:T(8,128)S(1)}) fusion(f32[1024,512]{0,1:T(8,128)S(1)} %copy-done.17, f32[4,128]{1,0:T(4,128)S(1)} %bitcast.235, f32[4,1024,1024]{2,1,0:T(8,128)} %fusion.106, pred[1024,1024]{1,0:T(8,128)(4,1)S(1)} %copy-done.14, f32[4,128,1024]{2,1,0:T(8,128)S(1)} %fusion.105, ...), kind=kOutput, calls=%fused_computation.66 | convolution fusion | flops 6467608576 | bytes 28348416 | tf_op jit(solution)/shard_map/jvp(htu,uhd->thd)/dot_general | solution.py:55
  168.4 1.9 fusion.96
  170.3 1.3 copy-done.2
  171.6 4.6 fusion.30
  176.3 2.9 fusion.35
  179.3 4.6 convolution_multiply_fusion.1
  183.9 1.7 multiply_reduce_fusion.3
  185.6 22.8 %fusion.2 = f32[4,1024,1024]{2,1,0:T(8,128)} fusion(f32[4,1024,1024]{2,1,0:T(8,128)} %fusion.106, pred[1024,1024]{1,0:T(8,128)(4,1)S(1)} %copy-done.15, f32[1024,4,128]{0,2,1:T(8,128)S(1)} %copy-done.3, f32[1024,512]{1,0:T(8,128)S(1)} %get-tuple-element.444), kind=kOutput, calls=%fused_computation.10 | convolution fusion | flops 6471811072 | bytes 38797312 | tf_op jit(solution)/shard_map/transpose(jvp(htu,uhd->thd))/dot_general | solution.py:55
  208.4 19.7 %fusion.59 = f32[1024,4,16]{0,2,1:T(8,128)S(1)} fusion(f32[1024,4,16]{0,2,1:T(8,128)S(1)} %get-tuple-element.408, f32[1024,4,16]{0,2,1:T(8,128)S(1)} %get-tuple-element.407, f32[4,1024,16]{1,2,0:T(8,128)S(1)} %fusion.35, f32[4,1024,1024]{2,1,0:T(8,128)} %fusion.2, f32[1024,4,16]{0,2,1:T(8,128)S(1)} %bitcast.211), kind=kOutput, calls=%fused_computation.85 | convolution fusion | flops 805568512 | bytes 18087936 | tf_op jit(solution)/shard_map/transpose(jvp(thf,uhf->htu))/dot_general | solution.py:51
  229.1 2.9 collective-permute-start.3
  232.8 1.9 fusion.32
  234.7 19.1 %all-gather.3 = f32[64,16,128]{2,1,0:T(8,128)} all-gather(f32[4,16,128]{2,1,0:T(8,128)S(1)} %fusion.32), channel_id=5, replica_groups=mesh['seq'=16,'tp'=8] {'seq'}, dimensions={0}, use_global_device_ids=true | all-gather | bytes 557056 | tf_op jit(solution)/shard_map/all_gather | solution.py:25
  253.8 9.6 %convolution_bitcast_fusion.1 = f32[1024,4,16]{0,2,1:T(8,128)} fusion(f32[4,1024,1024]{2,1,0:T(8,128)S(1)} %copy-done.1, f32[1024,4,16]{0,2,1:T(8,128)S(1)} %bitcast.219), kind=kOutput, calls=%fused_computation.80 | convolution fusion | flops 805306368 | bytes 17301504 | tf_op jit(solution)/shard_map/transpose(jvp(thf,uhf->htu))/dot_general | solution.py:51
  263.5 17.4 %fusion.3 = f32[4,128,1024]{2,1,0:T(8,128)} fusion(f32[4,1024,1024]{2,1,0:T(8,128)} %fusion.106, pred[1024,1024]{1,0:T(8,128)(4,1)S(1)} %copy-done.15, f32[1024,4,128]{0,2,1:T(8,128)S(1)} %copy-done.3), kind=kOutput, calls=%fused_computation.12 | convolution fusion | flops 6463422464 | bytes 22020096 | tf_op jit(solution)/shard_map/transpose(jvp(htu,uhd->thd))/dot_general | solution.py:55
  280.9 17.6 %all-gather.5 = f32[16,4,128]{2,1,0:T(4,128)S(1)} all-gather(f32[1,4,128]{2,1,0:T(4,128)S(1)} %bitcast.234), channel_id=4, replica_groups=mesh['seq'=16,'tp'=8] {'seq'}, dimensions={0}, use_global_device_ids=true | all-gather | bytes 34816 | tf_op jit(solution)/shard_map/all_gather | solution.py:25
  298.5 1.9 rev.10
  300.3 1.7 split.24
  302.9 1.4 scatter-add.10
  304.3 1.8 copy.121
  306.1 7.7 %rev.11 = f32[16,4,256,128]{3,2,1,0:T(8,128)} reverse(f32[16,4,256,128]{3,2,1,0:T(8,128)} %bitcast.220), dimensions={0} | reverse | bytes 16777216 | tf_op jit(solution)/shard_map/rev | solution.py:27
  313.8 30.5 %while.40 = (s32[]{:T(128)}, f32[4,128]{1,0:T(4,128)S(1)}, f32[4,16,128]{2,1,0:T(8,128)S(1)}, f32[4,256,128]{2,1,0:T(8,128)S(1)}, s32[]{:T(128)}, /*index=5*/f32...) while((s32[]{:T(128)}, f32[4,128]{1,0:T(4,128)S(1)}, ...), condition=%wide.region_9.10_spmd.clone, body=%wide.region_8.9_spmd.clone.sunk | while | flops 419332 | bytes 1677449 | solution.py:37
  344.3 1.8 fusion.109
  346.1 3.7 convolution_multiply_fusion
  349.8 1.8 multiply_reduce_fusion.1
  351.7 1.9 fusion.72
  355.4 2.7 add_add_fusion.2
  358.2 2.1 copy.130
  360.2 2.4 broadcast_multiply_fusion
  362.7 2.2 collective-permute-start.4
  366.4 2.2 collective-permute-start.5
  370.6 1.4 fusion.88
  372.0 11.0 %convolution_bitcast_fusion = f32[4096,640]{0,1:T(8,128)} fusion(bf16[1024,4096]{1,0:T(8,128)(2,1)} %param.19, bf16[1024,512]{1,0:T(8,128)(2,1)} %fusion.88, bf16[1024,64]{1,0:T(8,128)(2,1)S(1)} %copy.122, bf16[1024,64]{1,0:T(8,128)(2,1)S(1)} %copy-done.31), kind=kOutput, calls=%fused_computation.22 | convolution fusion | flops 5372641280 | bytes 20185088 | tf_op jit(solution)/shard_map/td,tc->dc/dot_general | solution.py:130
  383.9 8.1 %fusion.107 = f32[1024,4096]{1,0:T(8,128)} fusion(bf16[1024,64]{0,1:T(8,128)(2,1)S(1)} %copy-done.29, bf16[4096,64]{0,1:T(8,128)(2,1)S(1)} %copy-done), kind=kOutput, calls=%fused_computation.153 | convolution fusion | flops 536870912 | bytes 17432576 | tf_op jit(solution)/shard_map/tc,dc->td/dot_general | solution.py:117
  392.0 8.6 %fusion.108 = f32[1024,4096]{1,0:T(8,128)} fusion(bf16[1024,64]{0,1:T(8,128)(2,1)S(1)} %scatter-add.11, bf16[4096,64]{0,1:T(8,128)(2,1)S(1)} %copy-done.26), kind=kOutput, calls=%fused_computation.154 | convolution fusion | flops 536870912 | bytes 17432576 | tf_op jit(solution)/shard_map/tc,dc->td/dot_general | solution.py:118
  400.6 20.5 %add_add_fusion = f32[1024,4096]{1,0:T(8,128)} fusion(f32[1024,4096]{1,0:T(8,128)} %fusion.107, f32[1024,4096]{1,0:T(8,128)} %fusion.108, bf16[1024,512]{1,0:T(8,128)(2,1)S(1)} %copy-done.13, bf16[4096,512]{1,0:T(8,128)(2,1)} %param.22), kind=kOutput, calls=%fused_computation.11 | convolution fusion | flops 4303355904 | bytes 55574528 | tf_op jit(solution)/shard_map/tc,dc->td/dot_general | solution.py:121
  421.1 1.6 copy-done.16
  422.7 1.8 copy.123
  424.5 36.7 %reduce-scatter.5.cloned.1.call-done = f32[256,640]{0,1:T(8,128)} async-done(((f32[4096,640]{0,1:T(8,128)}), f32[256,640]{0,1:T(8,128)}) %reduce-scatter.5.cloned.1.call-update) | async-done | bytes 655376 | tf_op jit(solution)/shard_map/reduce_scatter | solution.py:129
  463.3 1.5 fusion.99
  464.8 197.3 %reduce-scatter.3.cloned.1.call-done = f32[1024,512]{1,0:T(8,128)} async-done(((f32[1024,4096]{1,0:T(8,128)}), f32[1024,512]{1,0:T(8,128)}) %reduce-scatter.3.cloned.1.call-update) | async-done | bytes 2097168 | tf_op jit(solution)/shard_map/reduce_scatter | solution.py:124
  662.1 2.7 convert_element_type.15
  (218 shorter events, 69.1 us)
Async XLA Ops:
  7.2 25.9 %copy-start = (bf16[4096,64]{0,1:T(8,128)(2,1)S(1)}, bf16[4096,64]{0,1:T(8,128)(2,1)}, u32[]{:S(2)}) copy-start(bf16[4096,64]{0,1:T(8,128)(2,1)} %param.20) | copy-start | bytes 1572868
  7.2 10.3 %copy-start.25 = (bf16[4096,64]{0,1:T(8,128)(2,1)S(1)}, bf16[4096,64]{0,1:T(8,128)(2,1)}, u32[]{:S(2)}) copy-start(bf16[4096,64]{0,1:T(8,128)(2,1)} %param.21) | copy-start | bytes 1572868
  7.2 99.0 %all-gather.9.cloned.1.call-start = ((), (), s32[]{:S(2)}) async-start(), calls=%async_computation.4 | async-start | bytes 8912896 | tf_op jit(solution)/shard_map/all_gather | solution.py:25
  7.2 10.3 %copy-start.4 = (bf16[1024,4096]{1,0:T(8,128)(2,1)S(1)}, bf16[1024,4096]{1,0:T(8,128)(2,1)}, u32[]{:S(2)}) copy-start(bf16[1024,4096]{1,0:T(8,128)(2,1)} %param.19) | copy-start | bytes 25165828
  15.5 8.2 %copy-start.39 = (f32[3,512]{1,0:T(4,128)S(1)}, f32[3,512]{1,0:T(4,128)}, u32[]{:S(2)}) copy-start(f32[3,512]{1,0:T(4,128)} %param.25) | copy-start | bytes 18436
  15.6 8.2 %copy-start.41 = (f32[3,64]{1,0:T(4,128)S(1)}, f32[3,64]{1,0:T(4,128)}, u32[]{:S(2)}) copy-start(f32[3,64]{1,0:T(4,128)} %param.24) | copy-start | bytes 2308
  15.6 10.8 %collective-permute-start = (f32[2,512]{1,0:T(2,128)S(1)}, f32[2,512]{1,0:T(2,128)S(1)}, u32[]{:S(2)}, u32[]{:S(2)}) collective-permute-start(f32[2,512]{1,0:T(2,128)S(1)} %slice.147), channel_id=1, source_target_pairs={{0,8},{8,16},{16,24},{24,32},{32,40},{40,48},{48,56},{56,64},{64,7... | collective-permute-start | bytes 12296 | tf_op jit(solution)/shard_map/ppermute | solution.py:20
  20.3 5.2 collective-permute-start.1
  23.8 2.5 copy-start.33
  23.8 2.5 copy-start.35
  23.8 2.5 copy-start.37
  26.4 2.0 copy-start.5
  33.0 9.8 %copy-start.42 = (f32[3,64]{1,0:T(4,128)S(1)}, f32[3,64]{1,0:T(4,128)}, u32[]{:S(2)}) copy-start(f32[3,64]{1,0:T(4,128)} %param.23) | copy-start | bytes 2308
  33.0 273.1 %all-gather.11.cloned.1.call-start = ((), (), s32[]{:S(2)}) async-start(), calls=%async_computation.5 | async-start | bytes 8912896 | tf_op jit(solution)/shard_map/all_gather | solution.py:25
  39.1 2.4 copy-start.28
  39.2 6.5 collective-permute-start.2
  47.1 2.6 copy-start.11
  136.5 7.8 %copy-start.10 = (f32[4,256,128]{2,1,0:T(8,128)}, f32[4,256,128]{2,1,0:T(8,128)S(1)}, u32[]{:S(2)}) copy-start(f32[4,256,128]{2,1,0:T(8,128)S(1)} %get-tuple-element.325) | copy-start | bytes 1572868
  139.5 4.8 copy-start.14
  139.5 4.8 copy-start.17
  139.6 4.8 copy-start.40
  168.4 3.2 copy-start.7
  170.3 1.3 copy-start.2
  176.2 285.0 %reduce-scatter.5.cloned.1.call-start = ((), (), s32[]{:S(2)}) async-start(), calls=%async_computation.3 | async-start | bytes 11141120 | tf_op jit(solution)/shard_map/reduce_scatter | solution.py:129
  176.3 2.9 copy-start.3
  179.3 4.6 copy-start.12
  183.9 1.7 copy-start.15
  208.4 45.4 %copy-start.1 = (f32[4,1024,1024]{2,1,0:T(8,128)S(1)}, f32[4,1024,1024]{2,1,0:T(8,128)}, u32[]{:S(2)}) copy-start(f32[4,1024,1024]{2,1,0:T(8,128)} %fusion.2) | copy-start | bytes 50331652
  228.2 25.6 %copy-start.22 = (f32[1024,64]{0,1:T(8,128)}, f32[1024,64]{0,1:T(8,128)S(1)}, u32[]{:S(2)}) copy-start(f32[1024,64]{0,1:T(8,128)S(1)} %get-tuple-element.454) | copy-start | bytes 786436
  228.2 25.6 %copy-start.23 = (f32[1024,64]{0,1:T(8,128)}, f32[1024,64]{0,1:T(8,128)S(1)}, u32[]{:S(2)}) copy-start(f32[1024,64]{0,1:T(8,128)S(1)} %get-tuple-element.455) | copy-start | bytes 786436
  228.2 25.6 %copy-start.24 = (f32[1024,64]{0,1:T(8,128)}, f32[1024,64]{0,1:T(8,128)S(1)}, u32[]{:S(2)}) copy-start(f32[1024,64]{0,1:T(8,128)S(1)} %get-tuple-element.456) | copy-start | bytes 786436
  229.1 73.0 %collective-permute-start.3 = (f32[2,64]{0,1:T(8,128)}, f32[2,64]{0,1:T(8,128)S(1)}, u32[]{:S(2)}, u32[]{:S(2)}) collective-permute-start(f32[2,64]{0,1:T(8,128)} %pad_add_fusion.4), channel_id=1, source_target_pairs={{8,0},{16,8},{24,16},{32,24},{40,32},{48,40},{56,48},{64,56},{72,6... | collective-permute-start | bytes 1544 | tf_op jit(solution)/shard_map/ppermute | solution.py:20
  349.8 1.9 copy-start.30
  349.8 5.6 copy-start.27
  351.6 1.9 copy-start.34
  351.7 1.9 copy-start.36
  351.7 1.9 copy-start.38
  351.7 3.7 copy-start.6
  353.7 4.4 copy-start.18
  353.7 4.4 copy-start.20
  362.7 3.1 copy-start.8
  362.7 3.1 copy-start.9
  362.7 7.2 %collective-permute-start.4 = (f32[2,64]{0,1:T(8,128)}, f32[2,64]{0,1:T(8,128)S(1)}, u32[]{:S(2)}, u32[]{:S(2)}) collective-permute-start(f32[2,64]{0,1:T(8,128)} %pad_add_fusion.3), channel_id=1, source_target_pairs={{8,0},{16,8},{24,16},{32,24},{40,32},{48,40},{56,48},{64,56},{72,6... | collective-permute-start | bytes 1544 | tf_op jit(solution)/shard_map/ppermute | solution.py:20
  366.4 3.5 copy-start.32
  366.4 3.6 copy-start.19
  366.4 3.6 copy-start.21
  366.4 4.2 collective-permute-start.5
  370.6 1.4 copy-start.31
  383.0 0.9 copy-start.29
  383.0 9.0 %copy-start.26 = (bf16[4096,64]{0,1:T(8,128)(2,1)S(1)}, bf16[4096,64]{0,1:T(8,128)(2,1)}, u32[]{:S(2)}) copy-start(bf16[4096,64]{0,1:T(8,128)(2,1)} %param.21) | copy-start | bytes 1572868
  383.0 279.1 %reduce-scatter.3.cloned.1.call-start = ((), (), s32[]{:S(2)}) async-start(), calls=%async_computation.2 | async-start | bytes 18874368 | tf_op jit(solution)/shard_map/reduce_scatter | solution.py:124
  392.0 8.6 %copy-start.13 = (bf16[1024,512]{1,0:T(8,128)(2,1)S(1)}, bf16[1024,512]{1,0:T(8,128)(2,1)}, u32[]{:S(2)}) copy-start(bf16[1024,512]{1,0:T(8,128)(2,1)} %fusion.88) | copy-start | bytes 3145732
  421.1 1.6 copy-start.16
Sparse Core Ops, SparseCore 0:
  33.1 54.4 all-gather.8
  176.4 52.6 all-gather.10
  383.1 78.0 reduce-scatter.4
  465.0 197.0 reduce-scatter.2
where the time goes:
time: 684 us; the launch traced here: 672 us
  waiting for transfers between devices  236 us (35%)
  matrix products  212 us (31%)
  other arithmetic  84.8 us (12%)
  blocking collectives  76.2 us (11%)
  local copies, waits for them, and re-layouts  32 us (5%)
  starting transfers between devices  15.2 us (2%)
  between operations  15.1 us (2%)
    reduce_scatter x1, waiting for transfers between devices, local(): lax.psum_scatter(input_term, 'tp', scatter_dimension=1, tiled=True)  197 us
    all_gather x4, blocking collectives, carried_in(): pieces = jax.tree.map(lambda part: lax.all_gather(part, axis), value)  76.2 us
    dot_general x3, matrix products, attend(): inner = jnp.einsum('htu,uhd->thd', kernel, values, precision=HIGHEST)  64.2 us
    select_n x90, other arithmetic, step(): jnp.where(position < mine, new, old)  60 us
    dot_general x3, matrix products, attend(): score = jnp.einsum('thf,uhf->htu', query_one, key_one, precision=HIGHEST)  45.1 us
    reduce_scatter x1, waiting for transfers between devices, local(): lax.psum_scatter(jnp.einsum('td,tc->dc', inputs, all_grads, preferred_ele...  36.7 us
    dot_general x1, matrix products, local(): jnp.einsum('tc,dc->td', round_v, w_value, preferred_element_type=jnp.floa...  20.5 us
    ppermute x6, starting transfers between devices, passed_along(): return lax.ppermute(x, axis, pairs)  15 us
  transfers between devices with their start and end apart: 10, of which 3 were waited for; matrix products, arithmetic and copies ran while one was open for 25% of the time, Pallas kernels for 0%

commit v1 on v0

v1 whole, which is shorter than its diff:
```python
import functools

import jax
import jax.numpy as jnp
import numpy as np
from jax import lax
from jax.experimental import pallas as pl
from jax.experimental.pallas import tpu as pltpu
from jax.sharding import PartitionSpec as P

FEAT = 16
HDIM = 128
HEADS = 4
CHUNK = 256
LEN = 1024
CHUNKS = LEN // CHUNK
NF = 160
WIDE = 256
EPS = 1e-05
F32, BF16 = jnp.float32, jnp.bfloat16


def feature_matrices():
    pairs = [(i, j) for i in range(FEAT) for j in range(i, FEAT)]
    pick = np.zeros((2, HEADS, 64, 2 * WIDE), np.float32)
    bias = np.zeros((1, 2 * WIDE), np.float32)
    for head in range(HEADS):
        base = head * FEAT
        for f, (i, j) in enumerate(pairs):
            pick[:, head, base + i, f] = 1.0
            pick[0, head, base + j, WIDE + f] = 0.5 if i == j else 1.0
            pick[1, head, base + j, WIDE + f] = 1.0
        for i in range(FEAT):
            pick[:, head, base + i, len(pairs) + i] = 1.0
    ones = len(pairs) + FEAT
    bias[0, ones] = 1.0
    bias[0, WIDE + len(pairs) : WIDE + ones + 1] = 1.0
    packed = np.zeros((2, HEADS, WIDE, 2 * WIDE), np.float32)
    packed[0, :, 0:64] = pick[0]
    packed[0, :, 64:128] = pick[0]
    packed[1, :, 0:64] = pick[1]
    packed[1, :, 128:192] = pick[1]
    back = np.zeros((2, HEADS, 2 * WIDE, 128), np.float32)
    back[:, :, :, 0:64] = pick.transpose(0, 1, 3, 2)
    return packed, bias, back


def nn(a, b):
    return lax.dot_general(a, b, (((1,), (0,)), ((), ())), preferred_element_type=F32)


def nt(a, b):
    return lax.dot_general(a, b, (((1,), (1,)), ((), ())), preferred_element_type=F32)


def halves(x):
    hi = x.astype(BF16)
    return hi, (x - hi.astype(F32)).astype(BF16)


def side(*parts):
    return jnp.concatenate(parts, axis=1)


def nn3(a_hi, a_lo, b_hi, b_lo):
    both = nn(a_hi, side(b_hi, b_lo))
    n = b_hi.shape[1]
    return both[:, :n] + both[:, n:] + nn(a_lo, b_hi)


def nt3(a_hi, a_lo, b_hi, b_lo):
    return nt(side(a_hi, a_lo), side(b_hi, b_hi)) + nt(a_hi, b_lo)


def factors(packed, pick, bias):
    both = nn(packed, pick) + bias
    return both[:, :WIDE], both[:, WIDE:]


def padded(state):
    return jnp.concatenate([state, jnp.zeros((WIDE - NF, HDIM), F32)], axis=0)


def head_mask(width, head):
    lane = lax.broadcasted_iota(jnp.int32, (1, width), 1)
    return (lane % 64) // FEAT == head


def cols(head):
    return slice(head * HDIM, (head + 1) * HDIM)


def call(body, grid, ins, outs, shapes, args, scratch=(), prefetch=0, flops=0, moved=0):
    return pl.pallas_call(
        body,
        grid_spec=pltpu.PrefetchScalarGridSpec(
            num_scalar_prefetch=prefetch, grid=grid, in_specs=ins, out_specs=outs, scratch_shapes=list(scratch)
        ),
        out_shape=shapes,
        compiler_params=pltpu.CompilerParams(vmem_limit_bytes=56 * 2**20),
        cost_estimate=pl.CostEstimate(flops=int(flops), bytes_accessed=int(moved), transcendentals=0),
    )(*args)


def full(*shape):
    return pl.BlockSpec(shape, lambda *_: (0,) * len(shape))


def arr(shape, dtype=F32):
    return jax.ShapeDtypeStruct(shape, dtype)


def project_kernel(x_ref, wq_ref, wk_ref, wv_ref, qk_ref, v_ref, wqk):
    @pl.when(pl.program_id(0) == 0)
    def _():
        wqk[0:64] = wq_ref[...]
        wqk[64:128] = wk_ref[...]

    x = x_ref[...]
    qk_ref[...] = nt(x, wqk[...])
    v_ref[...] = nn(x, wv_ref[...])


def project(x, wq_t, wk_t, wv):
    depth = x.shape[1]
    rows = lambda c: (c, 0)
    return call(
        project_kernel,
        (CHUNKS,),
        [pl.BlockSpec((CHUNK, depth), rows), full(64, depth), full(64, depth), full(depth, 512)],
        [pl.BlockSpec((CHUNK, 128), rows), pl.BlockSpec((CHUNK, 512), rows)],
        [arr((LEN, 128)), arr((LEN, 512))],
        (x, wq_t, wk_t, wv),
        [pltpu.VMEM((128, depth), BF16)],
        flops=2 * LEN * depth * 640,
        moved=14e6,
    )


def conv(x, tail, taps):
    row = lax.broadcasted_iota(jnp.int32, (8, 1), 0)
    once, twice = pltpu.roll(x, 1, 0), pltpu.roll(x, 2, 0)
    top1 = jnp.where(row == 0, tail[7:8], once[0:8])
    top2 = jnp.where(row == 0, tail[6:7], jnp.where(row == 1, tail[7:8], twice[0:8]))
    once = jnp.concatenate([top1, once[8:]], axis=0)
    twice = jnp.concatenate([top2, twice[8:]], axis=0)
    return taps[0:1] * x + taps[1:2] * once + taps[2:3] * twice


def state_kernel(
    qk_ref, v_ref, qkp_ref, vp_ref, t_ref, wq_ref, wk_ref, wv_ref, tqk_ref, tv_ref, pick_ref, biast_ref,
    ql_ref, kr_ref, vh_ref, vl_ref, sp_ref, st_ref, tail_qk, tail_v,
):
    c = pl.program_id(0)

    @pl.when(c == 0)
    def _():
        t = t_ref[...]
        tail_qk[...] = nt(t, jnp.concatenate([wq_ref[...], wk_ref[...]], axis=0))[8:16]
        tail_v[...] = nn(t, wv_ref[...])[8:16]
        st_ref[...] = jnp.zeros_like(st_ref)

    @pl.when(c > 0)
    def _():
        tail_qk[...] = qkp_ref[...]
        tail_v[...] = vp_ref[...]

    qk = conv(qk_ref[...], tail_qk[...], tqk_ref[...]) * 0.5
    v = conv(v_ref[...], tail_v[...], tv_ref[...])
    lane = lax.broadcasted_iota(jnp.int32, (1, 128), 1)
    low = lane < 64
    turned = pltpu.roll(qk, 64, 1)
    hi = qk.astype(BF16).astype(F32)
    lo = qk - hi
    turned_hi = turned.astype(BF16).astype(F32)
    turned_lo = turned - turned_hi
    zero = jnp.zeros_like(qk)
    ql = side(jnp.where(low, hi, turned_lo), jnp.where(low, hi, zero)).astype(BF16)
    kr = side(jnp.where(low, turned_hi, hi), jnp.where(low, turned_lo, zero)).astype(BF16)
    ql_ref[...] = ql
    kr_ref[...] = kr
    v_hi, v_lo = halves(v)
    vh_ref[...] = v_hi
    vl_ref[...] = v_lo
    for head in range(HEADS):
        ab = nt(pick_ref[head], kr) + biast_ref[...]
        p_hi, p_lo = halves(ab[:NF] * ab[WIDE : WIDE + NF])
        own = nn3(p_hi, p_lo, v_hi[:, cols(head)], v_lo[:, cols(head)])
        sp_ref[0, head] = st_ref[head]
        st_ref[head] += own


def shard_state(qk, v, tail, wq_t, wk_t, wv, taps_qk, taps_v, pick_kt, bias_t):
    depth = tail.shape[1]
    rows = lambda c: (c, 0)
    before = lambda c: (jnp.maximum(c * (CHUNK // 8) - 1, 0), 0)
    return call(
        state_kernel,
        (CHUNKS,),
        [
            pl.BlockSpec((CHUNK, 128), rows),
            pl.BlockSpec((CHUNK, 512), rows),
            pl.BlockSpec((8, 128), before),
            pl.BlockSpec((8, 512), before),
            full(16, depth),
            full(64, depth),
            full(64, depth),
            full(depth, 512),
            full(3, 128),
            full(3, 512),
            full(HEADS, 2 * WIDE, WIDE),
            full(2 * WIDE, 1),
        ],
        [
            pl.BlockSpec((CHUNK, WIDE), rows),
            pl.BlockSpec((CHUNK, WIDE), rows),
            pl.BlockSpec((CHUNK, 512), rows),
            pl.BlockSpec((CHUNK, 512), rows),
            pl.BlockSpec((1, HEADS, NF, HDIM), lambda c: (c, 0, 0, 0)),
            full(HEADS, NF, HDIM),
        ],
        [
            arr((LEN, WIDE), BF16),
            arr((LEN, WIDE), BF16),
            arr((LEN, 512), BF16),
            arr((LEN, 512), BF16),
            arr((CHUNKS, HEADS, NF, HDIM)),
            arr((HEADS, NF, HDIM)),
        ],
        (qk, v, qk, v, tail, wq_t, wk_t, wv, taps_qk, taps_v, pick_kt, bias_t),
        [pltpu.VMEM((8, 128), F32), pltpu.VMEM((8, 512), F32)],
        flops=4e9,
        moved=15e6,
    )


def running_kernel(backward, x_ref, o_ref):
    count = x_ref.shape[0]
    order = range(count - 1, -1, -1) if backward else range(count)
    total = jnp.zeros(x_ref.shape[1:], F32)
    for i in order:
        o_ref[i] = total
        total = total + x_ref[i]


def carried_in(state, backward):
    count = lax.axis_size("seq")
    rows = HEADS * NF // count
    pieces = lax.all_to_all(state.reshape(count, rows, HDIM), "seq", 0, 0)
    shape = (count, rows, HDIM)
    sums = call(
        functools.partial(running_kernel, backward), (1,), [full(*shape)], full(*shape), arr(shape), (pieces,), moved=6e5
    )
    return lax.all_to_all(sums, "seq", 0, 0).reshape(HEADS, NF, HDIM)


def lower():
    row = lax.broadcasted_iota(jnp.int32, (CHUNK, CHUNK), 0)
    col = lax.broadcasted_iota(jnp.int32, (CHUNK, CHUNK), 1)
    return row >= col


def inner_kernel(ql_ref, kr_ref, vh_ref, vl_ref, num_ref):
    ql, kr = ql_ref[...], kr_ref[...]
    causal = lower()
    for head in range(HEADS):
        mine = jnp.where(head_mask(WIDE, head), ql, jnp.zeros_like(ql))
        s = nt(mine, kr)
        w_hi, w_lo = halves(jnp.where(causal, 1.0 + s + 0.5 * s * s, 0.0))
        num_ref[:, cols(head)] = nn3(w_hi, w_lo, vh_ref[:, cols(head)], vl_ref[:, cols(head)])


def inner(ql, kr, vh, vl):
    rows = lambda c: (c, 0)
    narrow, wide = pl.BlockSpec((CHUNK, WIDE), rows), pl.BlockSpec((CHUNK, 512), rows)
    return call(
        inner_kernel, (CHUNKS,), [narrow, narrow, wide, wide], wide, arr((LEN, 512)), (ql, kr, vh, vl), flops=6e9, moved=6e6
    )


def forward_kernel(ql_ref, num_ref, sp_ref, se_ref, og_ref, gain_ref, pick_ref, pickt_ref, bias_ref, biast_ref,
                   out_ref, dh_ref, dl_ref, gs_ref, gt_ref):
    @pl.when(pl.program_id(0) == 0)
    def _():
        gt_ref[...] = jnp.zeros_like(gt_ref)

    ql = ql_ref[...]
    for head in range(HEADS):
        a, b = factors(ql, pick_ref[head], bias_ref[...])
        p_hi, p_lo = halves(a * b)
        s_hi, s_lo = halves(padded(sp_ref[0, head] + se_ref[head]))
        num = num_ref[:, cols(head)] + nn3(p_hi, p_lo, s_hi, s_lo)
        r = lax.rsqrt(jnp.mean(num * num, axis=-1, keepdims=True) + EPS)
        gain = gain_ref[:, cols(head)]
        unit = num * r
        out_ref[:, cols(head)] = unit * gain
        g = og_ref[:, cols(head)] * gain
        d = r * (g - unit * jnp.mean(g * unit, axis=-1, keepdims=True))
        d_hi, d_lo = halves(d)
        dh_ref[:, cols(head)] = d_hi
        dl_ref[:, cols(head)] = d_lo
        ab = nt(pickt_ref[head], ql) + biast_ref[...]
        pt_hi, pt_lo = halves(ab[:NF] * ab[WIDE : WIDE + NF])
        own = nn3(pt_hi, pt_lo, d_hi, d_lo)
        gs_ref[0, head] = own
        gt_ref[head] += own


def forward(ql, num, sp, se, og, gain, pick, pick_t, bias, bias_t):
    rows = lambda c: (c, 0)
    narrow, wide = pl.BlockSpec((CHUNK, WIDE), rows), pl.BlockSpec((CHUNK, 512), rows)
    states = pl.BlockSpec((1, HEADS, NF, HDIM), lambda c: (c, 0, 0, 0))
    return call(
        forward_kernel,
        (CHUNKS,),
        [
            narrow, wide, states, full(HEADS, NF, HDIM), wide, full(1, 512),
            full(HEADS, WIDE, 2 * WIDE), full(HEADS, 2 * WIDE, WIDE), full(1, 2 * WIDE), full(2 * WIDE, 1),
        ],
        [wide, wide, wide, states, full(HEADS, NF, HDIM)],
        [
            arr((LEN, 512)), arr((LEN, 512), BF16), arr((LEN, 512), BF16),
            arr((CHUNKS, HEADS, NF, HDIM)), arr((HEADS, NF, HDIM)),
        ],
        (ql, num, sp, se, og, gain, pick, pick_t, bias, bias_t),
        flops=8e9,
        moved=12e6,
    )


def backward_kernel(ql_ref, kr_ref, vh_ref, vl_ref, dh_ref, dl_ref, sp_ref, se_ref, pick_ref, bias_ref, back_ref,
                    gq_ref, gk_ref, gv_ref):
    ql, kr = ql_ref[...], kr_ref[...]
    row = lax.broadcasted_iota(jnp.int32, (CHUNK, CHUNK), 0)
    col = lax.broadcasted_iota(jnp.int32, (CHUNK, CHUNK), 1)
    gq = jnp.zeros((CHUNK, WIDE), F32)
    gk = jnp.zeros((CHUNK, WIDE), F32)
    du = jnp.zeros((CHUNK, 128), F32)
    for head in range(HEADS):
        mask = head_mask(WIDE, head)
        q = jnp.where(mask, ql, jnp.zeros_like(ql))
        k = jnp.where(mask, kr, jnp.zeros_like(kr))
        v_hi, v_lo = vh_ref[:, cols(head)], vl_ref[:, cols(head)]
        d_hi, d_lo = dh_ref[:, cols(head)], dl_ref[:, cols(head)]
        s = nt(q, kr)
        slope = jnp.where(row >= col, 1.0 + s, 0.0)
        ds_hi, ds_lo = halves(nt3(d_hi, d_lo, v_hi, v_lo) * slope)
        gq = gq + nn(ds_hi, k) + nn(ds_lo, k)
        st = nt(k, ql)
        slope = jnp.where(col >= row, 1.0 + st, 0.0)
        dst_hi, dst_lo = halves(nt3(v_hi, v_lo, d_hi, d_lo) * slope)
        gk = gk + nn(dst_hi, q) + nn(dst_lo, q)
        w_hi, w_lo = halves(jnp.where(col >= row, 1.0 + st + 0.5 * st * st, 0.0))
        gv_ref[:, cols(head)] = nn3(w_hi, w_lo, d_hi, d_lo)
        s_hi, s_lo = halves(padded(sp_ref[0, head] + se_ref[head]))
        dp = nt3(d_hi, d_lo, s_hi, s_lo)
        a, b = factors(ql, pick_ref[head], bias_ref[...])
        dab_hi, dab_lo = halves(side(dp * b, dp * a))
        du = du + nn(dab_hi, back_ref[head]) + nn(dab_lo, back_ref[head])
    gq_ref[...] = gq[:, :128] + gq[:, 128:] + du
    gk_ref[...] = gk[:, :128] + pltpu.roll(gk[:, :128], 64, 1)


def backward(ql, kr, vh, vl, dh, dl, sp, se, pick, bias, back):
    rows = lambda c: (c, 0)
    narrow, wide = pl.BlockSpec((CHUNK, WIDE), rows), pl.BlockSpec((CHUNK, 512), rows)
    half = pl.BlockSpec((CHUNK, 128), rows)
    states = pl.BlockSpec((1, HEADS, NF, HDIM), lambda c: (c, 0, 0, 0))
    return call(
        backward_kernel,
        (CHUNKS,),
        [
            narrow, narrow, wide, wide, wide, wide, states, full(HEADS, NF, HDIM),
            full(HEADS, WIDE, 2 * WIDE), full(1, 2 * WIDE), full(HEADS, 2 * WIDE, 128),
        ],
        [half, half, wide],
        [arr((LEN, 128)), arr((LEN, 128)), arr((LEN, 512))],
        (ql, kr, vh, vl, dh, dl, sp, se, pick, bias, back),
        flops=16e9,
        moved=12e6,
    )


def later_kernel(first, last, kr_ref, vh_ref, vl_ref, gs_ref, gl_ref, gq_ref, gk_ref, gv_ref, pick_ref, bias_ref,
                 back_ref, oqk_ref, ov_ref, total):
    @pl.when(pl.program_id(0) == 0)
    def _():
        begin = gl_ref[...]
        for c in range(CHUNKS - 1, last - 1, -1):
            begin = begin + gs_ref[c]
        total[...] = begin

    kr = kr_ref[...]
    du = jnp.zeros((CHUNK, 128), F32)
    for head in range(HEADS):
        a, b = factors(kr, pick_ref[head], bias_ref[...])
        p_hi, p_lo = halves(a * b)
        l_hi, l_lo = halves(padded(total[head]))
        v_hi, v_lo = vh_ref[:, cols(head)], vl_ref[:, cols(head)]
        ov_ref[:, cols(head)] = gv_ref[:, cols(head)] + nn3(p_hi, p_lo, l_hi, l_lo)
        dp = nt3(v_hi, v_lo, l_hi, l_lo)
        dab_hi, dab_lo = halves(side(dp * b, dp * a))
        du = du + nn(dab_hi, back_ref[head]) + nn(dab_lo, back_ref[head])
    low = lax.broadcasted_iota(jnp.int32, (1, 128), 1) < 64
    oqk_ref[...] = 0.5 * jnp.where(low, gq_ref[...], pltpu.roll(gk_ref[...] + du, 64, 1))
    total[...] += gs_ref[last - 1 - pl.program_id(0)]


def later(first, last, kr, vh, vl, gs, gl, gq, gk, gv, pick, bias, back):
    count = last - first
    rows = lambda c: (last - 1 - c, 0)
    to = lambda c: (count - 1 - c, 0)
    narrow, wide = pl.BlockSpec((CHUNK, WIDE), rows), pl.BlockSpec((CHUNK, 512), rows)
    half = pl.BlockSpec((CHUNK, 128), rows)
    return call(
        functools.partial(later_kernel, first, last),
        (count,),
        [
            narrow, wide, wide, full(CHUNKS, HEADS, NF, HDIM), full(HEADS, NF, HDIM), half, half, wide,
            full(HEADS, WIDE, 2 * WIDE), full(1, 2 * WIDE), full(HEADS, 2 * WIDE, 128),
        ],
        [pl.BlockSpec((CHUNK, 128), to), pl.BlockSpec((CHUNK, 512), to)],
        [arr((count * CHUNK, 128)), arr((count * CHUNK, 512))],
        (kr, vh, vl, gs, gl, gq, gk, gv, pick, bias, back),
        [pltpu.VMEM((HEADS, NF, HDIM), F32)],
        flops=2e9 * count,
        moved=3e6 * count,
    )


def conv_back(x, tail, taps):
    n = x.shape[0]
    row = lax.broadcasted_iota(jnp.int32, (8, 1), 0)
    once, twice = pltpu.roll(x, n - 1, 0), pltpu.roll(x, n - 2, 0)
    end1 = jnp.where(row == 7, tail[0:1], once[n - 8 :])
    end2 = jnp.where(row == 7, tail[1:2], jnp.where(row == 6, tail[0:1], twice[n - 8 :]))
    once = jnp.concatenate([once[: n - 8], end1], axis=0)
    twice = jnp.concatenate([twice[: n - 8], end2], axis=0)
    return (taps[0:1] * x + taps[1:2] * once + taps[2:3] * twice).astype(BF16)


def unconv_kernel(aqk_ref, av_ref, bqk_ref, bv_ref, hqk_ref, hv_ref, tqk_ref, tv_ref, dqk_ref, dv_ref, dt_ref):
    for a_ref, b_ref, h_ref, t_ref, d_ref, base in (
        (aqk_ref, bqk_ref, hqk_ref, tqk_ref, dqk_ref, 0),
        (av_ref, bv_ref, hv_ref, tv_ref, dv_ref, 128),
    ):
        n = a_ref.shape[0]
        for start in range(0, LEN, CHUNK):
            src = a_ref[start : start + CHUNK] if start < n else b_ref[start - n : start - n + CHUNK]
            end = start + CHUNK
            if end == LEN:
                tail = h_ref[...]
            else:
                tail = a_ref[end : end + 8] if end < n else b_ref[end - n : end - n + 8]
            got = conv_back(src, tail, t_ref[...])
            d_ref[start:end] = got
            dt_ref[base : base + got.shape[1], start:end] = got.T


def unconv(aqk, av, bqk, bv, hqk, hv, taps_qk, taps_v):
    n, m = aqk.shape[0], bqk.shape[0]
    return call(
        unconv_kernel,
        (1,),
        [full(n, 128), full(n, 512), full(m, 128), full(m, 512), full(8, 128), full(8, 512), full(3, 128), full(3, 512)],
        [full(LEN, 128), full(LEN, 512), full(640, LEN)],
        [arr((LEN, 128), BF16), arr((LEN, 512), BF16), arr((640, LEN), BF16)],
        (aqk, av, bqk, bv, hqk, hv, taps_qk, taps_v),
        moved=6e6,
    )


def input_kernel(dqk_ref, dv_ref, wq_ref, wk_ref, wv_ref, o_ref):
    w = jnp.concatenate([wq_ref[...], wk_ref[...]], axis=0)
    o_ref[0] = (nt(dv_ref[...], wv_ref[...]) + nn(dqk_ref[...], w)).astype(o_ref.dtype)


def input_blocks(dqk, dv, wq_t, wk_t, wv):
    parts = wv.shape[0] // 512
    at = lambda p: (0, p)
    return call(
        input_kernel,
        (parts,),
        [full(LEN, 128), full(LEN, 512), pl.BlockSpec((64, 512), at), pl.BlockSpec((64, 512), at),
         pl.BlockSpec((512, 512), lambda p: (p, 0))],
        pl.BlockSpec((1, LEN, 512), lambda p: (p, 0, 0)),
        arr((parts, LEN, 512), BF16),
        (dqk, dv, wq_t, wk_t, wv),
        flops=2 * LEN * 640 * 4096,
        moved=15e6,
    )


def weight_kernel(dt_ref, x_ref, o_ref):
    o_ref[0] = nn(dt_ref[...], x_ref[...]).astype(o_ref.dtype)


def weight_blocks(dt, x):
    parts = lax.axis_size("seq")
    width = x.shape[1] // parts
    return call(
        weight_kernel,
        (parts,),
        [full(640, LEN), pl.BlockSpec((LEN, width), lambda p: (0, p))],
        pl.BlockSpec((1, 640, width), lambda p: (p, 0, 0)),
        arr((parts, 640, width), BF16),
        (dt, x),
        flops=2 * LEN * 640 * 4096,
        moved=15e6,
    )


def along(x, by):
    n = lax.axis_size("seq")
    return lax.ppermute(x, "seq", [(i, i + by) for i in range(n) if 0 <= i + by < n])


def local(inputs, w_query, w_key, w_value, taps_query, taps_key, taps_value, out_gain, out_grad):
    packed, bias, back = feature_matrices()
    pick_q, pick_k = (jnp.asarray(packed[i], BF16) for i in range(2))
    pick_qt, pick_kt = (jnp.asarray(packed[i].transpose(0, 2, 1), BF16) for i in range(2))
    back_q, back_k = (jnp.asarray(back[i], BF16) for i in range(2))
    bias, bias_t = jnp.asarray(bias), jnp.asarray(bias.T)
    wq_t, wk_t = w_query.T, w_key.T
    taps_qk = jnp.concatenate([taps_query, taps_key], axis=1)

    tail = along(inputs[-16:], 1)
    proj_qk, proj_v = project(inputs, wq_t, wk_t, w_value)
    ql, kr, vh, vl, before, own = shard_state(
        proj_qk, proj_v, tail, wq_t, wk_t, w_value, taps_qk, taps_value, pick_kt, bias_t
    )
    earlier = carried_in(own, False)
    num = inner(ql, kr, vh, vl)
    outputs, dh, dl, grads, own_grad = forward(
        ql, num, before, earlier, out_grad, out_gain.reshape(1, 512), pick_q, pick_qt, bias, bias_t
    )
    after = carried_in(own_grad, True)
    gq, gk, gv = backward(ql, kr, vh, vl, dh, dl, before, earlier, pick_q, bias, back_q)
    rest = (kr, vh, vl, grads, after, gq, gk, gv, pick_k, bias, back_k)
    aqk, av = later(0, 1, *rest)
    hqk, hv = along(aqk[:8], -1), along(av[:8], -1)
    bqk, bv = later(1, CHUNKS, *rest)
    dqk, dv, dt = unconv(aqk, av, bqk, bv, hqk, hv, taps_qk, taps_value)
    blocks = lax.all_to_all(input_blocks(dqk, dv, wq_t, wk_t, w_value), "tp", 0, 0)
    input_grad = jnp.sum(blocks.astype(F32), axis=0).astype(BF16)
    pieces = lax.all_to_all(weight_blocks(dt, inputs), "seq", 0, 0)
    summed = jnp.sum(pieces.astype(F32), axis=0)
    return (outputs, input_grad, summed[0:64].T, summed[64:128].T, summed[128:].T)


def solution(mesh):
    return jax.shard_map(
        local,
        mesh=mesh,
        in_specs=(
            P("seq", None),
            P(None, "tp"),
            P(None, "tp"),
            P(None, "tp"),
            P(None, "tp"),
            P(None, "tp"),
            P(None, "tp"),
            P("tp"),
            P("seq", "tp"),
        ),
        out_specs=(P("seq", "tp"), P("seq", "tp"), P("seq", "tp"), P("seq", "tp"), P("seq", "tp")),
        check_vma=False,
    )
```

time: 684 us -> 338 us (0.49); the launches traced: 672 us -> 336 us
  matrix products: 212 us -> 0 us
  Pallas kernels: 0 us -> 111 us
  waiting for transfers between devices: 236 us -> 150 us
  other arithmetic: 84.8 us -> 9.74 us
  blocking collectives: 76.2 us -> 25.2 us
  local copies, waits for them, and re-layouts: 32 us -> 6.73 us
  starting transfers between devices: 15.2 us -> 31.9 us
  between operations: 15.1 us -> 0.78 us
    reduce_scatter x2 -> x0, waiting for transfers between devices: 234 us -> none  [the longest x1 197 us: local(): lax.psum_scatter(input_term, 'tp', scatter_dimension=1, tiled=True)]
    dot_general x25 -> x0, matrix products: 212 us -> none  [the longest x3 64.2 us: attend(): inner = jnp.einsum('htu,uhd->thd', kernel, values, precision=HIGHEST)]
    all_to_all x0 -> x4, waiting for transfers between devices: none -> 150 us  [the longest x1 91.1 us: local(): lax.all_to_all(input_blocks(dqk, dv, wq_t, wk_t, w_value), 'tp', 0, 0)]
    pallas_call x0 -> x12, Pallas kernels: none -> 111 us  [call(): pl.pallas_call(body, grid_spec=pltpu.PrefetchScalarGridSpec(num_scalar_pr...]
    all_gather x4 -> x0, blocking collectives: 76.2 us -> none  [carried_in(): pieces = jax.tree.map(lambda part: lax.all_gather(part, axis), value)]
    select_n x90 -> x0, other arithmetic: 60 us -> none  [step(): jnp.where(position < mine, new, old)]
    all_to_all x0 -> x4, starting transfers between devices: none -> 25.7 us  [the longest x2 12.1 us: carried_in(): return lax.all_to_all(sums, 'seq', 0, 0).reshape(HEADS, NF, HDIM)]
    all_to_all x0 -> x2, blocking collectives: none -> 25.2 us  [carried_in(): pieces = lax.all_to_all(state.reshape(count, rows, HDIM), 'seq', 0, 0)]
  transfers between devices with their start and end apart: 10 -> 7, of which waited for: 3 -> 2; matrix products, arithmetic and copies ran while one was open for 25% -> 2% of each run, Pallas kernels for 0% -> 17%
where the time goes in v1:
time: 338 us; the launch traced here: 336 us
  waiting for transfers between devices  150 us (44%)
  Pallas kernels  111 us (33%)
  starting transfers between devices  31.9 us (9%)
  blocking collectives  25.2 us (7%)
  other arithmetic  9.74 us (3%)
  local copies, waits for them, and re-layouts  6.73 us (2%)
    pallas_call x12, Pallas kernels, call(): pl.pallas_call(body, grid_spec=pltpu.PrefetchScalarGridSpec(num_scalar_pr...  111 us
    all_to_all x1, waiting for transfers between devices, local(): lax.all_to_all(input_blocks(dqk, dv, wq_t, wk_t, w_value), 'tp', 0, 0)  91.1 us
    all_to_all x1, waiting for transfers between devices, local(): pieces = lax.all_to_all(weight_blocks(dt, inputs), 'seq', 0, 0)  59.2 us
    all_to_all x2, blocking collectives, carried_in(): pieces = lax.all_to_all(state.reshape(count, rows, HDIM), 'seq', 0, 0)  25.2 us
    all_to_all x2, starting transfers between devices, carried_in(): return lax.all_to_all(sums, 'seq', 0, 0).reshape(HEADS, NF, HDIM)  12.1 us
    all_to_all x1, starting transfers between devices, local(): lax.all_to_all(input_blocks(dqk, dv, wq_t, wk_t, w_value), 'tp', 0, 0)  7.65 us
  transfers between devices with their start and end apart: 7, of which 2 were waited for; matrix products, arithmetic and copies ran while one was open for 2% of the time, Pallas kernels for 17%

profile of v1, /device:TPU:2, one launch (start us, length us, event | category | flops | bytes accessed | tf_op | source)
XLA Modules:
  0.0 335.9 jit_solution(18097674203724106269)
XLA Ops:
  0.6 0.9 slice.18
  1.6 1.9 collective-permute-start
  3.5 0.0 copy-start.4
  3.5 0.0 copy-start.5
  3.5 11.3 %shard_map.200 = (f32[1024,128]{1,0:T(8,128)}, f32[1024,512]{1,0:T(8,128)}) custom-call(bf16[1024,4096]{1,0:T(8,128)(2,1)} %x_ref.3, bf16[64,4096]{1,0:T(8,128)(2,1)} %bitcast.19, bf16[64,4096]{1,0:T(8,128)(2,1)} %bitcast.22, bf16[4096,512]{1,0:T(8,128)(2,1)} %wv_ref.5), custom_call_target="tpu_custom_call" | custom-call | flops 5368709120 | bytes 14000000 | tf_op jit(solution)/shard_map/pallas_call | solution.py:94
  14.8 0.0 copy-done.4
  14.8 0.0 copy-done.5
  14.8 0.6 pad_maximum_fusion.tqk_ref
  15.4 0.0 collective-permute-done.t_ref
  15.4 0.0 copy-start.6
  15.4 0.7 copy-done.6
  16.1 10.4 %shard_map.201 = (bf16[1024,256]{1,0:T(8,128)(2,1)}, bf16[1024,256]{1,0:T(8,128)(2,1)}, bf16[1024,512]{1,0:T(8,128)(2,1)}, bf16[1024,512]{1,0:T(8,128)(2,1)}, f3...) custom-call(f32[1024,128]{1,0:T(8,128)} %get-tuple-element.28.qk_ref.qkp_ref, ...), custom_call_target="tpu_custom_call" | custom-call | flops 4000000000 | bytes 15000000 | tf_op jit(solution)/shard_map/pallas_call | solution.py:94
  26.5 12.8 %all_to_all.30.x_ref = f32[16,40,128]{2,1,0:T(8,128)} all-to-all(f32[16,40,128]{2,1,0:T(8,128)} %bitcast.17), channel_id=1, replica_groups=mesh['seq'=16,'tp'=8] {'seq'}, dimensions={0} | all-to-all | bytes 655360 | tf_op jit(solution)/shard_map/all_to_all | solution.py:249
  39.3 1.7 shard_map.203
  41.0 6.0 %all-to-all-start.1 = ((f32[16,40,128]{2,1,0:T(8,128)}), f32[16,40,128]{2,1,0:T(8,128)S(1)}, u32[]{:S(2)}, u32[]{:S(2)}) async-start(f32[16,40,128]{2,1,0:T(8,128)} %shard_map.203), calls=%async_computation.1 | async-start | bytes 655360 | tf_op jit(solution)/shard_map/all_to_all | solution.py:254
  47.1 6.3 %shard_map.202.num_ref = f32[1024,512]{1,0:T(8,128)} custom-call(bf16[1024,256]{1,0:T(8,128)(2,1)} %get-tuple-element.30.ql_ref, bf16[1024,256]{1,0:T(8,128)(2,1)} %get-tuple-element.31.kr_ref, bf16[1024,512]{1,0:T(8,128)(2,1)} %get-tuple-element.32.vh_ref, bf16[1024,512]{1,0:T(8,128)(2,1)} %get-tuple-element.33.vl_ref), custom_call_target="tpu_custom_call" | custom-call | flops 6000000000 | bytes 6000000 | tf_op jit(solution)/shard_map/pallas_call | solution.py:94
  53.4 0.0 all-to-all-done.1
  53.4 0.0 copy-start.1
  53.4 0.7 copy-done.1
  54.1 14.2 %shard_map.204 = (f32[1024,512]{1,0:T(8,128)}, bf16[1024,512]{1,0:T(8,128)(2,1)}, bf16[1024,512]{1,0:T(8,128)(2,1)}, f32[4,4,160,128]{3,2,1,0:T(8,128)}, f32[4,160,128]{2,1,0:T(8,128)}) custom-call(bf16[1024,256]{1,0:T(8,128)(2,1)} %get-tuple-element.30.ql_ref, f32[1024,512]{1,0:T(8,128)} %shard_map.202.num_ref, ...), custom_call_target="tpu_custom_call" | custom-call | flops 8000000000 | bytes 12000000 | tf_op jit(solution)/shard_map/pallas_call | solution.py:94
  68.3 12.4 %all_to_all.31.x_ref = f32[16,40,128]{2,1,0:T(8,128)} all-to-all(f32[16,40,128]{2,1,0:T(8,128)} %bitcast.18), channel_id=1, replica_groups=mesh['seq'=16,'tp'=8] {'seq'}, dimensions={0} | all-to-all | bytes 655360 | tf_op jit(solution)/shard_map/all_to_all | solution.py:249
  80.8 1.7 shard_map.205
  82.5 6.0 %all-to-all-start.3 = ((f32[16,40,128]{2,1,0:T(8,128)}), f32[16,40,128]{2,1,0:T(8,128)S(1)}, u32[]{:S(2)}, u32[]{:S(2)}) async-start(f32[16,40,128]{2,1,0:T(8,128)} %shard_map.205), calls=%async_computation.3 | async-start | bytes 655360 | tf_op jit(solution)/shard_map/all_to_all | solution.py:254
  88.6 16.9 %shard_map.206 = (f32[1024,128]{1,0:T(8,128)}, f32[1024,128]{1,0:T(8,128)}, f32[1024,512]{1,0:T(8,128)}) custom-call(bf16[1024,256]{1,0:T(8,128)(2,1)} %get-tuple-element.30.ql_ref, bf16[1024,256]{1,0:T(8,128)(2,1)} %get-tuple-element.31.kr_ref, bf16[1024,512]{1,0:T(8,128)(2,1)} %get-tuple-element.32.vh_ref, bf16[1024,512]{1,0:T(8,128)(2,1)} %get-tuple-element.33.vl_ref, ...), custom_call_target="tpu_custom_call" | custom-call | flops 16000000000 | bytes 12000000 | tf_op jit(solution)/shard_map/pallas_call | solution.py:94
  105.5 0.0 all-to-all-done.3
  105.5 0.0 copy-start
  105.5 0.7 copy-done
  106.3 5.7 %shard_map.207 = (f32[256,128]{1,0:T(8,128)}, f32[256,512]{1,0:T(8,128)}) custom-call(bf16[1024,256]{1,0:T(8,128)(2,1)} %get-tuple-element.31.kr_ref, bf16[1024,512]{1,0:T(8,128)(2,1)} %get-tuple-element.32.vh_ref, bf16[1024,512]{1,0:T(8,128)(2,1)} %get-tuple-element.33.vl_ref, f32[4,4,160,128]{3,2,1,0:T(8,128)} %get-tuple-element.37.gs_ref, ...), custom_call_target="tpu_custom_call" | custom-call | flops 2000000000 | bytes 3000000 | tf_op jit(solution)/shard_map/pallas_call | solution.py:94
  112.0 0.7 slice.19
  112.6 2.0 collective-permute-start.1
  114.7 0.7 slice.20
  115.4 2.3 collective-permute-start.2
  117.7 11.5 %shard_map.208 = (f32[768,128]{1,0:T(8,128)}, f32[768,512]{1,0:T(8,128)}) custom-call(bf16[1024,256]{1,0:T(8,128)(2,1)} %get-tuple-element.31.kr_ref, bf16[1024,512]{1,0:T(8,128)(2,1)} %get-tuple-element.32.vh_ref, bf16[1024,512]{1,0:T(8,128)(2,1)} %get-tuple-element.33.vl_ref, f32[4,4,160,128]{3,2,1,0:T(8,128)} %get-tuple-element.37.gs_ref, ...), custom_call_target="tpu_custom_call" | custom-call | flops 6000000000 | bytes 9000000 | tf_op jit(solution)/shard_map/pallas_call | solution.py:94
  129.2 0.0 collective-permute-done.1.hqk_ref
  129.2 0.0 copy-start.3
  129.3 0.0 collective-permute-done.2.hv_ref
  129.3 0.0 copy-start.2
  129.3 0.6 copy-done.3
  129.8 0.0 copy-done.2
  129.9 4.0 %shard_map.209 = (bf16[1024,128]{1,0:T(8,128)(2,1)}, bf16[1024,512]{1,0:T(8,128)(2,1)}, bf16[640,1024]{1,0:T(8,128)(2,1)}) custom-call(f32[256,128]{1,0:T(8,128)} %get-tuple-element.44.aqk_ref, f32[256,512]{1,0:T(8,128)} %get-tuple-element.45.av_ref, f32[768,128]{1,0:T(8,128)} %get-tuple-element.46.bqk_ref, f32[768,512]{1,0:T(8,128)} %get-tuple-element.47.bv_ref, ...), custom_call_target="tpu_custom_call" | custom-call | bytes 6000000 | tf_op jit(solution)/shard_map/pallas_call | solution.py:94
  133.9 15.4 %shard_map.211 = bf16[16,640,256]{2,1,0:T(8,128)(2,1)} custom-call(bf16[640,1024]{1,0:T(8,128)(2,1)} %get-tuple-element.50.dt_ref, bf16[1024,4096]{1,0:T(8,128)(2,1)} %x_ref.3), custom_call_target="tpu_custom_call" | custom-call | flops 5368709120 | bytes 15000000 | tf_op jit(solution)/shard_map/pallas_call | solution.py:94
  149.2 5.9 %all-to-all-start.5 = ((bf16[16,640,256]{2,1,0:T(8,128)(2,1)}), bf16[16,640,256]{2,1,0:T(8,128)(2,1)}, u32[]{:S(2)}, u32[]{:S(2)}) async-start(bf16[16,640,256]{2,1,0:T(8,128)(2,1)} %shard_map.211), calls=%async_computation.5 | async-start | bytes 10485760 | tf_op jit(solution)/shard_map/all_to_all | solution.py:546
  155.2 11.9 %shard_map.210 = bf16[8,1024,512]{2,1,0:T(8,128)(2,1)} custom-call(bf16[1024,128]{1,0:T(8,128)(2,1)} %get-tuple-element.48.dqk_ref, bf16[1024,512]{1,0:T(8,128)(2,1)} %get-tuple-element.49.dv_ref, bf16[64,4096]{1,0:T(8,128)(2,1)} %bitcast.21, bf16[64,4096]{1,0:T(8,128)(2,1)} %bitcast.24, bf16[4096,512]{1,0:T(8,128)(2,1)} %wv_ref.5), custom_call_target="tpu_custom_call" | custom-call | flops 5368709120 | bytes 15000000 | tf_op jit(solution)/shard_map/pallas_call | solution.py:94
  167.1 59.2 %all-to-all-done.5 = bf16[16,640,256]{2,1,0:T(8,128)(2,1)} async-done(((bf16[16,640,256]{2,1,0:T(8,128)(2,1)}), bf16[16,640,256]{2,1,0:T(8,128)(2,1)}, u32[]{:S(2)}, u32[]{:S(2)}) %all-to-all-start.5) | async-done | bytes 5242912 | tf_op jit(solution)/shard_map/all_to_all | solution.py:546
  226.3 7.7 %all-to-all-start.4 = ((bf16[8,1024,512]{2,1,0:T(8,128)(2,1)}), bf16[8,1024,512]{2,1,0:T(8,128)(2,1)}, u32[]{:S(2)}, u32[]{:S(2)}) async-start(bf16[8,1024,512]{2,1,0:T(8,128)(2,1)} %shard_map.210), calls=%async_computation.4 | async-start | bytes 16777216 | tf_op jit(solution)/shard_map/all_to_all | solution.py:544
  234.0 3.3 convert_reduce_fusion
  237.3 1.0 copy.24
  238.3 0.7 slice_bitcast_fusion.1
  238.9 91.1 %all-to-all-done.4 = bf16[8,1024,512]{2,1,0:T(8,128)(2,1)} async-done(((bf16[8,1024,512]{2,1,0:T(8,128)(2,1)}), bf16[8,1024,512]{2,1,0:T(8,128)(2,1)}, u32[]{:S(2)}, u32[]{:S(2)}) %all-to-all-start.4) | async-done | bytes 8388640 | tf_op jit(solution)/shard_map/all_to_all | solution.py:544
  330.1 5.9 %reduce_sum.21 = bf16[1024,512]{1,0:T(8,128)(2,1)} reduce(bf16[8,1024,512]{2,1,0:T(8,128)(2,1)} %all-to-all-done.4, bf16[]{:T(256)} %constant.18.clone.1), dimensions={0}, to_apply=%region_0.0 | reduce | flops 3670016 | bytes 9437186 | tf_op jit(solution)/shard_map/reduce_sum | solution.py:545
  (1 shorter events, 0.0 us)
Async XLA Ops:
  1.6 13.9 %collective-permute-start = (bf16[16,4096]{1,0:T(8,128)(2,1)S(1)}, bf16[16,4096]{1,0:T(8,128)(2,1)S(1)}, u32[]{:S(2)}, u32[]{:S(2)}) collective-permute-start(bf16[16,4096]{1,0:T(8,128)(2,1)S(1)} %slice.18), channel_id=1, source_target_pairs={{0,8},{8,16},{16,24},{24,32},{32,40},{40,48},{48,56},{56,64},{64,7... | collective-permute-start | bytes 393224 | tf_op jit(solution)/shard_map/ppermute | solution.py:515
  3.5 11.3 %copy-start.4 = (f32[3,64]{1,0:T(4,128)S(1)}, f32[3,64]{1,0:T(4,128)}, u32[]{:S(2)}) copy-start(f32[3,64]{1,0:T(4,128)} %param.22) | copy-start | bytes 2308
  3.5 11.3 %copy-start.5 = (f32[3,64]{1,0:T(4,128)S(1)}, f32[3,64]{1,0:T(4,128)}, u32[]{:S(2)}) copy-start(f32[3,64]{1,0:T(4,128)} %param.21) | copy-start | bytes 2308
  15.4 0.7 copy-start.6
  41.0 12.4 %all-to-all-start.1 = ((f32[16,40,128]{2,1,0:T(8,128)}), f32[16,40,128]{2,1,0:T(8,128)S(1)}, u32[]{:S(2)}, u32[]{:S(2)}) async-start(f32[16,40,128]{2,1,0:T(8,128)} %shard_map.203), calls=%async_computation.1 | async-start | bytes 655360 | tf_op jit(solution)/shard_map/all_to_all | solution.py:254
  53.4 0.7 copy-start.1
  82.5 23.0 %all-to-all-start.3 = ((f32[16,40,128]{2,1,0:T(8,128)}), f32[16,40,128]{2,1,0:T(8,128)S(1)}, u32[]{:S(2)}, u32[]{:S(2)}) async-start(f32[16,40,128]{2,1,0:T(8,128)} %shard_map.205), calls=%async_computation.3 | async-start | bytes 655360 | tf_op jit(solution)/shard_map/all_to_all | solution.py:254
  105.5 0.7 copy-start
  112.6 16.6 %collective-permute-start.1 = (f32[8,128]{1,0:T(8,128)S(1)}, f32[8,128]{1,0:T(8,128)S(1)}, u32[]{:S(2)}, u32[]{:S(2)}) collective-permute-start(f32[8,128]{1,0:T(8,128)S(1)} %slice.19), channel_id=1, source_target_pairs={{8,0},{16,8},{24,16},{32,24},{40,32},{48,40},{56,48},{64,56},{72,6... | collective-permute-start | bytes 12296 | tf_op jit(solution)/shard_map/ppermute | solution.py:515
  115.4 13.9 %collective-permute-start.2 = (f32[8,512]{1,0:T(8,128)S(1)}, f32[8,512]{1,0:T(8,128)S(1)}, u32[]{:S(2)}, u32[]{:S(2)}) collective-permute-start(f32[8,512]{1,0:T(8,128)S(1)} %slice.20), channel_id=1, source_target_pairs={{8,0},{16,8},{24,16},{32,24},{40,32},{48,40},{56,48},{64,56},{72,6... | collective-permute-start | bytes 49160 | tf_op jit(solution)/shard_map/ppermute | solution.py:515
  129.2 0.6 copy-start.3
  129.3 0.6 copy-start.2
  149.2 77.1 %all-to-all-start.5 = ((bf16[16,640,256]{2,1,0:T(8,128)(2,1)}), bf16[16,640,256]{2,1,0:T(8,128)(2,1)}, u32[]{:S(2)}, u32[]{:S(2)}) async-start(bf16[16,640,256]{2,1,0:T(8,128)(2,1)} %shard_map.211), calls=%async_computation.5 | async-start | bytes 10485760 | tf_op jit(solution)/shard_map/all_to_all | solution.py:546
  226.3 103.7 %all-to-all-start.4 = ((bf16[8,1024,512]{2,1,0:T(8,128)(2,1)}), bf16[8,1024,512]{2,1,0:T(8,128)(2,1)}, u32[]{:S(2)}, u32[]{:S(2)}) async-start(bf16[8,1024,512]{2,1,0:T(8,128)(2,1)} %shard_map.210), calls=%async_computation.4 | async-start | bytes 16777216 | tf_op jit(solution)/shard_map/all_to_all | solution.py:544

commit v2 on v1

--- a/solution.py
+++ b/solution.py
@@ -17,6 +17,7 @@
 NF = 160
 WIDE = 256
 EPS = 1e-05
+STEP = 128
 F32, BF16 = jnp.float32, jnp.bfloat16
 
 
@@ -90,7 +91,13 @@
     return slice(head * HDIM, (head + 1) * HDIM)
 
 
-def call(body, grid, ins, outs, shapes, args, scratch=(), prefetch=0, flops=0, moved=0):
+def call(body, grid, ins, outs, shapes, args, scratch=(), prefetch=0, flops=0, moved=0, after=()):
+    if after:
+        kept, skip = body, len(after)
+        at = prefetch + len(ins)
+        body = lambda *refs: kept(*refs[:at], *refs[at + skip :])
+        ins = [*ins] + [pl.BlockSpec(memory_space=pl.ANY)] * skip
+        args = (*args, *after)
     return pl.pallas_call(
         body,
         grid_spec=pltpu.PrefetchScalarGridSpec(
@@ -128,10 +135,9 @@
         project_kernel,
         (CHUNKS,),
         [pl.BlockSpec((CHUNK, depth), rows), full(64, depth), full(64, depth), full(depth, 512)],
-        [pl.BlockSpec((CHUNK, 128), rows), pl.BlockSpec((CHUNK, 512), rows)],
-        [arr((LEN, 128)), arr((LEN, 512))],
+        [pl.BlockSpec((CHUNK, 128), rows), pl.BlockSpec((CHUNK, 512), rows), full(128, depth)],
+        [arr((LEN, 128)), arr((LEN, 512)), arr((128, depth), BF16)],
         (x, wq_t, wk_t, wv),
-        [pltpu.VMEM((128, depth), BF16)],
         flops=2 * LEN * depth * 640,
         moved=14e6,
     )
@@ -148,7 +154,7 @@
 
 
 def state_kernel(
-    qk_ref, v_ref, qkp_ref, vp_ref, t_ref, wq_ref, wk_ref, wv_ref, tqk_ref, tv_ref, pick_ref, biast_ref,
+    qk_ref, v_ref, qkp_ref, vp_ref, t_ref, wqk_ref, wv_ref, tqk_ref, tv_ref, pick_ref, biast_ref,
     ql_ref, kr_ref, vh_ref, vl_ref, sp_ref, st_ref, tail_qk, tail_v,
 ):
     c = pl.program_id(0)
@@ -156,7 +162,7 @@
     @pl.when(c == 0)
     def _():
         t = t_ref[...]
-        tail_qk[...] = nt(t, jnp.concatenate([wq_ref[...], wk_ref[...]], axis=0))[8:16]
+        tail_qk[...] = nt(t, wqk_ref[...])[8:16]
         tail_v[...] = nn(t, wv_ref[...])[8:16]
         st_ref[...] = jnp.zeros_like(st_ref)
 
@@ -190,7 +196,7 @@
         st_ref[head] += own
 
 
-def shard_state(qk, v, tail, wq_t, wk_t, wv, taps_qk, taps_v, pick_kt, bias_t):
+def shard_state(qk, v, tail, wqk_t, wv, taps_qk, taps_v, pick_kt, bias_t):
     depth = tail.shape[1]
     rows = lambda c: (c, 0)
     before = lambda c: (jnp.maximum(c * (CHUNK // 8) - 1, 0), 0)
@@ -203,8 +209,7 @@
             pl.BlockSpec((8, 128), before),
             pl.BlockSpec((8, 512), before),
             full(16, depth),
-            full(64, depth),
-            full(64, depth),
+            full(128, depth),
             full(depth, 512),
             full(3, 128),
             full(3, 512),
@@ -227,7 +232,7 @@
             arr((CHUNKS, HEADS, NF, HDIM)),
             arr((HEADS, NF, HDIM)),
         ],
-        (qk, v, qk, v, tail, wq_t, wk_t, wv, taps_qk, taps_v, pick_kt, bias_t),
+        (qk, v, qk, v, tail, wqk_t, wv, taps_qk, taps_v, pick_kt, bias_t),
         [pltpu.VMEM((8, 128), F32), pltpu.VMEM((8, 512), F32)],
         flops=4e9,
         moved=15e6,
@@ -328,13 +333,10 @@
     )
 
 
-def backward_kernel(ql_ref, kr_ref, vh_ref, vl_ref, dh_ref, dl_ref, sp_ref, se_ref, pick_ref, bias_ref, back_ref,
-                    gq_ref, gk_ref, gv_ref):
+def query_kernel(ql_ref, kr_ref, vh_ref, vl_ref, dh_ref, dl_ref, sp_ref, se_ref, pick_ref, bias_ref, back_ref, gq_ref):
     ql, kr = ql_ref[...], kr_ref[...]
-    row = lax.broadcasted_iota(jnp.int32, (CHUNK, CHUNK), 0)
-    col = lax.broadcasted_iota(jnp.int32, (CHUNK, CHUNK), 1)
+    causal = lower()
     gq = jnp.zeros((CHUNK, WIDE), F32)
-    gk = jnp.zeros((CHUNK, WIDE), F32)
     du = jnp.zeros((CHUNK, 128), F32)
     for head in range(HEADS):
         mask = head_mask(WIDE, head)
@@ -342,22 +344,34 @@
         k = jnp.where(mask, kr, jnp.zeros_like(kr))
         v_hi, v_lo = vh_ref[:, cols(head)], vl_ref[:, cols(head)]
         d_hi, d_lo = dh_ref[:, cols(head)], dl_ref[:, cols(head)]
-        s = nt(q, kr)
-        slope = jnp.where(row >= col, 1.0 + s, 0.0)
+        slope = jnp.where(causal, 1.0 + nt(q, kr), 0.0)
         ds_hi, ds_lo = halves(nt3(d_hi, d_lo, v_hi, v_lo) * slope)
         gq = gq + nn(ds_hi, k) + nn(ds_lo, k)
-        st = nt(k, ql)
-        slope = jnp.where(col >= row, 1.0 + st, 0.0)
-        dst_hi, dst_lo = halves(nt3(v_hi, v_lo, d_hi, d_lo) * slope)
-        gk = gk + nn(dst_hi, q) + nn(dst_lo, q)
-        w_hi, w_lo = halves(jnp.where(col >= row, 1.0 + st + 0.5 * st * st, 0.0))
-        gv_ref[:, cols(head)] = nn3(w_hi, w_lo, d_hi, d_lo)
         s_hi, s_lo = halves(padded(sp_ref[0, head] + se_ref[head]))
         dp = nt3(d_hi, d_lo, s_hi, s_lo)
         a, b = factors(ql, pick_ref[head], bias_ref[...])
         dab_hi, dab_lo = halves(side(dp * b, dp * a))
         du = du + nn(dab_hi, back_ref[head]) + nn(dab_lo, back_ref[head])
     gq_ref[...] = gq[:, :128] + gq[:, 128:] + du
+
+
+def key_kernel(ql_ref, kr_ref, vh_ref, vl_ref, dh_ref, dl_ref, gk_ref, gv_ref):
+    ql, kr = ql_ref[...], kr_ref[...]
+    row = lax.broadcasted_iota(jnp.int32, (CHUNK, CHUNK), 0)
+    col = lax.broadcasted_iota(jnp.int32, (CHUNK, CHUNK), 1)
+    causal = col >= row
+    gk = jnp.zeros((CHUNK, WIDE), F32)
+    for head in range(HEADS):
+        mask = head_mask(WIDE, head)
+        q = jnp.where(mask, ql, jnp.zeros_like(ql))
+        k = jnp.where(mask, kr, jnp.zeros_like(kr))
+        v_hi, v_lo = vh_ref[:, cols(head)], vl_ref[:, cols(head)]
+        d_hi, d_lo = dh_ref[:, cols(head)], dl_ref[:, cols(head)]
+        s = nt(k, ql)
+        ds_hi, ds_lo = halves(nt3(v_hi, v_lo, d_hi, d_lo) * jnp.where(causal, 1.0 + s, 0.0))
+        gk = gk + nn(ds_hi, q) + nn(ds_lo, q)
+        w_hi, w_lo = halves(jnp.where(causal, 1.0 + s + 0.5 * s * s, 0.0))
+        gv_ref[:, cols(head)] = nn3(w_hi, w_lo, d_hi, d_lo)
     gk_ref[...] = gk[:, :128] + pltpu.roll(gk[:, :128], 64, 1)
 
 
@@ -366,23 +380,34 @@
     narrow, wide = pl.BlockSpec((CHUNK, WIDE), rows), pl.BlockSpec((CHUNK, 512), rows)
     half = pl.BlockSpec((CHUNK, 128), rows)
     states = pl.BlockSpec((1, HEADS, NF, HDIM), lambda c: (c, 0, 0, 0))
-    return call(
-        backward_kernel,
+    gk, gv = call(
+        key_kernel,
+        (CHUNKS,),
+        [narrow, narrow, wide, wide, wide, wide],
+        [half, wide],
+        [arr((LEN, 128)), arr((LEN, 512))],
+        (ql, kr, vh, vl, dh, dl),
+        flops=8e9,
+        moved=8e6,
+    )
+    gq = call(
+        query_kernel,
         (CHUNKS,),
         [
             narrow, narrow, wide, wide, wide, wide, states, full(HEADS, NF, HDIM),
             full(HEADS, WIDE, 2 * WIDE), full(1, 2 * WIDE), full(HEADS, 2 * WIDE, 128),
         ],
-        [half, half, wide],
-        [arr((LEN, 128)), arr((LEN, 128)), arr((LEN, 512))],
+        half,
+        arr((LEN, 128)),
         (ql, kr, vh, vl, dh, dl, sp, se, pick, bias, back),
-        flops=16e9,
-        moved=12e6,
-    )
+        flops=8e9,
+        moved=8e6,
+    )
+    return gq, gk, gv
 
 
 def later_kernel(first, last, kr_ref, vh_ref, vl_ref, gs_ref, gl_ref, gq_ref, gk_ref, gv_ref, pick_ref, bias_ref,
-                 back_ref, oqk_ref, ov_ref, total):
+                 back_ref, o_ref, total):
     @pl.when(pl.program_id(0) == 0)
     def _():
         begin = gl_ref[...]
@@ -397,12 +422,12 @@
         p_hi, p_lo = halves(a * b)
         l_hi, l_lo = halves(padded(total[head]))
         v_hi, v_lo = vh_ref[:, cols(head)], vl_ref[:, cols(head)]
-        ov_ref[:, cols(head)] = gv_ref[:, cols(head)] + nn3(p_hi, p_lo, l_hi, l_lo)
+        o_ref[:, 128 + head * HDIM : 256 + head * HDIM] = gv_ref[:, cols(head)] + nn3(p_hi, p_lo, l_hi, l_lo)
         dp = nt3(v_hi, v_lo, l_hi, l_lo)
         dab_hi, dab_lo = halves(side(dp * b, dp * a))
         du = du + nn(dab_hi, back_ref[head]) + nn(dab_lo, back_ref[head])
     low = lax.broadcasted_iota(jnp.int32, (1, 128), 1) < 64
-    oqk_ref[...] = 0.5 * jnp.where(low, gq_ref[...], pltpu.roll(gk_ref[...] + du, 64, 1))
+    o_ref[:, :128] = 0.5 * jnp.where(low, gq_ref[...], pltpu.roll(gk_ref[...] + du, 64, 1))
     total[...] += gs_ref[last - 1 - pl.program_id(0)]
 
 
@@ -419,8 +444,8 @@
             narrow, wide, wide, full(CHUNKS, HEADS, NF, HDIM), full(HEADS, NF, HDIM), half, half, wide,
             full(HEADS, WIDE, 2 * WIDE), full(1, 2 * WIDE), full(HEADS, 2 * WIDE, 128),
         ],
-        [pl.BlockSpec((CHUNK, 128), to), pl.BlockSpec((CHUNK, 512), to)],
-        [arr((count * CHUNK, 128)), arr((count * CHUNK, 512))],
+        pl.BlockSpec((CHUNK, 640), to),
+        arr((count * CHUNK, 640)),
         (kr, vh, vl, gs, gl, gq, gk, gv, pick, bias, back),
         [pltpu.VMEM((HEADS, NF, HDIM), F32)],
         flops=2e9 * count,
@@ -439,74 +464,185 @@
     return (taps[0:1] * x + taps[1:2] * once + taps[2:3] * twice).astype(BF16)
 
 
-def unconv_kernel(aqk_ref, av_ref, bqk_ref, bv_ref, hqk_ref, hv_ref, tqk_ref, tv_ref, dqk_ref, dv_ref, dt_ref):
-    for a_ref, b_ref, h_ref, t_ref, d_ref, base in (
-        (aqk_ref, bqk_ref, hqk_ref, tqk_ref, dqk_ref, 0),
-        (av_ref, bv_ref, hv_ref, tv_ref, dv_ref, 128),
-    ):
-        n = a_ref.shape[0]
-        for start in range(0, LEN, CHUNK):
-            src = a_ref[start : start + CHUNK] if start < n else b_ref[start - n : start - n + CHUNK]
-            end = start + CHUNK
-            if end == LEN:
-                tail = h_ref[...]
-            else:
-                tail = a_ref[end : end + 8] if end < n else b_ref[end - n : end - n + 8]
-            got = conv_back(src, tail, t_ref[...])
-            d_ref[start:end] = got
-            dt_ref[base : base + got.shape[1], start:end] = got.T
-
-
-def unconv(aqk, av, bqk, bv, hqk, hv, taps_qk, taps_v):
-    n, m = aqk.shape[0], bqk.shape[0]
+def unconv_kernel(a_ref, b_ref, h_ref, t_ref, d_ref, dt_ref):
+    n = a_ref.shape[0]
+    for start in range(0, LEN, STEP):
+        end = start + STEP
+        src = a_ref[start:end] if start < n else b_ref[start - n : end - n]
+        if end == LEN:
+            tail = h_ref[...]
+        else:
+            tail = a_ref[end : end + 8] if end < n else b_ref[end - n : end - n + 8]
+        got = conv_back(src, tail, t_ref[...])
+        d_ref[start:end] = got
+        dt_ref[:, start:end] = got.T
+
+
+def unconv(a, b, halo, taps):
+    n, m = a.shape[0], b.shape[0]
     return call(
         unconv_kernel,
         (1,),
-        [full(n, 128), full(n, 512), full(m, 128), full(m, 512), full(8, 128), full(8, 512), full(3, 128), full(3, 512)],
-        [full(LEN, 128), full(LEN, 512), full(640, LEN)],
-        [arr((LEN, 128), BF16), arr((LEN, 512), BF16), arr((640, LEN), BF16)],
-        (aqk, av, bqk, bv, hqk, hv, taps_qk, taps_v),
+        [full(n, 640), full(m, 640), full(8, 640), full(3, 640)],
+        [full(LEN, 640), full(640, LEN)],
+        [arr((LEN, 640), BF16), arr((640, LEN), BF16)],
+        (a, b, halo, taps),
         moved=6e6,
     )
 
 
-def input_kernel(dqk_ref, dv_ref, wq_ref, wk_ref, wv_ref, o_ref):
-    w = jnp.concatenate([wq_ref[...], wk_ref[...]], axis=0)
-    o_ref[0] = (nt(dv_ref[...], wv_ref[...]) + nn(dqk_ref[...], w)).astype(o_ref.dtype)
-
-
-def input_blocks(dqk, dv, wq_t, wk_t, wv):
+def f32(x):
+    return x.astype(F32)
+
+
+def flip(x, axis, bit):
+    return lax.ppermute(x, axis, [(i, i ^ bit) for i in range(lax.axis_size(axis))])
+
+
+def input_kernel(d_ref, wv_ref, wqk_ref, o_ref):
+    d = d_ref[...]
+    o_ref[0] = (nt(d[:, 128:], wv_ref[...]) + nn(d[:, :128], wqk_ref[...])).astype(BF16)
+
+
+def input_products(d, wv, wqk):
     parts = wv.shape[0] // 512
-    at = lambda p: (0, p)
     return call(
         input_kernel,
         (parts,),
-        [full(LEN, 128), full(LEN, 512), pl.BlockSpec((64, 512), at), pl.BlockSpec((64, 512), at),
-         pl.BlockSpec((512, 512), lambda p: (p, 0))],
-        pl.BlockSpec((1, LEN, 512), lambda p: (p, 0, 0)),
+        [full(LEN, 640), pl.BlockSpec((512, 512), lambda i: (i, 0)), pl.BlockSpec((128, 512), lambda i: (0, i))],
+        pl.BlockSpec((1, LEN, 512), lambda i: (i, 0, 0)),
         arr((parts, LEN, 512), BF16),
-        (dqk, dv, wq_t, wk_t, wv),
+        (d, wv, wqk),
         flops=2 * LEN * 640 * 4096,
         moved=15e6,
     )
 
 
-def weight_kernel(dt_ref, x_ref, o_ref):
-    o_ref[0] = nn(dt_ref[...], x_ref[...]).astype(o_ref.dtype)
-
-
-def weight_blocks(dt, x):
-    parts = lax.axis_size("seq")
-    width = x.shape[1] // parts
-    return call(
+def sum_kernel(p_ref, o_ref):
+    total = f32(p_ref[0])
+    for i in range(1, p_ref.shape[0]):
+        total = total + f32(p_ref[i])
+    o_ref[...] = total.astype(BF16)
+
+
+def summed(parts, after):
+    count, rows, width = parts.shape
+    return call(
+        sum_kernel,
+        (8,),
+        [pl.BlockSpec((count, rows // 8, width), lambda i: (0, i, 0))],
+        pl.BlockSpec((rows // 8, width), lambda i: (i, 0)),
+        arr((rows, width), BF16),
+        (parts,),
+        moved=9e6,
+        after=after,
+    )
+
+
+def weight_kernel(dest_ref, d_ref, x_ref, theirs_ref, ours_ref):
+    got = nn(d_ref[...], x_ref[...]).astype(BF16)
+
+    @pl.when(pl.program_id(0) < 8)
+    def _():
+        theirs_ref[0] = got
+
+    @pl.when(pl.program_id(0) >= 8)
+    def _():
+        ours_ref[0] = got
+
+
+def split_kernel(mine_ref, came_ref, *outs):
+    step = pl.program_id(0)
+    got = f32(mine_ref[0]) + f32(came_ref[0])
+    for j in range(4):
+
+        @pl.when(step // 2 == j)
+        def _(j=j):
+            outs[j][0] = got.astype(BF16)
+
+
+def row_sum_kernel(mine_ref, a_ref, b_ref, c_ref, keep_ref, send_ref):
+    for r, out in enumerate((keep_ref, send_ref)):
+        out[...] = (f32(mine_ref[r]) + f32(a_ref[r]) + f32(b_ref[r]) + f32(c_ref[r])).astype(out.dtype)
+
+
+def finish_kernel(keep_ref, came_ref, q_ref, k_ref, v_ref):
+    step = pl.program_id(0)
+    total = keep_ref[...] + f32(came_ref[...])
+
+    @pl.when(step == 0)
+    def _():
+        q_ref[...] = total[:64]
+        k_ref[...] = total[64:]
+
+    @pl.when(step > 0)
+    def _():
+        v_ref[...] = total.T
+
+
+def to_x(x, by):
+    return lax.ppermute(x, "seq", [(s, s // 8 * 8 + (s % 8 + 2 * by) % 8) for s in range(16)])
+
+
+def reduce_weight_grad(dt, x, before):
+    me = lax.axis_index("seq")
+    y, px, core = me // 8, me // 2 % 4, me % 2
+    width = x.shape[1] // 16
+    chips = jnp.stack([((y ^ r) * 4 + (px + dx) % 4) * 2 for dx in range(4) for r in range(2)])
+    dest = jnp.concatenate([chips + 1 - core, chips + core]).astype(jnp.int32)
+    theirs, ours = call(
         weight_kernel,
-        (parts,),
-        [full(640, LEN), pl.BlockSpec((LEN, width), lambda p: (0, p))],
-        pl.BlockSpec((1, 640, width), lambda p: (p, 0, 0)),
-        arr((parts, 640, width), BF16),
-        (dt, x),
+        (16,),
+        [pl.BlockSpec((640, LEN), lambda i, dest: (0, 0)), pl.BlockSpec((LEN, width), lambda i, dest: (0, dest[i]))],
+        [
+            pl.BlockSpec((1, 640, width), lambda i, dest: (jnp.minimum(i, 7), 0, 0)),
+            pl.BlockSpec((1, 640, width), lambda i, dest: (jnp.maximum(i - 8, 0), 0, 0)),
+        ],
+        [arr((8, 640, width), BF16)] * 2,
+        (dest, dt, x),
+        prefetch=1,
+        after=(before,),
         flops=2 * LEN * 640 * 4096,
         moved=15e6,
+    )
+    came = flip(theirs, "seq", 1)
+    block = pl.BlockSpec((1, 640, width), lambda i: (i, 0, 0))
+    parts = call(
+        split_kernel,
+        (8,),
+        [block, block],
+        [pl.BlockSpec((1, 640, width), lambda i, j=j: (jnp.clip(i - 2 * j, 0, 1), 0, 0)) for j in range(4)],
+        [arr((2, 640, width), BF16)] * 4,
+        (ours, came),
+        moved=8e6,
+    )
+    mine, *rest = parts
+    rest = [to_x(part, dx) for dx, part in enumerate(rest, 1)]
+    pair = pl.BlockSpec((2, 128, width), lambda i: (0, i, 0))
+    one = pl.BlockSpec((128, width), lambda i: (i, 0))
+    keep, send = call(
+        row_sum_kernel,
+        (5,),
+        [pair] * 4,
+        [one] * 2,
+        [arr((640, width)), arr((640, width), BF16)],
+        (mine, *rest),
+        moved=4e6,
+    )
+    return keep, flip(send, "seq", 8)
+
+
+def finish_weight_grad(keep, came):
+    width = keep.shape[1]
+    one = pl.BlockSpec((128, width), lambda i: (i, 0))
+    return call(
+        finish_kernel,
+        (5,),
+        [one, one],
+        [full(64, width), full(64, width), pl.BlockSpec((width, 128), lambda i: (0, jnp.maximum(i - 1, 0)))],
+        [arr((64, width)), arr((64, width)), arr((width, 512))],
+        (keep, came),
+        moved=2e6,
     )
 
 
@@ -523,11 +659,12 @@
     bias, bias_t = jnp.asarray(bias), jnp.asarray(bias.T)
     wq_t, wk_t = w_query.T, w_key.T
     taps_qk = jnp.concatenate([taps_query, taps_key], axis=1)
+    taps = jnp.concatenate([taps_qk, taps_value], axis=1)
 
     tail = along(inputs[-16:], 1)
-    proj_qk, proj_v = project(inputs, wq_t, wk_t, w_value)
+    proj_qk, proj_v, wqk_t = project(inputs, wq_t, wk_t, w_value)
     ql, kr, vh, vl, before, own = shard_state(
-        proj_qk, proj_v, tail, wq_t, wk_t, w_value, taps_qk, taps_value, pick_kt, bias_t
+        proj_qk, proj_v, tail, wqk_t, w_value, taps_qk, taps_value, pick_kt, bias_t
     )
     earlier = carried_in(own, False)
     num = inner(ql, kr, vh, vl)
@@ -537,15 +674,15 @@
     after = carried_in(own_grad, True)
     gq, gk, gv = backward(ql, kr, vh, vl, dh, dl, before, earlier, pick_q, bias, back_q)
     rest = (kr, vh, vl, grads, after, gq, gk, gv, pick_k, bias, back_k)
-    aqk, av = later(0, 1, *rest)
-    hqk, hv = along(aqk[:8], -1), along(av[:8], -1)
-    bqk, bv = later(1, CHUNKS, *rest)
-    dqk, dv, dt = unconv(aqk, av, bqk, bv, hqk, hv, taps_qk, taps_value)
-    blocks = lax.all_to_all(input_blocks(dqk, dv, wq_t, wk_t, w_value), "tp", 0, 0)
-    input_grad = jnp.sum(blocks.astype(F32), axis=0).astype(BF16)
-    pieces = lax.all_to_all(weight_blocks(dt, inputs), "seq", 0, 0)
-    summed = jnp.sum(pieces.astype(F32), axis=0)
-    return (outputs, input_grad, summed[0:64].T, summed[64:128].T, summed[128:].T)
+    ga = later(0, 1, *rest)
+    halo = along(ga[:8], -1)
+    gb = later(1, CHUNKS, *rest)
+    d, dt = unconv(ga, gb, halo, taps)
+    blocks = input_products(d, w_value, wqk_t)
+    parts = lax.all_to_all(blocks, "tp", 0, 0)
+    grad_query, grad_key, grad_value = finish_weight_grad(*reduce_weight_grad(dt, inputs, blocks))
+    input_grad = summed(parts, (grad_query,))
+    return (outputs, input_grad, grad_query.T, grad_key.T, grad_value)
 
 
 def solution(mesh):

time: 338 us -> 264 us (0.78)
  waiting for transfers between devices: 150 us -> 66.9 us
  Pallas kernels: 111 us -> 140 us
  blocking collectives: 25.2 us -> 0 us
  starting transfers between devices: 31.9 us -> 42.7 us
  other arithmetic: 9.74 us -> 1.92 us
    all_to_all x2 -> x3, waiting for transfers between devices: 150 us -> 5.26 us  [the longest x2 5.25 us: carried_in(): pieces = lax.all_to_all(state.reshape(count, rows, HDIM), 'seq', 0, 0)]
    ppermute x0 -> x5, waiting for transfers between devices: none -> 61.7 us  [the longest x2 33.5 us: flip(): lax.ppermute(x, axis, [(i, i ^ bit) for i in range(lax.axis_size(axis))])]
    pallas_call x12 -> x17, Pallas kernels: 111 us -> 140 us  [call(): pl.pallas_call(body, grid_spec=pltpu.PrefetchScalarGridSpec(num_scalar_pr...]
    all_to_all x2 -> x0, blocking collectives: 25.2 us -> none  [carried_in(): pieces = lax.all_to_all(state.reshape(count, rows, HDIM), 'seq', 0, 0)]
    reduce_sum x2 -> x0, other arithmetic: 9.12 us -> none  [the longest x1 5.85 us: local(): input_grad = jnp.sum(blocks.astype(F32), axis=0).astype(BF16)]
    ppermute x0 -> x5, starting transfers between devices: none -> 6.79 us  [the longest x3 5.21 us: to_x(): lax.ppermute(x, 'seq', [(s, s // 8 * 8 + (s % 8 + 2 * by) % 8) for s in r...]
    all_to_all x2 -> x3, starting transfers between devices: 13.6 us -> 20.2 us  [the longest x2 12.6 us: carried_in(): pieces = lax.all_to_all(state.reshape(count, rows, HDIM), 'seq', 0, 0)]
    unnamed x15 -> x28, local copies, waits for them, and re-layouts: 3.73 us -> 7.29 us
  transfers between devices with their start and end apart: 7 -> 12, of which waited for: 2 -> 6; matrix products, arithmetic and copies ran while one was open for 2% -> 1% of each run, Pallas kernels for 17% -> 32%
where the time goes in v2:
time: 264 us; the launch traced here: 261 us
  Pallas kernels  140 us (53%)
  waiting for transfers between devices  66.9 us (25%)
  starting transfers between devices  42.7 us (16%)
  local copies, waits for them, and re-layouts  9.02 us (3%)
    pallas_call x17, Pallas kernels, call(): pl.pallas_call(body, grid_spec=pltpu.PrefetchScalarGridSpec(num_scalar_pr...  140 us
    ppermute x2, waiting for transfers between devices, flip(): lax.ppermute(x, axis, [(i, i ^ bit) for i in range(lax.axis_size(axis))])  33.5 us
    ppermute x3, waiting for transfers between devices, to_x(): lax.ppermute(x, 'seq', [(s, s // 8 * 8 + (s % 8 + 2 * by) % 8) for s in r...  28.2 us
    all_to_all x2, starting transfers between devices, carried_in(): pieces = lax.all_to_all(state.reshape(count, rows, HDIM), 'seq', 0, 0)  12.6 us
    all_to_all x2, starting transfers between devices, carried_in(): return lax.all_to_all(sums, 'seq', 0, 0).reshape(HEADS, NF, HDIM)  11.8 us
    all_to_all x1, starting transfers between devices, local(): parts = lax.all_to_all(blocks, 'tp', 0, 0)  7.66 us
    unnamed x28, local copies, waits for them, and re-layouts  7.29 us
  transfers between devices with their start and end apart: 12, of which 6 were waited for; matrix products, arithmetic and copies ran while one was open for 1% of the time, Pallas kernels for 32%

profile of v2, /device:TPU:2, one launch (start us, length us, event | category | flops | bytes accessed | tf_op | source)
XLA Modules:
  0.0 261.0 jit_solution(5304905753665078776)
XLA Ops:
  0.6 0.9 slice.6
  1.6 1.9 collective-permute-start
  3.5 0.0 copy-start.11
  3.5 0.0 copy-start.12
  3.5 11.3 %shard_map.200 = (f32[1024,128]{1,0:T(8,128)}, f32[1024,512]{1,0:T(8,128)}, bf16[128,4096]{1,0:T(8,128)(2,1)}) custom-call(bf16[1024,4096]{1,0:T(8,128)(2,1)} %refs_2_.1, bf16[64,4096]{1,0:T(8,128)(2,1)} %bitcast.24, bf16[64,4096]{1,0:T(8,128)(2,1)} %bitcast.25, bf16[4096,512]{1,0:T(8,128)(2,1)} %wv_ref.5), custom_call_target="tpu_custom_call" | custom-call | flops 5368709120 | bytes 14000000 | tf_op jit(solution)/shard_map/pallas_call | solution.py:101
  14.8 0.0 copy-done.11
  14.8 0.0 copy-done.12
  14.8 0.7 pad_maximum_fusion.1.tqk_ref
  15.4 0.0 collective-permute-done.t_ref
  15.5 0.7 copy-done.13
  16.1 10.6 %shard_map.201 = (bf16[1024,256]{1,0:T(8,128)(2,1)}, bf16[1024,256]{1,0:T(8,128)(2,1)}, bf16[1024,512]{1,0:T(8,128)(2,1)}, bf16[1024,512]{1,0:T(8,128)(2,1)}, f3...) custom-call(f32[1024,128]{1,0:T(8,128)} %get-tuple-element.34.qk_ref.qkp_ref, ...), custom_call_target="tpu_custom_call" | custom-call | flops 4000000000 | bytes 15000000 | tf_op jit(solution)/shard_map/pallas_call | solution.py:101
  26.7 6.8 %all-to-all-start = ((f32[16,40,128]{2,1,0:T(8,128)}), f32[16,40,128]{2,1,0:T(8,128)S(1)}, u32[]{:S(2)}, u32[]{:S(2)}) async-start(f32[16,40,128]{2,1,0:T(8,128)} %bitcast.21), calls=%async_computation | async-start | bytes 655360 | tf_op jit(solution)/shard_map/all_to_all | solution.py:254
  33.5 0.7 pad_maximum_fusion.t_ref
  34.1 5.2 %all-to-all-done.x_ref = f32[16,40,128]{2,1,0:T(8,128)S(1)} async-done(((f32[16,40,128]{2,1,0:T(8,128)}), f32[16,40,128]{2,1,0:T(8,128)S(1)}, u32[]{:S(2)}, u32[]{:S(2)}) %all-to-all-start) | async-done | bytes 327712 | tf_op jit(solution)/shard_map/all_to_all | solution.py:254
  39.4 0.7 copy-done.2
  40.1 1.7 shard_map.203
  41.8 6.0 %all-to-all-start.1 = ((f32[16,40,128]{2,1,0:T(8,128)}), f32[16,40,128]{2,1,0:T(8,128)S(1)}, u32[]{:S(2)}, u32[]{:S(2)}) async-start(f32[16,40,128]{2,1,0:T(8,128)} %shard_map.203), calls=%async_computation.1 | async-start | bytes 655360 | tf_op jit(solution)/shard_map/all_to_all | solution.py:259
  47.9 6.3 %shard_map.202.num_ref = f32[1024,512]{1,0:T(8,128)} custom-call(bf16[1024,256]{1,0:T(8,128)(2,1)} %get-tuple-element.37.ql_ref, bf16[1024,256]{1,0:T(8,128)(2,1)} %get-tuple-element.38.kr_ref, bf16[1024,512]{1,0:T(8,128)(2,1)} %get-tuple-element.39.vh_ref, bf16[1024,512]{1,0:T(8,128)(2,1)} %get-tuple-element.40.vl_ref), custom_call_target="tpu_custom_call" | custom-call | flops 6000000000 | bytes 6000000 | tf_op jit(solution)/shard_map/pallas_call | solution.py:101
  54.2 0.0 all-to-all-done.1
  54.2 0.7 copy-done.7
  54.9 14.2 %shard_map.204 = (f32[1024,512]{1,0:T(8,128)}, bf16[1024,512]{1,0:T(8,128)(2,1)}, bf16[1024,512]{1,0:T(8,128)(2,1)}, f32[4,4,160,128]{3,2,1,0:T(8,128)}, f32[4,160,128]{2,1,0:T(8,128)}) custom-call(bf16[1024,256]{1,0:T(8,128)(2,1)} %get-tuple-element.37.ql_ref, f32[1024,512]{1,0:T(8,128)} %shard_map.202.num_ref, ...), custom_call_target="tpu_custom_call" | custom-call | flops 8000000000 | bytes 12000000 | tf_op jit(solution)/shard_map/pallas_call | solution.py:101
  69.1 5.8 %all-to-all-start.2 = ((f32[16,40,128]{2,1,0:T(8,128)}), f32[16,40,128]{2,1,0:T(8,128)S(1)}, u32[]{:S(2)}, u32[]{:S(2)}) async-start(f32[16,40,128]{2,1,0:T(8,128)} %bitcast.22), calls=%async_computation.2 | async-start | bytes 655360 | tf_op jit(solution)/shard_map/all_to_all | solution.py:254
  74.9 8.1 %shard_map.207 = (f32[1024,128]{1,0:T(8,128)}, f32[1024,512]{1,0:T(8,128)}) custom-call(bf16[1024,256]{1,0:T(8,128)(2,1)} %get-tuple-element.37.ql_ref, bf16[1024,256]{1,0:T(8,128)(2,1)} %get-tuple-element.38.kr_ref, bf16[1024,512]{1,0:T(8,128)(2,1)} %get-tuple-element.39.vh_ref, bf16[1024,512]{1,0:T(8,128)(2,1)} %get-tuple-element.40.vl_ref, ...), custom_call_target="tpu_custom_call" | custom-call | flops 8000000000 | bytes 8000000 | tf_op jit(solution)/shard_map/pallas_call | solution.py:101
  83.0 0.0 all-to-all-done.2.x_ref
  83.0 0.0 copy-start.1
  83.0 0.7 copy-done.1
  83.7 1.7 shard_map.205
  85.5 5.7 %all-to-all-start.3 = ((f32[16,40,128]{2,1,0:T(8,128)}), f32[16,40,128]{2,1,0:T(8,128)S(1)}, u32[]{:S(2)}, u32[]{:S(2)}) async-start(f32[16,40,128]{2,1,0:T(8,128)} %shard_map.205), calls=%async_computation.3 | async-start | bytes 655360 | tf_op jit(solution)/shard_map/all_to_all | solution.py:259
  91.2 13.5 %shard_map.206.gq_ref = f32[1024,128]{1,0:T(8,128)} custom-call(bf16[1024,256]{1,0:T(8,128)(2,1)} %get-tuple-element.37.ql_ref, bf16[1024,256]{1,0:T(8,128)(2,1)} %get-tuple-element.38.kr_ref, bf16[1024,512]{1,0:T(8,128)(2,1)} %get-tuple-element.39.vh_ref, bf16[1024,512]{1,0:T(8,128)(2,1)} %get-tuple-element.40.vl_ref, ...), custom_call_target="tpu_custom_call" | custom-call | flops 8000000000 | bytes 8000000 | tf_op jit(solution)/shard_map/pallas_call | solution.py:101
  104.7 0.0 all-to-all-done.3
  104.7 0.0 copy-start.3
  104.7 0.7 copy-done.3
  105.4 5.9 %shard_map.208.a_ref = f32[256,640]{1,0:T(8,128)} custom-call(bf16[1024,256]{1,0:T(8,128)(2,1)} %get-tuple-element.38.kr_ref, bf16[1024,512]{1,0:T(8,128)(2,1)} %get-tuple-element.39.vh_ref, bf16[1024,512]{1,0:T(8,128)(2,1)} %get-tuple-element.40.vl_ref, f32[4,4,160,128]{3,2,1,0:T(8,128)} %get-tuple-element.44.gs_ref, f32[4,160,128]{2,1,0:T(8,128)} %bitcast.17, ...), custom_call_target="tpu_custom_call" | custom-call | flops 2000000000 | bytes 3000000 | tf_op jit(solution)/shard_map/pallas_call | solution.py:101
  111.4 0.7 slice.8
  112.1 2.0 collective-permute-start.1
  114.1 11.7 %shard_map.209.b_ref = f32[768,640]{1,0:T(8,128)} custom-call(bf16[1024,256]{1,0:T(8,128)(2,1)} %get-tuple-element.38.kr_ref, bf16[1024,512]{1,0:T(8,128)(2,1)} %get-tuple-element.39.vh_ref, bf16[1024,512]{1,0:T(8,128)(2,1)} %get-tuple-element.40.vl_ref, f32[4,4,160,128]{3,2,1,0:T(8,128)} %get-tuple-element.44.gs_ref, f32[4,160,128]{2,1,0:T(8,128)} %bitcast.18, ...), custom_call_target="tpu_custom_call" | custom-call | flops 6000000000 | bytes 9000000 | tf_op jit(solution)/shard_map/pallas_call | solution.py:101
  125.8 0.0 collective-permute-done.1.h_ref
  125.8 0.0 copy-start.9
  125.8 0.6 copy-done.9
  126.4 4.1 %shard_map.210 = (bf16[1024,640]{1,0:T(8,128)(2,1)}, bf16[640,1024]{1,0:T(8,128)(2,1)}) custom-call(f32[256,640]{1,0:T(8,128)} %shard_map.208.a_ref, f32[768,640]{1,0:T(8,128)} %shard_map.209.b_ref, f32[8,640]{1,0:T(8,128)} %copy-done.9, f32[3,640]{1,0:T(4,128)} %pad_maximum_fusion.t_ref), custom_call_target="tpu_custom_call" | custom-call | bytes 6000000 | tf_op jit(solution)/shard_map/pallas_call | solution.py:101
  130.6 11.9 %shard_map.211.refs_3_ = bf16[8,1024,512]{2,1,0:T(8,128)(2,1)} custom-call(bf16[1024,640]{1,0:T(8,128)(2,1)} %get-tuple-element.50.d_ref, bf16[4096,512]{1,0:T(8,128)(2,1)} %wv_ref.5, bf16[128,4096]{1,0:T(8,128)(2,1)} %get-tuple-element.36.wqk_ref), custom_call_target="tpu_custom_call" | custom-call | flops 5368709120 | bytes 15000000 | tf_op jit(solution)/shard_map/pallas_call | solution.py:101
  142.5 7.7 %all-to-all-start.4 = ((bf16[8,1024,512]{2,1,0:T(8,128)(2,1)}), bf16[8,1024,512]{2,1,0:T(8,128)(2,1)}, u32[]{:S(2)}, u32[]{:S(2)}) async-start(bf16[8,1024,512]{2,1,0:T(8,128)(2,1)} %shard_map.211.refs_3_), calls=%async_computation.4 | async-start | bytes 16777216 | tf_op jit(solution)/shard_map/all_to_all | solution.py:682
  150.2 0.1 stack.35
  150.3 0.6 pad_add_fusion.refs_0_
  150.9 16.3 %shard_map.212 = (bf16[8,640,256]{2,1,0:T(8,128)(2,1)}, bf16[8,640,256]{2,1,0:T(8,128)(2,1)}) custom-call(s32[16]{0:T(128)} %pad_add_fusion.refs_0_, bf16[640,1024]{1,0:T(8,128)(2,1)} %get-tuple-element.51.refs_1_, bf16[1024,4096]{1,0:T(8,128)(2,1)} %refs_2_.1, bf16[8,1024,512]{2,1,0:T(8,128)(2,1)} %shard_map.211.refs_3_), custom_call_target="tpu_custom_call" | custom-call | flops 5368709120 | bytes 15000000 | tf_op jit(solution)/shard_map/pallas_call | solution.py:101
  167.2 0.2 collective-permute-start.2
  167.4 5.0 %collective-permute-done.2.came_ref = bf16[8,640,256]{2,1,0:T(8,128)(2,1)S(1)} collective-permute-done((bf16[8,640,256]{2,1,0:T(8,128)(2,1)}, bf16[8,640,256]{2,1,0:T(8,128)(2,1)S(1)}, u32[]{:S(2)}, u32[]{:S(2)}) %collective-permute-start.2) | collective-permute-done | bytes 2621472 | tf_op jit(solution)/shard_map/ppermute | solution.py:499
  172.3 1.5 copy-done
  173.8 7.1 %shard_map.213 = (bf16[2,640,256]{2,1,0:T(8,128)(2,1)}, bf16[2,640,256]{2,1,0:T(8,128)(2,1)}, bf16[2,640,256]{2,1,0:T(8,128)(2,1)}, bf16[2,640,256]{2,1,0:T(8,128)(2,1)}) custom-call(bf16[8,640,256]{2,1,0:T(8,128)(2,1)} %get-tuple-element.52.mine_ref, bf16[8,640,256]{2,1,0:T(8,128)(2,1)} %copy-done), custom_call_target="tpu_custom_call" | custom-call | bytes 8000000 | tf_op jit(solution)/shard_map/pallas_call | solution.py:101
  181.0 1.7 collective-permute-start.3
  182.7 1.0 collective-permute-start.4
  183.6 2.6 collective-permute-start.5
  186.2 12.6 %collective-permute-done.3.a_ref = bf16[2,640,256]{2,1,0:T(8,128)(2,1)S(1)} collective-permute-done((bf16[2,640,256]{2,1,0:T(8,128)(2,1)}, bf16[2,640,256]{2,1,0:T(8,128)(2,1)S(1)}, u32[]{:S(2)}, u32[]{:S(2)}) %collective-permute-start.3) | collective-permute-done | bytes 655392 | tf_op jit(solution)/shard_map/ppermute | solution.py:584
  198.8 3.2 %collective-permute-done.4.b_ref = bf16[2,640,256]{2,1,0:T(8,128)(2,1)S(1)} collective-permute-done((bf16[2,640,256]{2,1,0:T(8,128)(2,1)}, bf16[2,640,256]{2,1,0:T(8,128)(2,1)S(1)}, u32[]{:S(2)}, u32[]{:S(2)}) %collective-permute-start.4) | collective-permute-done | bytes 655392 | tf_op jit(solution)/shard_map/ppermute | solution.py:584
  202.0 12.4 %collective-permute-done.5.c_ref = bf16[2,640,256]{2,1,0:T(8,128)(2,1)S(1)} collective-permute-done((bf16[2,640,256]{2,1,0:T(8,128)(2,1)}, bf16[2,640,256]{2,1,0:T(8,128)(2,1)S(1)}, u32[]{:S(2)}, u32[]{:S(2)}) %collective-permute-start.5) | collective-permute-done | bytes 655392 | tf_op jit(solution)/shard_map/ppermute | solution.py:584
  214.4 0.0 copy-done.5
  214.4 0.8 copy-done.6
  215.2 4.2 %shard_map.214 = (f32[640,256]{1,0:T(8,128)}, bf16[640,256]{1,0:T(8,128)(2,1)}) custom-call(bf16[2,640,256]{2,1,0:T(8,128)(2,1)} %get-tuple-element.54.mine_ref, bf16[2,640,256]{2,1,0:T(8,128)(2,1)} %copy-done.4, bf16[2,640,256]{2,1,0:T(8,128)(2,1)} %copy-done.5, bf16[2,640,256]{2,1,0:T(8,128)(2,1)} %copy-done.6), custom_call_target="tpu_custom_call" | custom-call | bytes 4000000 | tf_op jit(solution)/shard_map/pallas_call | solution.py:101
  219.5 1.4 collective-permute-start.6
  220.9 28.5 %collective-permute-done.6.came_ref = bf16[640,256]{1,0:T(8,128)(2,1)S(1)} collective-permute-done((bf16[640,256]{1,0:T(8,128)(2,1)}, bf16[640,256]{1,0:T(8,128)(2,1)S(1)}, u32[]{:S(2)}, u32[]{:S(2)}) %collective-permute-start.6) | collective-permute-done | bytes 327712 | tf_op jit(solution)/shard_map/ppermute | solution.py:499
  249.4 0.7 copy-done.8
  250.1 3.8 %shard_map.215 = (f32[64,256]{1,0:T(8,128)}, f32[64,256]{1,0:T(8,128)}, f32[256,512]{1,0:T(8,128)}) custom-call(f32[640,256]{1,0:T(8,128)} %get-tuple-element.58.keep_ref, bf16[640,256]{1,0:T(8,128)(2,1)} %copy-done.8), custom_call_target="tpu_custom_call" | custom-call | bytes 2000000 | tf_op jit(solution)/shard_map/pallas_call | solution.py:101
  253.9 0.0 all-to-all-done.4.refs_0_
  253.9 7.1 %shard_map.216 = bf16[1024,512]{1,0:T(8,128)(2,1)} custom-call(bf16[8,1024,512]{2,1,0:T(8,128)(2,1)} %all-to-all-done.4.refs_0_, f32[64,256]{1,0:T(8,128)} %get-tuple-element.60.refs_1_), custom_call_target="tpu_custom_call" | custom-call | bytes 9000000 | tf_op jit(solution)/shard_map/pallas_call | solution.py:101
  (12 shorter events, 0.0 us)
Async XLA Ops:
  1.6 13.9 %collective-permute-start = (bf16[16,4096]{1,0:T(8,128)(2,1)S(1)}, bf16[16,4096]{1,0:T(8,128)(2,1)S(1)}, u32[]{:S(2)}, u32[]{:S(2)}) collective-permute-start(bf16[16,4096]{1,0:T(8,128)(2,1)S(1)} %slice.6), channel_id=1, source_target_pairs={{0,8},{8,16},{16,24},{24,32},{32,40},{40,48},{48,56},{56,64},{64,7... | collective-permute-start | bytes 393224 | tf_op jit(solution)/shard_map/ppermute | solution.py:651
  3.5 11.3 %copy-start.11 = (f32[3,64]{1,0:T(4,128)S(1)}, f32[3,64]{1,0:T(4,128)}, u32[]{:S(2)}) copy-start(f32[3,64]{1,0:T(4,128)} %param.22) | copy-start | bytes 2308
  3.5 11.3 %copy-start.12 = (f32[3,64]{1,0:T(4,128)S(1)}, f32[3,64]{1,0:T(4,128)}, u32[]{:S(2)}) copy-start(f32[3,64]{1,0:T(4,128)} %param.21) | copy-start | bytes 2308
  15.5 0.7 copy-start.13
  16.1 17.3 %copy-start.10 = (f32[3,512]{1,0:T(4,128)S(1)}, f32[3,512]{1,0:T(4,128)}, u32[]{:S(2)}) copy-start(f32[3,512]{1,0:T(4,128)} %tv_ref.1) | copy-start | bytes 18436
  26.7 12.7 %all-to-all-start = ((f32[16,40,128]{2,1,0:T(8,128)}), f32[16,40,128]{2,1,0:T(8,128)S(1)}, u32[]{:S(2)}, u32[]{:S(2)}) async-start(f32[16,40,128]{2,1,0:T(8,128)} %bitcast.21), calls=%async_computation | async-start | bytes 655360 | tf_op jit(solution)/shard_map/all_to_all | solution.py:254
  39.4 0.7 copy-start.2
  41.8 12.4 %all-to-all-start.1 = ((f32[16,40,128]{2,1,0:T(8,128)}), f32[16,40,128]{2,1,0:T(8,128)S(1)}, u32[]{:S(2)}, u32[]{:S(2)}) async-start(f32[16,40,128]{2,1,0:T(8,128)} %shard_map.203), calls=%async_computation.1 | async-start | bytes 655360 | tf_op jit(solution)/shard_map/all_to_all | solution.py:259
  54.2 0.7 copy-start.7
  69.1 13.9 %all-to-all-start.2 = ((f32[16,40,128]{2,1,0:T(8,128)}), f32[16,40,128]{2,1,0:T(8,128)S(1)}, u32[]{:S(2)}, u32[]{:S(2)}) async-start(f32[16,40,128]{2,1,0:T(8,128)} %bitcast.22), calls=%async_computation.2 | async-start | bytes 655360 | tf_op jit(solution)/shard_map/all_to_all | solution.py:254
  83.0 0.7 copy-start.1
  85.5 19.2 %all-to-all-start.3 = ((f32[16,40,128]{2,1,0:T(8,128)}), f32[16,40,128]{2,1,0:T(8,128)S(1)}, u32[]{:S(2)}, u32[]{:S(2)}) async-start(f32[16,40,128]{2,1,0:T(8,128)} %shard_map.205), calls=%async_computation.3 | async-start | bytes 655360 | tf_op jit(solution)/shard_map/all_to_all | solution.py:259
  104.7 0.8 copy-start.3
  112.1 13.7 %collective-permute-start.1 = (f32[8,640]{1,0:T(8,128)S(1)}, f32[8,640]{1,0:T(8,128)S(1)}, u32[]{:S(2)}, u32[]{:S(2)}) collective-permute-start(f32[8,640]{1,0:T(8,128)S(1)} %slice.8), channel_id=1, source_target_pairs={{8,0},{16,8},{24,16},{32,24},{40,32},{48,40},{56,48},{64,56},{72,6... | collective-permute-start | bytes 61448 | tf_op jit(solution)/shard_map/ppermute | solution.py:651
  125.8 0.6 copy-start.9
  142.5 111.4 %all-to-all-start.4 = ((bf16[8,1024,512]{2,1,0:T(8,128)(2,1)}), bf16[8,1024,512]{2,1,0:T(8,128)(2,1)}, u32[]{:S(2)}, u32[]{:S(2)}) async-start(bf16[8,1024,512]{2,1,0:T(8,128)(2,1)} %shard_map.211.refs_3_), calls=%async_computation.4 | async-start | bytes 16777216 | tf_op jit(solution)/shard_map/all_to_all | solution.py:682
  167.2 5.1 %collective-permute-start.2 = (bf16[8,640,256]{2,1,0:T(8,128)(2,1)}, bf16[8,640,256]{2,1,0:T(8,128)(2,1)S(1)}, u32[]{:S(2)}, u32[]{:S(2)}) collective-permute-start(bf16[8,640,256]{2,1,0:T(8,128)(2,1)} %get-tuple-element.53), channel_id=1, source_target_pairs={{0,8},{8,0},{16,24},{24,16},{32,40},{40,32},{48,56},{56,48},{64,72... | collective-permute-start | bytes 7864328 | tf_op jit(solution)/shard_map/ppermute | solution.py:499
  172.3 1.5 copy-start
  181.0 17.8 %collective-permute-start.3 = (bf16[2,640,256]{2,1,0:T(8,128)(2,1)}, bf16[2,640,256]{2,1,0:T(8,128)(2,1)S(1)}, u32[]{:S(2)}, u32[]{:S(2)}) collective-permute-start(bf16[2,640,256]{2,1,0:T(8,128)(2,1)} %get-tuple-element.55), channel_id=1, source_target_pairs={{0,16},{8,24},{16,32},{24,40},{32,48},{40,56},{48,0},{56,8},{64,80... | collective-permute-start | bytes 1966088 | tf_op jit(solution)/shard_map/ppermute | solution.py:584
  182.7 19.3 %collective-permute-start.4 = (bf16[2,640,256]{2,1,0:T(8,128)(2,1)}, bf16[2,640,256]{2,1,0:T(8,128)(2,1)S(1)}, u32[]{:S(2)}, u32[]{:S(2)}) collective-permute-start(bf16[2,640,256]{2,1,0:T(8,128)(2,1)} %get-tuple-element.56), channel_id=1, source_target_pairs={{0,32},{8,40},{16,48},{24,56},{32,0},{40,8},{48,16},{56,24},{64,96... | collective-permute-start | bytes 1966088 | tf_op jit(solution)/shard_map/ppermute | solution.py:584
  183.6 30.7 %collective-permute-start.5 = (bf16[2,640,256]{2,1,0:T(8,128)(2,1)}, bf16[2,640,256]{2,1,0:T(8,128)(2,1)S(1)}, u32[]{:S(2)}, u32[]{:S(2)}) collective-permute-start(bf16[2,640,256]{2,1,0:T(8,128)(2,1)} %get-tuple-element.57), channel_id=1, source_target_pairs={{0,48},{8,56},{16,0},{24,8},{32,16},{40,24},{48,32},{56,40},{64,11... | collective-permute-start | bytes 1966088 | tf_op jit(solution)/shard_map/ppermute | solution.py:584
  198.8 15.6 %copy-start.4 = (bf16[2,640,256]{2,1,0:T(8,128)(2,1)}, bf16[2,640,256]{2,1,0:T(8,128)(2,1)S(1)}, u32[]{:S(2)}) copy-start(bf16[2,640,256]{2,1,0:T(8,128)(2,1)S(1)} %collective-permute-done.3.a_ref) | copy-start | bytes 1966084
  202.0 12.4 %copy-start.5 = (bf16[2,640,256]{2,1,0:T(8,128)(2,1)}, bf16[2,640,256]{2,1,0:T(8,128)(2,1)S(1)}, u32[]{:S(2)}) copy-start(bf16[2,640,256]{2,1,0:T(8,128)(2,1)S(1)} %collective-permute-done.4.b_ref) | copy-start | bytes 1966084
  214.4 0.8 copy-start.6
  219.5 29.9 %collective-permute-start.6 = (bf16[640,256]{1,0:T(8,128)(2,1)}, bf16[640,256]{1,0:T(8,128)(2,1)S(1)}, u32[]{:S(2)}, u32[]{:S(2)}) collective-permute-start(bf16[640,256]{1,0:T(8,128)(2,1)} %get-tuple-element.59), channel_id=1, source_target_pairs={{0,64},{8,72},{16,80},{24,88},{32,96},{40,104},{48,112},{56,120},{... | collective-permute-start | bytes 983048 | tf_op jit(solution)/shard_map/ppermute | solution.py:499
  249.4 0.7 copy-start.8

commit v3 on v2

--- a/solution.py
+++ b/solution.py
@@ -117,29 +117,46 @@
     return jax.ShapeDtypeStruct(shape, dtype)
 
 
-def project_kernel(x_ref, wq_ref, wk_ref, wv_ref, qk_ref, v_ref, wqk):
-    @pl.when(pl.program_id(0) == 0)
-    def _():
-        wqk[0:64] = wq_ref[...]
-        wqk[64:128] = wk_ref[...]
-
+def end_kernel(x_ref, wq_ref, wk_ref, wv_ref, o_ref, wqk_ref):
+    wqk_ref[0:64] = wq_ref[...]
+    wqk_ref[64:128] = wk_ref[...]
     x = x_ref[...]
-    qk_ref[...] = nt(x, wqk[...])
-    v_ref[...] = nn(x, wv_ref[...])
-
-
-def project(x, wq_t, wk_t, wv):
+    o_ref[:, :128] = nt(x, wqk_ref[...])
+    o_ref[:, 128:] = nn(x, wv_ref[...])
+
+
+def project_end(x, wq_t, wk_t, wv):
+    depth = x.shape[1]
+    return call(
+        end_kernel,
+        (1,),
+        [pl.BlockSpec((CHUNK, depth), lambda c: (CHUNKS - 1, 0)), full(64, depth), full(64, depth), full(depth, 512)],
+        [full(CHUNK, 640), full(128, depth)],
+        [arr((CHUNK, 640)), arr((128, depth), BF16)],
+        (x, wq_t, wk_t, wv),
+        flops=2 * CHUNK * depth * 640,
+        moved=8e6,
+    )
+
+
+def project_kernel(x_ref, wqk_ref, wv_ref, o_ref):
+    x = x_ref[...]
+    o_ref[:, :128] = nt(x, wqk_ref[...])
+    o_ref[:, 128:] = nn(x, wv_ref[...])
+
+
+def project(x, wqk_t, wv):
     depth = x.shape[1]
     rows = lambda c: (c, 0)
     return call(
         project_kernel,
-        (CHUNKS,),
-        [pl.BlockSpec((CHUNK, depth), rows), full(64, depth), full(64, depth), full(depth, 512)],
-        [pl.BlockSpec((CHUNK, 128), rows), pl.BlockSpec((CHUNK, 512), rows), full(128, depth)],
-        [arr((LEN, 128)), arr((LEN, 512)), arr((128, depth), BF16)],
-        (x, wq_t, wk_t, wv),
-        flops=2 * LEN * depth * 640,
-        moved=14e6,
+        (CHUNKS - 1,),
+        [pl.BlockSpec((CHUNK, depth), rows), full(128, depth), full(depth, 512)],
+        pl.BlockSpec((CHUNK, 640), rows),
+        arr((LEN - CHUNK, 640)),
+        (x, wqk_t, wv),
+        flops=2 * (LEN - CHUNK) * depth * 640,
+        moved=12e6,
     )
 
 
@@ -154,25 +171,18 @@
 
 
 def state_kernel(
-    qk_ref, v_ref, qkp_ref, vp_ref, t_ref, wqk_ref, wv_ref, tqk_ref, tv_ref, pick_ref, biast_ref,
-    ql_ref, kr_ref, vh_ref, vl_ref, sp_ref, st_ref, tail_qk, tail_v,
+    a_ref, b_ref, before_ref, tail_ref, taps_ref, pick_ref, biast_ref,
+    ql_ref, kr_ref, vh_ref, vl_ref, sp_ref, st_ref,
 ):
     c = pl.program_id(0)
 
     @pl.when(c == 0)
     def _():
-        t = t_ref[...]
-        tail_qk[...] = nt(t, wqk_ref[...])[8:16]
-        tail_v[...] = nn(t, wv_ref[...])[8:16]
         st_ref[...] = jnp.zeros_like(st_ref)
 
-    @pl.when(c > 0)
-    def _():
-        tail_qk[...] = qkp_ref[...]
-        tail_v[...] = vp_ref[...]
-
-    qk = conv(qk_ref[...], tail_qk[...], tqk_ref[...]) * 0.5
-    v = conv(v_ref[...], tail_v[...], tv_ref[...])
+    x = jnp.where(c < CHUNKS - 1, a_ref[...], b_ref[...])
+    both = conv(x, jnp.where(c > 0, before_ref[...], tail_ref[...]), taps_ref[...])
+    qk, v = both[:, :128] * 0.5, both[:, 128:]
     lane = lax.broadcasted_iota(jnp.int32, (1, 128), 1)
     low = lane < 64
     turned = pltpu.roll(qk, 64, 1)
@@ -196,23 +206,18 @@
         st_ref[head] += own
 
 
-def shard_state(qk, v, tail, wqk_t, wv, taps_qk, taps_v, pick_kt, bias_t):
-    depth = tail.shape[1]
+def shard_state(proj, end, tail, taps, pick_kt, bias_t):
     rows = lambda c: (c, 0)
     before = lambda c: (jnp.maximum(c * (CHUNK // 8) - 1, 0), 0)
     return call(
         state_kernel,
         (CHUNKS,),
         [
-            pl.BlockSpec((CHUNK, 128), rows),
-            pl.BlockSpec((CHUNK, 512), rows),
-            pl.BlockSpec((8, 128), before),
-            pl.BlockSpec((8, 512), before),
-            full(16, depth),
-            full(128, depth),
-            full(depth, 512),
-            full(3, 128),
-            full(3, 512),
+            pl.BlockSpec((CHUNK, 640), lambda c: (jnp.minimum(c, CHUNKS - 2), 0)),
+            full(CHUNK, 640),
+            pl.BlockSpec((8, 640), before),
+            full(8, 640),
+            full(3, 640),
             full(HEADS, 2 * WIDE, WIDE),
             full(2 * WIDE, 1),
         ],
@@ -232,8 +237,7 @@
             arr((CHUNKS, HEADS, NF, HDIM)),
             arr((HEADS, NF, HDIM)),
         ],
-        (qk, v, qk, v, tail, wqk_t, wv, taps_qk, taps_v, pick_kt, bias_t),
-        [pltpu.VMEM((8, 128), F32), pltpu.VMEM((8, 512), F32)],
+        (proj, end, proj, tail, taps, pick_kt, bias_t),
         flops=4e9,
         moved=15e6,
     )
@@ -345,13 +349,11 @@
         v_hi, v_lo = vh_ref[:, cols(head)], vl_ref[:, cols(head)]
         d_hi, d_lo = dh_ref[:, cols(head)], dl_ref[:, cols(head)]
         slope = jnp.where(causal, 1.0 + nt(q, kr), 0.0)
-        ds_hi, ds_lo = halves(nt3(d_hi, d_lo, v_hi, v_lo) * slope)
-        gq = gq + nn(ds_hi, k) + nn(ds_lo, k)
+        gq = gq + nn((nt3(d_hi, d_lo, v_hi, v_lo) * slope).astype(BF16), k)
         s_hi, s_lo = halves(padded(sp_ref[0, head] + se_ref[head]))
         dp = nt3(d_hi, d_lo, s_hi, s_lo)
         a, b = factors(ql, pick_ref[head], bias_ref[...])
-        dab_hi, dab_lo = halves(side(dp * b, dp * a))
-        du = du + nn(dab_hi, back_ref[head]) + nn(dab_lo, back_ref[head])
+        du = du + nn(side(dp * b, dp * a).astype(BF16), back_ref[head])
     gq_ref[...] = gq[:, :128] + gq[:, 128:] + du
 
 
@@ -419,13 +421,12 @@
     du = jnp.zeros((CHUNK, 128), F32)
     for head in range(HEADS):
         a, b = factors(kr, pick_ref[head], bias_ref[...])
-        p_hi, p_lo = halves(a * b)
         l_hi, l_lo = halves(padded(total[head]))
+        gained = nn((a * b).astype(BF16), side(l_hi, l_lo))
         v_hi, v_lo = vh_ref[:, cols(head)], vl_ref[:, cols(head)]
-        o_ref[:, 128 + head * HDIM : 256 + head * HDIM] = gv_ref[:, cols(head)] + nn3(p_hi, p_lo, l_hi, l_lo)
-        dp = nt3(v_hi, v_lo, l_hi, l_lo)
-        dab_hi, dab_lo = halves(side(dp * b, dp * a))
-        du = du + nn(dab_hi, back_ref[head]) + nn(dab_lo, back_ref[head])
+        o_ref[:, 128 + head * HDIM : 256 + head * HDIM] = gv_ref[:, cols(head)] + gained[:, :HDIM] + gained[:, HDIM:]
+        dp = nt(side(v_hi, v_lo), side(l_hi, l_hi))
+        du = du + nn(side(dp * b, dp * a).astype(BF16), back_ref[head])
     low = lax.broadcasted_iota(jnp.int32, (1, 128), 1) < 64
     o_ref[:, :128] = 0.5 * jnp.where(low, gq_ref[...], pltpu.roll(gk_ref[...] + du, 64, 1))
     total[...] += gs_ref[last - 1 - pl.program_id(0)]
@@ -464,33 +465,6 @@
     return (taps[0:1] * x + taps[1:2] * once + taps[2:3] * twice).astype(BF16)
 
 
-def unconv_kernel(a_ref, b_ref, h_ref, t_ref, d_ref, dt_ref):
-    n = a_ref.shape[0]
-    for start in range(0, LEN, STEP):
-        end = start + STEP
-        src = a_ref[start:end] if start < n else b_ref[start - n : end - n]
-        if end == LEN:
-            tail = h_ref[...]
-        else:
-            tail = a_ref[end : end + 8] if end < n else b_ref[end - n : end - n + 8]
-        got = conv_back(src, tail, t_ref[...])
-        d_ref[start:end] = got
-        dt_ref[:, start:end] = got.T
-
-
-def unconv(a, b, halo, taps):
-    n, m = a.shape[0], b.shape[0]
-    return call(
-        unconv_kernel,
-        (1,),
-        [full(n, 640), full(m, 640), full(8, 640), full(3, 640)],
-        [full(LEN, 640), full(640, LEN)],
-        [arr((LEN, 640), BF16), arr((640, LEN), BF16)],
-        (a, b, halo, taps),
-        moved=6e6,
-    )
-
-
 def f32(x):
     return x.astype(F32)
 
@@ -499,56 +473,53 @@
     return lax.ppermute(x, axis, [(i, i ^ bit) for i in range(lax.axis_size(axis))])
 
 
-def input_kernel(d_ref, wv_ref, wqk_ref, o_ref):
+def input_kernel(a_ref, b_ref, h_ref, t_ref, wv_ref, wqk_ref, o_ref, dt_ref, d_ref):
+    @pl.when(pl.program_id(0) == 0)
+    def _():
+        n = a_ref.shape[0]
+        for start in range(0, LEN, STEP):
+            end = start + STEP
+            src = a_ref[start:end] if start < n else b_ref[start - n : end - n]
+            if end == LEN:
+                tail = h_ref[...]
+            else:
+                tail = a_ref[end : end + 8] if end < n else b_ref[end - n : end - n + 8]
+            got = conv_back(src, tail, t_ref[...])
+            d_ref[start:end] = got
+            dt_ref[:, start:end] = got.T
+
     d = d_ref[...]
-    o_ref[0] = (nt(d[:, 128:], wv_ref[...]) + nn(d[:, :128], wqk_ref[...])).astype(BF16)
-
-
-def input_products(d, wv, wqk):
-    parts = wv.shape[0] // 512
+    for i in range(o_ref.shape[0]):
+        part = slice(512 * i, 512 * (i + 1))
+        o_ref[i] = (nt(d[:, 128:], wv_ref[part]) + nn(d[:, :128], wqk_ref[:, part])).astype(BF16)
+
+
+def input_products(a, b, halo, taps, wv, wqk):
+    parts, wide = wv.shape[0] // 512, 2
+    n, m = a.shape[0], b.shape[0]
     return call(
         input_kernel,
-        (parts,),
-        [full(LEN, 640), pl.BlockSpec((512, 512), lambda i: (i, 0)), pl.BlockSpec((128, 512), lambda i: (0, i))],
-        pl.BlockSpec((1, LEN, 512), lambda i: (i, 0, 0)),
-        arr((parts, LEN, 512), BF16),
-        (d, wv, wqk),
+        (parts // wide,),
+        [
+            full(n, 640), full(m, 640), full(8, 640), full(3, 640),
+            pl.BlockSpec((512 * wide, 512), lambda i: (i, 0)), pl.BlockSpec((128, 512 * wide), lambda i: (0, i)),
+        ],
+        [pl.BlockSpec((wide, LEN, 512), lambda i: (i, 0, 0)), full(640, LEN)],
+        [arr((parts, LEN, 512), BF16), arr((640, LEN), BF16)],
+        (a, b, halo, taps, wv, wqk),
+        [pltpu.VMEM((LEN, 640), BF16)],
         flops=2 * LEN * 640 * 4096,
-        moved=15e6,
-    )
-
-
-def sum_kernel(p_ref, o_ref):
-    total = f32(p_ref[0])
-    for i in range(1, p_ref.shape[0]):
-        total = total + f32(p_ref[i])
-    o_ref[...] = total.astype(BF16)
-
-
-def summed(parts, after):
-    count, rows, width = parts.shape
-    return call(
-        sum_kernel,
-        (8,),
-        [pl.BlockSpec((count, rows // 8, width), lambda i: (0, i, 0))],
-        pl.BlockSpec((rows // 8, width), lambda i: (i, 0)),
-        arr((rows, width), BF16),
-        (parts,),
-        moved=9e6,
-        after=after,
+        moved=18e6,
     )
 
 
 def weight_kernel(dest_ref, d_ref, x_ref, theirs_ref, ours_ref):
     got = nn(d_ref[...], x_ref[...]).astype(BF16)
-
-    @pl.when(pl.program_id(0) < 8)
-    def _():
-        theirs_ref[0] = got
-
-    @pl.when(pl.program_id(0) >= 8)
-    def _():
-        ours_ref[0] = got
+    half = got.shape[1] // 2
+    low, high = got[:, :half], got[:, half:]
+    first = dest_ref[8] == 0
+    theirs_ref[0] = jnp.where(first, high, low)
+    ours_ref[0] = jnp.where(first, low, high)
 
 
 def split_kernel(mine_ref, came_ref, *outs):
@@ -588,16 +559,13 @@
     me = lax.axis_index("seq")
     y, px, core = me // 8, me // 2 % 4, me % 2
     width = x.shape[1] // 16
-    chips = jnp.stack([((y ^ r) * 4 + (px + dx) % 4) * 2 for dx in range(4) for r in range(2)])
-    dest = jnp.concatenate([chips + 1 - core, chips + core]).astype(jnp.int32)
+    chips = [(y ^ r) * 4 + (px + dx) % 4 for dx in range(4) for r in range(2)]
+    dest = jnp.stack([*chips, core]).astype(jnp.int32)
     theirs, ours = call(
         weight_kernel,
-        (16,),
-        [pl.BlockSpec((640, LEN), lambda i, dest: (0, 0)), pl.BlockSpec((LEN, width), lambda i, dest: (0, dest[i]))],
-        [
-            pl.BlockSpec((1, 640, width), lambda i, dest: (jnp.minimum(i, 7), 0, 0)),
-            pl.BlockSpec((1, 640, width), lambda i, dest: (jnp.maximum(i - 8, 0), 0, 0)),
-        ],
+        (8,),
+        [pl.BlockSpec((640, LEN), lambda i, dest: (0, 0)), pl.BlockSpec((LEN, 2 * width), lambda i, dest: (0, dest[i]))],
+        [pl.BlockSpec((1, 640, width), lambda i, dest: (i, 0, 0))] * 2,
         [arr((8, 640, width), BF16)] * 2,
         (dest, dt, x),
         prefetch=1,
@@ -658,14 +626,12 @@
     back_q, back_k = (jnp.asarray(back[i], BF16) for i in range(2))
     bias, bias_t = jnp.asarray(bias), jnp.asarray(bias.T)
     wq_t, wk_t = w_query.T, w_key.T
-    taps_qk = jnp.concatenate([taps_query, taps_key], axis=1)
-    taps = jnp.concatenate([taps_qk, taps_value], axis=1)
-
-    tail = along(inputs[-16:], 1)
-    proj_qk, proj_v, wqk_t = project(inputs, wq_t, wk_t, w_value)
-    ql, kr, vh, vl, before, own = shard_state(
-        proj_qk, proj_v, tail, wqk_t, w_value, taps_qk, taps_value, pick_kt, bias_t
-    )
+    taps = jnp.concatenate([taps_query, taps_key, taps_value], axis=1)
+
+    end, wqk_t = project_end(inputs, wq_t, wk_t, w_value)
+    tail = along(end[-8:], 1)
+    proj = project(inputs, wqk_t, w_value)
+    ql, kr, vh, vl, before, own = shard_state(proj, end, tail, taps, pick_kt, bias_t)
     earlier = carried_in(own, False)
     num = inner(ql, kr, vh, vl)
     outputs, dh, dl, grads, own_grad = forward(
@@ -677,11 +643,10 @@
     ga = later(0, 1, *rest)
     halo = along(ga[:8], -1)
     gb = later(1, CHUNKS, *rest)
-    d, dt = unconv(ga, gb, halo, taps)
-    blocks = input_products(d, w_value, wqk_t)
+    blocks, dt = input_products(ga, gb, halo, taps, w_value, wqk_t)
     parts = lax.all_to_all(blocks, "tp", 0, 0)
     grad_query, grad_key, grad_value = finish_weight_grad(*reduce_weight_grad(dt, inputs, blocks))
-    input_grad = summed(parts, (grad_query,))
+    input_grad = jnp.sum(parts.astype(F32), axis=0).astype(BF16)
     return (outputs, input_grad, grad_query.T, grad_key.T, grad_value)
 
 

time: 264 us -> 251 us (0.951)
  Pallas kernels: 140 us -> 117 us
  blocking collectives: 0 us -> 12.8 us
  starting transfers between devices: 42.7 us -> 35.8 us
  other arithmetic: 1.92 us -> 6.53 us
    pallas_call x17 -> x16, Pallas kernels: 140 us -> 117 us  [call(): pl.pallas_call(body, grid_spec=pltpu.PrefetchScalarGridSpec(num_scalar_pr...]
    all_to_all x0 -> x1, blocking collectives: none -> 12.8 us  [carried_in(): pieces = lax.all_to_all(state.reshape(count, rows, HDIM), 'seq', 0, 0)]
    all_to_all x2 -> x1, starting transfers between devices: 12.6 us -> 5.8 us  [carried_in(): pieces = lax.all_to_all(state.reshape(count, rows, HDIM), 'seq', 0, 0)]
    reduce_sum x0 -> x1, other arithmetic: none -> 5.85 us  [local(): input_grad = jnp.sum(parts.astype(F32), axis=0).astype(BF16)]
    all_to_all x2 -> x1, waiting for transfers between devices: 5.25 us -> 0.01 us  [carried_in(): pieces = lax.all_to_all(state.reshape(count, rows, HDIM), 'seq', 0, 0)]
    ppermute x2, waiting for transfers between devices: 33.5 us -> 37.9 us  [flip(): lax.ppermute(x, axis, [(i, i ^ bit) for i in range(lax.axis_size(axis))])]
    unnamed x28 -> x26, local copies, waits for them, and re-layouts: 7.29 us -> 6.48 us
  transfers between devices with their start and end apart: 12 -> 11, of which waited for: 6 -> 5; matrix products, arithmetic and copies ran while one was open for 1% -> 1% of each run, Pallas kernels for 32% -> 28%
where the time goes in v3:
time: 251 us; the launch traced here: 248 us
  Pallas kernels  117 us (47%)
  waiting for transfers between devices  66.1 us (26%)
  starting transfers between devices  35.8 us (14%)
  blocking collectives  12.8 us (5%)
  local copies, waits for them, and re-layouts  8.54 us (3%)
  other arithmetic  6.53 us (3%)
    pallas_call x16, Pallas kernels, call(): pl.pallas_call(body, grid_spec=pltpu.PrefetchScalarGridSpec(num_scalar_pr...  117 us
    ppermute x2, waiting for transfers between devices, flip(): lax.ppermute(x, axis, [(i, i ^ bit) for i in range(lax.axis_size(axis))])  37.9 us
    ppermute x3, waiting for transfers between devices, to_x(): lax.ppermute(x, 'seq', [(s, s // 8 * 8 + (s % 8 + 2 * by) % 8) for s in r...  28.2 us
    all_to_all x1, blocking collectives, carried_in(): pieces = lax.all_to_all(state.reshape(count, rows, HDIM), 'seq', 0, 0)  12.8 us
    all_to_all x2, starting transfers between devices, carried_in(): return lax.all_to_all(sums, 'seq', 0, 0).reshape(HEADS, NF, HDIM)  11.8 us
    all_to_all x1, starting transfers between devices, local(): parts = lax.all_to_all(blocks, 'tp', 0, 0)  7.66 us
    unnamed x26, local copies, waits for them, and re-layouts  6.48 us
    reduce_sum x1, other arithmetic, local(): input_grad = jnp.sum(parts.astype(F32), axis=0).astype(BF16)  5.85 us
  transfers between devices with their start and end apart: 11, of which 5 were waited for; matrix products, arithmetic and copies ran while one was open for 1% of the time, Pallas kernels for 28%

profile of v3, /device:TPU:2, one launch (start us, length us, event | category | flops | bytes accessed | tf_op | source)
XLA Modules:
  0.0 247.8 jit_solution(1283090250660457817)
XLA Ops:
  0.6 5.8 %shard_map.200 = (f32[256,640]{1,0:T(8,128)}, bf16[128,4096]{1,0:T(8,128)(2,1)}) custom-call(bf16[1024,4096]{1,0:T(8,128)(2,1)} %refs_2_.1, bf16[64,4096]{1,0:T(8,128)(2,1)} %bitcast.20, bf16[64,4096]{1,0:T(8,128)(2,1)} %bitcast.21, bf16[4096,512]{1,0:T(8,128)(2,1)} %wv_ref.5), custom_call_target="tpu_custom_call" | custom-call | flops 1342177280 | bytes 8000000 | tf_op jit(solution)/shard_map/pallas_call | solution.py:101
  6.4 0.7 slice.6
  7.2 1.9 collective-permute-start
  9.1 0.0 copy-start.8
  9.1 0.0 copy-start.9
  9.1 0.0 copy-start.10
  9.1 9.4 %shard_map.201.a_ref.before_ref = f32[768,640]{1,0:T(8,128)} custom-call(bf16[1024,4096]{1,0:T(8,128)(2,1)} %refs_2_.1, bf16[128,4096]{1,0:T(8,128)(2,1)} %get-tuple-element.33.wqk_ref, bf16[4096,512]{1,0:T(8,128)(2,1)} %wv_ref.5), custom_call_target="tpu_custom_call" | custom-call | flops 4026531840 | bytes 12000000 | tf_op jit(solution)/shard_map/pallas_call | solution.py:101
  18.5 0.0 copy-done.8
  18.5 0.0 copy-done.9
  18.5 0.0 copy-done.10
  18.5 0.7 pad_maximum_fusion.taps_ref.t_ref
  19.2 0.0 collective-permute-done.tail_ref
  19.2 0.0 copy-start.12
  19.2 0.6 copy-done.12
  19.8 7.9 %shard_map.202 = (bf16[1024,256]{1,0:T(8,128)(2,1)}, bf16[1024,256]{1,0:T(8,128)(2,1)}, bf16[1024,512]{1,0:T(8,128)(2,1)}, bf16[1024,512]{1,0:T(8,128)(2,1)}, f3...) custom-call(f32[768,640]{1,0:T(8,128)} %shard_map.201.a_ref.before_ref, f32[256,640]{1,0:T(8,128)} %get-tuple-element.34.b_ref, ...), custom_call_target="tpu_custom_call" | custom-call | flops 4000000000 | bytes 15000000 | tf_op jit(solution)/shard_map/pallas_call | solution.py:101
  27.7 12.8 %all_to_all.25.x_ref = f32[16,40,128]{2,1,0:T(8,128)} all-to-all(f32[16,40,128]{2,1,0:T(8,128)} %bitcast.25), channel_id=1, replica_groups=mesh['seq'=16,'tp'=8] {'seq'}, dimensions={0} | all-to-all | bytes 655360 | tf_op jit(solution)/shard_map/all_to_all | solution.py:258
  40.6 1.7 shard_map.204
  42.3 6.0 %all-to-all-start.1 = ((f32[16,40,128]{2,1,0:T(8,128)}), f32[16,40,128]{2,1,0:T(8,128)S(1)}, u32[]{:S(2)}, u32[]{:S(2)}) async-start(f32[16,40,128]{2,1,0:T(8,128)} %shard_map.204), calls=%async_computation.1 | async-start | bytes 655360 | tf_op jit(solution)/shard_map/all_to_all | solution.py:263
  48.3 6.3 %shard_map.203.num_ref = f32[1024,512]{1,0:T(8,128)} custom-call(bf16[1024,256]{1,0:T(8,128)(2,1)} %get-tuple-element.35.ql_ref, bf16[1024,256]{1,0:T(8,128)(2,1)} %get-tuple-element.36.kr_ref, bf16[1024,512]{1,0:T(8,128)(2,1)} %get-tuple-element.37.vh_ref, bf16[1024,512]{1,0:T(8,128)(2,1)} %get-tuple-element.38.vl_ref), custom_call_target="tpu_custom_call" | custom-call | flops 6000000000 | bytes 6000000 | tf_op jit(solution)/shard_map/pallas_call | solution.py:101
  54.6 0.0 all-to-all-done.1
  54.6 0.7 copy-done.6
  55.3 14.2 %shard_map.205 = (f32[1024,512]{1,0:T(8,128)}, bf16[1024,512]{1,0:T(8,128)(2,1)}, bf16[1024,512]{1,0:T(8,128)(2,1)}, f32[4,4,160,128]{3,2,1,0:T(8,128)}, f32[4,160,128]{2,1,0:T(8,128)}) custom-call(bf16[1024,256]{1,0:T(8,128)(2,1)} %get-tuple-element.35.ql_ref, f32[1024,512]{1,0:T(8,128)} %shard_map.203.num_ref, ...), custom_call_target="tpu_custom_call" | custom-call | flops 8000000000 | bytes 12000000 | tf_op jit(solution)/shard_map/pallas_call | solution.py:101
  69.5 5.8 %all-to-all-start.2 = ((f32[16,40,128]{2,1,0:T(8,128)}), f32[16,40,128]{2,1,0:T(8,128)S(1)}, u32[]{:S(2)}, u32[]{:S(2)}) async-start(f32[16,40,128]{2,1,0:T(8,128)} %bitcast.24), calls=%async_computation.2 | async-start | bytes 655360 | tf_op jit(solution)/shard_map/all_to_all | solution.py:258
  75.4 8.0 %shard_map.208 = (f32[1024,128]{1,0:T(8,128)}, f32[1024,512]{1,0:T(8,128)}) custom-call(bf16[1024,256]{1,0:T(8,128)(2,1)} %get-tuple-element.35.ql_ref, bf16[1024,256]{1,0:T(8,128)(2,1)} %get-tuple-element.36.kr_ref, bf16[1024,512]{1,0:T(8,128)(2,1)} %get-tuple-element.37.vh_ref, bf16[1024,512]{1,0:T(8,128)(2,1)} %get-tuple-element.38.vl_ref, ...), custom_call_target="tpu_custom_call" | custom-call | flops 8000000000 | bytes 8000000 | tf_op jit(solution)/shard_map/pallas_call | solution.py:101
  83.4 0.0 all-to-all-done.2.x_ref
  83.4 0.0 copy-start.1
  83.4 0.7 copy-done.1
  84.1 1.7 shard_map.206
  85.9 5.8 %all-to-all-start.3 = ((f32[16,40,128]{2,1,0:T(8,128)}), f32[16,40,128]{2,1,0:T(8,128)S(1)}, u32[]{:S(2)}, u32[]{:S(2)}) async-start(f32[16,40,128]{2,1,0:T(8,128)} %shard_map.206), calls=%async_computation.3 | async-start | bytes 655360 | tf_op jit(solution)/shard_map/all_to_all | solution.py:263
  91.6 10.8 %shard_map.207.gq_ref = f32[1024,128]{1,0:T(8,128)} custom-call(bf16[1024,256]{1,0:T(8,128)(2,1)} %get-tuple-element.35.ql_ref, bf16[1024,256]{1,0:T(8,128)(2,1)} %get-tuple-element.36.kr_ref, bf16[1024,512]{1,0:T(8,128)(2,1)} %get-tuple-element.37.vh_ref, bf16[1024,512]{1,0:T(8,128)(2,1)} %get-tuple-element.38.vl_ref, ...), custom_call_target="tpu_custom_call" | custom-call | flops 8000000000 | bytes 8000000 | tf_op jit(solution)/shard_map/pallas_call | solution.py:101
  102.4 0.0 all-to-all-done.3
  102.4 0.0 copy-start.2
  102.4 0.7 copy-done.2
  103.1 4.5 %shard_map.209.a_ref = f32[256,640]{1,0:T(8,128)} custom-call(bf16[1024,256]{1,0:T(8,128)(2,1)} %get-tuple-element.36.kr_ref, bf16[1024,512]{1,0:T(8,128)(2,1)} %get-tuple-element.37.vh_ref, bf16[1024,512]{1,0:T(8,128)(2,1)} %get-tuple-element.38.vl_ref, f32[4,4,160,128]{3,2,1,0:T(8,128)} %get-tuple-element.42.gs_ref, f32[4,160,128]{2,1,0:T(8,128)} %bitcast.18, ...), custom_call_target="tpu_custom_call" | custom-call | flops 2000000000 | bytes 3000000 | tf_op jit(solution)/shard_map/pallas_call | solution.py:101
  107.6 0.7 slice.8
  108.3 2.0 collective-permute-start.1
  110.4 7.7 %shard_map.210.b_ref = f32[768,640]{1,0:T(8,128)} custom-call(bf16[1024,256]{1,0:T(8,128)(2,1)} %get-tuple-element.36.kr_ref, bf16[1024,512]{1,0:T(8,128)(2,1)} %get-tuple-element.37.vh_ref, bf16[1024,512]{1,0:T(8,128)(2,1)} %get-tuple-element.38.vl_ref, f32[4,4,160,128]{3,2,1,0:T(8,128)} %get-tuple-element.42.gs_ref, f32[4,160,128]{2,1,0:T(8,128)} %bitcast.19, ...), custom_call_target="tpu_custom_call" | custom-call | flops 6000000000 | bytes 9000000 | tf_op jit(solution)/shard_map/pallas_call | solution.py:101
  118.0 0.0 collective-permute-done.1.h_ref
  118.0 0.0 copy-start.11
  118.1 0.6 copy-done.11
  118.7 12.0 %shard_map.211 = (bf16[8,1024,512]{2,1,0:T(8,128)(2,1)}, bf16[640,1024]{1,0:T(8,128)(2,1)}) custom-call(f32[256,640]{1,0:T(8,128)} %shard_map.209.a_ref, f32[768,640]{1,0:T(8,128)} %shard_map.210.b_ref, f32[8,640]{1,0:T(8,128)} %copy-done.11, f32[3,640]{1,0:T(4,128)} %pad_maximum_fusion.taps_ref.t_ref, bf16[4096,512]{1,0:T(8,128)(2,1)} %wv_ref.5, ...), custom_call_target="tpu_custom_call" | custom-call | flops 5368709120 | bytes 18000000 | tf_op jit(solution)/shard_map/pallas_call | solution.py:101
  130.6 7.7 %all-to-all-start.4 = ((bf16[8,1024,512]{2,1,0:T(8,128)(2,1)}), bf16[8,1024,512]{2,1,0:T(8,128)(2,1)}, u32[]{:S(2)}, u32[]{:S(2)}) async-start(bf16[8,1024,512]{2,1,0:T(8,128)(2,1)} %get-tuple-element.48.refs_3_), calls=%async_computation.4 | async-start | bytes 16777216 | tf_op jit(solution)/shard_map/all_to_all | solution.py:647
  138.3 0.6 stack.39.refs_0_
  138.9 12.2 %shard_map.212 = (bf16[8,640,256]{2,1,0:T(8,128)(2,1)}, bf16[8,640,256]{2,1,0:T(8,128)(2,1)}) custom-call(s32[9]{0:T(128)} %stack.39.refs_0_, bf16[640,1024]{1,0:T(8,128)(2,1)} %get-tuple-element.49.refs_1_, bf16[1024,4096]{1,0:T(8,128)(2,1)} %refs_2_.1, bf16[8,1024,512]{2,1,0:T(8,128)(2,1)} %get-tuple-element.48.refs_3_), custom_call_target="tpu_custom_call" | custom-call | flops 5368709120 | bytes 15000000 | tf_op jit(solution)/shard_map/pallas_call | solution.py:101
  151.0 0.1 collective-permute-start.2
  151.1 5.0 %collective-permute-done.2.came_ref = bf16[8,640,256]{2,1,0:T(8,128)(2,1)S(1)} collective-permute-done((bf16[8,640,256]{2,1,0:T(8,128)(2,1)}, bf16[8,640,256]{2,1,0:T(8,128)(2,1)S(1)}, u32[]{:S(2)}, u32[]{:S(2)}) %collective-permute-start.2) | collective-permute-done | bytes 2621472 | tf_op jit(solution)/shard_map/ppermute | solution.py:473
  156.2 1.5 copy-done
  157.7 7.1 %shard_map.213 = (bf16[2,640,256]{2,1,0:T(8,128)(2,1)}, bf16[2,640,256]{2,1,0:T(8,128)(2,1)}, bf16[2,640,256]{2,1,0:T(8,128)(2,1)}, bf16[2,640,256]{2,1,0:T(8,128)(2,1)}) custom-call(bf16[8,640,256]{2,1,0:T(8,128)(2,1)} %get-tuple-element.50.mine_ref, bf16[8,640,256]{2,1,0:T(8,128)(2,1)} %copy-done), custom_call_target="tpu_custom_call" | custom-call | bytes 8000000 | tf_op jit(solution)/shard_map/pallas_call | solution.py:101
  164.8 1.6 collective-permute-start.3
  166.5 1.0 collective-permute-start.4
  167.4 2.6 %collective-permute-start.5 = (bf16[2,640,256]{2,1,0:T(8,128)(2,1)}, bf16[2,640,256]{2,1,0:T(8,128)(2,1)S(1)}, u32[]{:S(2)}, u32[]{:S(2)}) collective-permute-start(bf16[2,640,256]{2,1,0:T(8,128)(2,1)} %get-tuple-element.55), channel_id=1, source_target_pairs={{0,48},{8,56},{16,0},{24,8},{32,16},{40,24},{48,32},{56,40},{64,11... | collective-permute-start | bytes 1966088 | tf_op jit(solution)/shard_map/ppermute | solution.py:555
  170.0 12.6 %collective-permute-done.3.a_ref = bf16[2,640,256]{2,1,0:T(8,128)(2,1)S(1)} collective-permute-done((bf16[2,640,256]{2,1,0:T(8,128)(2,1)}, bf16[2,640,256]{2,1,0:T(8,128)(2,1)S(1)}, u32[]{:S(2)}, u32[]{:S(2)}) %collective-permute-start.3) | collective-permute-done | bytes 655392 | tf_op jit(solution)/shard_map/ppermute | solution.py:555
  182.6 3.2 %collective-permute-done.4.b_ref = bf16[2,640,256]{2,1,0:T(8,128)(2,1)S(1)} collective-permute-done((bf16[2,640,256]{2,1,0:T(8,128)(2,1)}, bf16[2,640,256]{2,1,0:T(8,128)(2,1)S(1)}, u32[]{:S(2)}, u32[]{:S(2)}) %collective-permute-start.4) | collective-permute-done | bytes 655392 | tf_op jit(solution)/shard_map/ppermute | solution.py:555
  185.8 12.4 %collective-permute-done.5.c_ref = bf16[2,640,256]{2,1,0:T(8,128)(2,1)S(1)} collective-permute-done((bf16[2,640,256]{2,1,0:T(8,128)(2,1)}, bf16[2,640,256]{2,1,0:T(8,128)(2,1)S(1)}, u32[]{:S(2)}, u32[]{:S(2)}) %collective-permute-start.5) | collective-permute-done | bytes 655392 | tf_op jit(solution)/shard_map/ppermute | solution.py:555
  198.2 0.0 copy-done.3
  198.2 0.0 copy-done.4
  198.2 0.8 copy-done.5
  199.0 4.2 %shard_map.214 = (f32[640,256]{1,0:T(8,128)}, bf16[640,256]{1,0:T(8,128)(2,1)}) custom-call(bf16[2,640,256]{2,1,0:T(8,128)(2,1)} %get-tuple-element.52.mine_ref, bf16[2,640,256]{2,1,0:T(8,128)(2,1)} %copy-done.3, bf16[2,640,256]{2,1,0:T(8,128)(2,1)} %copy-done.4, bf16[2,640,256]{2,1,0:T(8,128)(2,1)} %copy-done.5), custom_call_target="tpu_custom_call" | custom-call | bytes 4000000 | tf_op jit(solution)/shard_map/pallas_call | solution.py:101
  203.3 1.4 collective-permute-start.6
  204.6 32.8 %collective-permute-done.6.came_ref = bf16[640,256]{1,0:T(8,128)(2,1)S(1)} collective-permute-done((bf16[640,256]{1,0:T(8,128)(2,1)}, bf16[640,256]{1,0:T(8,128)(2,1)S(1)}, u32[]{:S(2)}, u32[]{:S(2)}) %collective-permute-start.6) | collective-permute-done | bytes 327712 | tf_op jit(solution)/shard_map/ppermute | solution.py:473
  237.5 0.7 copy-done.7
  238.2 3.8 %shard_map.215 = (f32[64,256]{1,0:T(8,128)}, f32[64,256]{1,0:T(8,128)}, f32[256,512]{1,0:T(8,128)}) custom-call(f32[640,256]{1,0:T(8,128)} %get-tuple-element.56.keep_ref, bf16[640,256]{1,0:T(8,128)(2,1)} %copy-done.7), custom_call_target="tpu_custom_call" | custom-call | bytes 2000000 | tf_op jit(solution)/shard_map/pallas_call | solution.py:101
  242.0 0.0 all-to-all-done.4
  242.0 5.9 %reduce_sum.12 = bf16[1024,512]{1,0:T(8,128)(2,1)} reduce(bf16[8,1024,512]{2,1,0:T(8,128)(2,1)} %all-to-all-done.4, bf16[]{:T(256)} %constant.85.clone.1), dimensions={0}, to_apply=%region_0.1 | reduce | flops 3670016 | bytes 9437186 | tf_op jit(solution)/shard_map/reduce_sum | solution.py:649
  (6 shorter events, 0.0 us)
Async XLA Ops:
  7.2 12.1 %collective-permute-start = (f32[8,640]{1,0:T(8,128)S(1)}, f32[8,640]{1,0:T(8,128)S(1)}, u32[]{:S(2)}, u32[]{:S(2)}) collective-permute-start(f32[8,640]{1,0:T(8,128)S(1)} %slice.6), channel_id=1, source_target_pairs={{0,8},{8,16},{16,24},{24,32},{32,40},{40,48},{48,56},{56,64},{64,7... | collective-permute-start | bytes 61448 | tf_op jit(solution)/shard_map/ppermute | solution.py:619
  9.1 9.5 %copy-start.8 = (f32[3,512]{1,0:T(4,128)S(1)}, f32[3,512]{1,0:T(4,128)}, u32[]{:S(2)}) copy-start(f32[3,512]{1,0:T(4,128)} %param.23) | copy-start | bytes 18436
  9.1 9.4 %copy-start.9 = (f32[3,64]{1,0:T(4,128)S(1)}, f32[3,64]{1,0:T(4,128)}, u32[]{:S(2)}) copy-start(f32[3,64]{1,0:T(4,128)} %param.22) | copy-start | bytes 2308
  9.1 9.4 %copy-start.10 = (f32[3,64]{1,0:T(4,128)S(1)}, f32[3,64]{1,0:T(4,128)}, u32[]{:S(2)}) copy-start(f32[3,64]{1,0:T(4,128)} %param.21) | copy-start | bytes 2308
  19.2 0.6 copy-start.12
  42.3 12.3 %all-to-all-start.1 = ((f32[16,40,128]{2,1,0:T(8,128)}), f32[16,40,128]{2,1,0:T(8,128)S(1)}, u32[]{:S(2)}, u32[]{:S(2)}) async-start(f32[16,40,128]{2,1,0:T(8,128)} %shard_map.204), calls=%async_computation.1 | async-start | bytes 655360 | tf_op jit(solution)/shard_map/all_to_all | solution.py:263
  54.6 0.7 copy-start.6
  69.5 13.9 %all-to-all-start.2 = ((f32[16,40,128]{2,1,0:T(8,128)}), f32[16,40,128]{2,1,0:T(8,128)S(1)}, u32[]{:S(2)}, u32[]{:S(2)}) async-start(f32[16,40,128]{2,1,0:T(8,128)} %bitcast.24), calls=%async_computation.2 | async-start | bytes 655360 | tf_op jit(solution)/shard_map/all_to_all | solution.py:258
  83.4 0.7 copy-start.1
  85.9 16.5 %all-to-all-start.3 = ((f32[16,40,128]{2,1,0:T(8,128)}), f32[16,40,128]{2,1,0:T(8,128)S(1)}, u32[]{:S(2)}, u32[]{:S(2)}) async-start(f32[16,40,128]{2,1,0:T(8,128)} %shard_map.206), calls=%async_computation.3 | async-start | bytes 655360 | tf_op jit(solution)/shard_map/all_to_all | solution.py:263
  102.4 0.7 copy-start.2
  108.3 9.7 %collective-permute-start.1 = (f32[8,640]{1,0:T(8,128)S(1)}, f32[8,640]{1,0:T(8,128)S(1)}, u32[]{:S(2)}, u32[]{:S(2)}) collective-permute-start(f32[8,640]{1,0:T(8,128)S(1)} %slice.8), channel_id=1, source_target_pairs={{8,0},{16,8},{24,16},{32,24},{40,32},{48,40},{56,48},{64,56},{72,6... | collective-permute-start | bytes 61448 | tf_op jit(solution)/shard_map/ppermute | solution.py:619
  118.0 0.6 copy-start.11
  130.6 111.4 %all-to-all-start.4 = ((bf16[8,1024,512]{2,1,0:T(8,128)(2,1)}), bf16[8,1024,512]{2,1,0:T(8,128)(2,1)}, u32[]{:S(2)}, u32[]{:S(2)}) async-start(bf16[8,1024,512]{2,1,0:T(8,128)(2,1)} %get-tuple-element.48.refs_3_), calls=%async_computation.4 | async-start | bytes 16777216 | tf_op jit(solution)/shard_map/all_to_all | solution.py:647
  151.0 5.1 %collective-permute-start.2 = (bf16[8,640,256]{2,1,0:T(8,128)(2,1)}, bf16[8,640,256]{2,1,0:T(8,128)(2,1)S(1)}, u32[]{:S(2)}, u32[]{:S(2)}) collective-permute-start(bf16[8,640,256]{2,1,0:T(8,128)(2,1)} %get-tuple-element.51), channel_id=1, source_target_pairs={{0,8},{8,0},{16,24},{24,16},{32,40},{40,32},{48,56},{56,48},{64,72... | collective-permute-start | bytes 7864328 | tf_op jit(solution)/shard_map/ppermute | solution.py:473
  156.2 1.5 copy-start
  164.8 17.8 %collective-permute-start.3 = (bf16[2,640,256]{2,1,0:T(8,128)(2,1)}, bf16[2,640,256]{2,1,0:T(8,128)(2,1)S(1)}, u32[]{:S(2)}, u32[]{:S(2)}) collective-permute-start(bf16[2,640,256]{2,1,0:T(8,128)(2,1)} %get-tuple-element.53), channel_id=1, source_target_pairs={{0,16},{8,24},{16,32},{24,40},{32,48},{40,56},{48,0},{56,8},{64,80... | collective-permute-start | bytes 1966088 | tf_op jit(solution)/shard_map/ppermute | solution.py:555
  166.5 19.3 %collective-permute-start.4 = (bf16[2,640,256]{2,1,0:T(8,128)(2,1)}, bf16[2,640,256]{2,1,0:T(8,128)(2,1)S(1)}, u32[]{:S(2)}, u32[]{:S(2)}) collective-permute-start(bf16[2,640,256]{2,1,0:T(8,128)(2,1)} %get-tuple-element.54), channel_id=1, source_target_pairs={{0,32},{8,40},{16,48},{24,56},{32,0},{40,8},{48,16},{56,24},{64,96... | collective-permute-start | bytes 1966088 | tf_op jit(solution)/shard_map/ppermute | solution.py:555
  167.4 30.7 %collective-permute-start.5 = (bf16[2,640,256]{2,1,0:T(8,128)(2,1)}, bf16[2,640,256]{2,1,0:T(8,128)(2,1)S(1)}, u32[]{:S(2)}, u32[]{:S(2)}) collective-permute-start(bf16[2,640,256]{2,1,0:T(8,128)(2,1)} %get-tuple-element.55), channel_id=1, source_target_pairs={{0,48},{8,56},{16,0},{24,8},{32,16},{40,24},{48,32},{56,40},{64,11... | collective-permute-start | bytes 1966088 | tf_op jit(solution)/shard_map/ppermute | solution.py:555
  182.6 15.6 %copy-start.3 = (bf16[2,640,256]{2,1,0:T(8,128)(2,1)}, bf16[2,640,256]{2,1,0:T(8,128)(2,1)S(1)}, u32[]{:S(2)}) copy-start(bf16[2,640,256]{2,1,0:T(8,128)(2,1)S(1)} %collective-permute-done.3.a_ref) | copy-start | bytes 1966084
  185.8 12.4 %copy-start.4 = (bf16[2,640,256]{2,1,0:T(8,128)(2,1)}, bf16[2,640,256]{2,1,0:T(8,128)(2,1)S(1)}, u32[]{:S(2)}) copy-start(bf16[2,640,256]{2,1,0:T(8,128)(2,1)S(1)} %collective-permute-done.4.b_ref) | copy-start | bytes 1966084
  198.2 0.8 copy-start.5
  203.3 34.2 %collective-permute-start.6 = (bf16[640,256]{1,0:T(8,128)(2,1)}, bf16[640,256]{1,0:T(8,128)(2,1)S(1)}, u32[]{:S(2)}, u32[]{:S(2)}) collective-permute-start(bf16[640,256]{1,0:T(8,128)(2,1)} %get-tuple-element.57), channel_id=1, source_target_pairs={{0,64},{8,72},{16,80},{24,88},{32,96},{40,104},{48,112},{56,120},{... | collective-permute-start | bytes 983048 | tf_op jit(solution)/shard_map/ppermute | solution.py:473
  237.5 0.7 copy-start.7

commit v4 on v3

--- a/solution.py
+++ b/solution.py
@@ -117,12 +117,13 @@
     return jax.ShapeDtypeStruct(shape, dtype)
 
 
-def end_kernel(x_ref, wq_ref, wk_ref, wv_ref, o_ref, wqk_ref):
+def end_kernel(x_ref, wq_ref, wk_ref, wv_ref, o_ref, tail_ref, wqk_ref):
     wqk_ref[0:64] = wq_ref[...]
     wqk_ref[64:128] = wk_ref[...]
     x = x_ref[...]
     o_ref[:, :128] = nt(x, wqk_ref[...])
     o_ref[:, 128:] = nn(x, wv_ref[...])
+    tail_ref[...] = o_ref[CHUNK - 8 :]
 
 
 def project_end(x, wq_t, wk_t, wv):
@@ -131,8 +132,8 @@
         end_kernel,
         (1,),
         [pl.BlockSpec((CHUNK, depth), lambda c: (CHUNKS - 1, 0)), full(64, depth), full(64, depth), full(depth, 512)],
-        [full(CHUNK, 640), full(128, depth)],
-        [arr((CHUNK, 640)), arr((128, depth), BF16)],
+        [full(CHUNK, 640), full(8, 640), full(128, depth)],
+        [arr((CHUNK, 640)), arr((8, 640)), arr((128, depth), BF16)],
         (x, wq_t, wk_t, wv),
         flops=2 * CHUNK * depth * 640,
         moved=8e6,
@@ -287,18 +288,44 @@
     )
 
 
-def forward_kernel(ql_ref, num_ref, sp_ref, se_ref, og_ref, gain_ref, pick_ref, pickt_ref, bias_ref, biast_ref,
+def feature_kernel(ql_ref, pick_ref, pickt_ref, bias_ref, biast_ref, ph_ref, pl_ref, th_ref, tl_ref):
+    ql = ql_ref[...]
+    for head in range(HEADS):
+        part = slice(head * WIDE, (head + 1) * WIDE)
+        a, b = factors(ql, pick_ref[head], bias_ref[...])
+        ph_ref[:, part], pl_ref[:, part] = halves(a * b)
+        ab = nt(pickt_ref[head], ql) + biast_ref[...]
+        th_ref[head], tl_ref[head] = halves(ab[:NF] * ab[WIDE : WIDE + NF])
+
+
+def query_features(ql, pick, pick_t, bias, bias_t):
+    rows = lambda c: (c, 0)
+    wide, turned = pl.BlockSpec((CHUNK, HEADS * WIDE), rows), pl.BlockSpec((HEADS, NF, CHUNK), lambda c: (0, 0, c))
+    return call(
+        feature_kernel,
+        (CHUNKS,),
+        [
+            pl.BlockSpec((CHUNK, WIDE), rows),
+            full(HEADS, WIDE, 2 * WIDE), full(HEADS, 2 * WIDE, WIDE), full(1, 2 * WIDE), full(2 * WIDE, 1),
+        ],
+        [wide, wide, turned, turned],
+        [arr((LEN, HEADS * WIDE), BF16)] * 2 + [arr((HEADS, NF, LEN), BF16)] * 2,
+        (ql, pick, pick_t, bias, bias_t),
+        flops=4e9,
+        moved=10e6,
+    )
+
+
+def forward_kernel(ph_ref, pl_ref, th_ref, tl_ref, num_ref, sp_ref, se_ref, og_ref, gain_ref,
                    out_ref, dh_ref, dl_ref, gs_ref, gt_ref):
     @pl.when(pl.program_id(0) == 0)
     def _():
         gt_ref[...] = jnp.zeros_like(gt_ref)
 
-    ql = ql_ref[...]
-    for head in range(HEADS):
-        a, b = factors(ql, pick_ref[head], bias_ref[...])
-        p_hi, p_lo = halves(a * b)
+    for head in range(HEADS):
+        part = slice(head * WIDE, (head + 1) * WIDE)
         s_hi, s_lo = halves(padded(sp_ref[0, head] + se_ref[head]))
-        num = num_ref[:, cols(head)] + nn3(p_hi, p_lo, s_hi, s_lo)
+        num = num_ref[:, cols(head)] + nn3(ph_ref[:, part], pl_ref[:, part], s_hi, s_lo)
         r = lax.rsqrt(jnp.mean(num * num, axis=-1, keepdims=True) + EPS)
         gain = gain_ref[:, cols(head)]
         unit = num * r
@@ -308,32 +335,28 @@
         d_hi, d_lo = halves(d)
         dh_ref[:, cols(head)] = d_hi
         dl_ref[:, cols(head)] = d_lo
-        ab = nt(pickt_ref[head], ql) + biast_ref[...]
-        pt_hi, pt_lo = halves(ab[:NF] * ab[WIDE : WIDE + NF])
-        own = nn3(pt_hi, pt_lo, d_hi, d_lo)
+        own = nn3(th_ref[head], tl_ref[head], d_hi, d_lo)
         gs_ref[0, head] = own
         gt_ref[head] += own
 
 
-def forward(ql, num, sp, se, og, gain, pick, pick_t, bias, bias_t):
+def forward(features, num, sp, se, og, gain):
     rows = lambda c: (c, 0)
-    narrow, wide = pl.BlockSpec((CHUNK, WIDE), rows), pl.BlockSpec((CHUNK, 512), rows)
+    packed, turned = pl.BlockSpec((CHUNK, HEADS * WIDE), rows), pl.BlockSpec((HEADS, NF, CHUNK), lambda c: (0, 0, c))
+    wide = pl.BlockSpec((CHUNK, 512), rows)
     states = pl.BlockSpec((1, HEADS, NF, HDIM), lambda c: (c, 0, 0, 0))
     return call(
         forward_kernel,
         (CHUNKS,),
-        [
-            narrow, wide, states, full(HEADS, NF, HDIM), wide, full(1, 512),
-            full(HEADS, WIDE, 2 * WIDE), full(HEADS, 2 * WIDE, WIDE), full(1, 2 * WIDE), full(2 * WIDE, 1),
-        ],
+        [packed, packed, turned, turned, wide, states, full(HEADS, NF, HDIM), wide, full(1, 512)],
         [wide, wide, wide, states, full(HEADS, NF, HDIM)],
         [
             arr((LEN, 512)), arr((LEN, 512), BF16), arr((LEN, 512), BF16),
             arr((CHUNKS, HEADS, NF, HDIM)), arr((HEADS, NF, HDIM)),
         ],
-        (ql, num, sp, se, og, gain, pick, pick_t, bias, bias_t),
-        flops=8e9,
-        moved=12e6,
+        (*features, num, sp, se, og, gain),
+        flops=5e9,
+        moved=18e6,
     )
 
 
@@ -353,7 +376,8 @@
         s_hi, s_lo = halves(padded(sp_ref[0, head] + se_ref[head]))
         dp = nt3(d_hi, d_lo, s_hi, s_lo)
         a, b = factors(ql, pick_ref[head], bias_ref[...])
-        du = du + nn(side(dp * b, dp * a).astype(BF16), back_ref[head])
+        dab_hi, dab_lo = halves(side(dp * b, dp * a))
+        du = du + nn(dab_hi, back_ref[head]) + nn(dab_lo, back_ref[head])
     gq_ref[...] = gq[:, :128] + gq[:, 128:] + du
 
 
@@ -409,7 +433,7 @@
 
 
 def later_kernel(first, last, kr_ref, vh_ref, vl_ref, gs_ref, gl_ref, gq_ref, gk_ref, gv_ref, pick_ref, bias_ref,
-                 back_ref, o_ref, total):
+                 back_ref, o_ref, head_ref, total):
     @pl.when(pl.program_id(0) == 0)
     def _():
         begin = gl_ref[...]
@@ -426,9 +450,11 @@
         v_hi, v_lo = vh_ref[:, cols(head)], vl_ref[:, cols(head)]
         o_ref[:, 128 + head * HDIM : 256 + head * HDIM] = gv_ref[:, cols(head)] + gained[:, :HDIM] + gained[:, HDIM:]
         dp = nt(side(v_hi, v_lo), side(l_hi, l_hi))
-        du = du + nn(side(dp * b, dp * a).astype(BF16), back_ref[head])
+        dab_hi, dab_lo = halves(side(dp * b, dp * a))
+        du = du + nn(dab_hi, back_ref[head]) + nn(dab_lo, back_ref[head])
     low = lax.broadcasted_iota(jnp.int32, (1, 128), 1) < 64
     o_ref[:, :128] = 0.5 * jnp.where(low, gq_ref[...], pltpu.roll(gk_ref[...] + du, 64, 1))
+    head_ref[...] = o_ref[:8]
     total[...] += gs_ref[last - 1 - pl.program_id(0)]
 
 
@@ -445,8 +471,8 @@
             narrow, wide, wide, full(CHUNKS, HEADS, NF, HDIM), full(HEADS, NF, HDIM), half, half, wide,
             full(HEADS, WIDE, 2 * WIDE), full(1, 2 * WIDE), full(HEADS, 2 * WIDE, 128),
         ],
-        pl.BlockSpec((CHUNK, 640), to),
-        arr((count * CHUNK, 640)),
+        [pl.BlockSpec((CHUNK, 640), to), full(8, 640)],
+        [arr((count * CHUNK, 640)), arr((8, 640))],
         (kr, vh, vl, gs, gl, gq, gk, gv, pick, bias, back),
         [pltpu.VMEM((HEADS, NF, HDIM), F32)],
         flops=2e9 * count,
@@ -600,7 +626,7 @@
     return keep, flip(send, "seq", 8)
 
 
-def finish_weight_grad(keep, came):
+def finish_weight_grad(keep, came, before):
     width = keep.shape[1]
     one = pl.BlockSpec((128, width), lambda i: (i, 0))
     return call(
@@ -611,6 +637,7 @@
         [arr((64, width)), arr((64, width)), arr((width, 512))],
         (keep, came),
         moved=2e6,
+        after=(before,),
     )
 
 
@@ -628,25 +655,24 @@
     wq_t, wk_t = w_query.T, w_key.T
     taps = jnp.concatenate([taps_query, taps_key, taps_value], axis=1)
 
-    end, wqk_t = project_end(inputs, wq_t, wk_t, w_value)
-    tail = along(end[-8:], 1)
+    end, tail, wqk_t = project_end(inputs, wq_t, wk_t, w_value)
+    tail = along(tail, 1)
     proj = project(inputs, wqk_t, w_value)
     ql, kr, vh, vl, before, own = shard_state(proj, end, tail, taps, pick_kt, bias_t)
     earlier = carried_in(own, False)
     num = inner(ql, kr, vh, vl)
-    outputs, dh, dl, grads, own_grad = forward(
-        ql, num, before, earlier, out_grad, out_gain.reshape(1, 512), pick_q, pick_qt, bias, bias_t
-    )
+    features = query_features(ql, pick_q, pick_qt, bias, bias_t)
+    outputs, dh, dl, grads, own_grad = forward(features, num, before, earlier, out_grad, out_gain.reshape(1, 512))
     after = carried_in(own_grad, True)
     gq, gk, gv = backward(ql, kr, vh, vl, dh, dl, before, earlier, pick_q, bias, back_q)
     rest = (kr, vh, vl, grads, after, gq, gk, gv, pick_k, bias, back_k)
-    ga = later(0, 1, *rest)
-    halo = along(ga[:8], -1)
-    gb = later(1, CHUNKS, *rest)
+    ga, halo = later(0, 1, *rest)
+    halo = along(halo, -1)
+    gb, _ = later(1, CHUNKS, *rest)
     blocks, dt = input_products(ga, gb, halo, taps, w_value, wqk_t)
     parts = lax.all_to_all(blocks, "tp", 0, 0)
-    grad_query, grad_key, grad_value = finish_weight_grad(*reduce_weight_grad(dt, inputs, blocks))
     input_grad = jnp.sum(parts.astype(F32), axis=0).astype(BF16)
+    grad_query, grad_key, grad_value = finish_weight_grad(*reduce_weight_grad(dt, inputs, blocks), input_grad)
     return (outputs, input_grad, grad_query.T, grad_key.T, grad_value)
 
 

time: 251 us -> 249 us (level)
  blocking collectives: 12.8 us -> 0 us
  Pallas kernels: 117 us -> 124 us
  starting transfers between devices: 35.8 us -> 42.3 us
    ppermute x2, waiting for transfers between devices: 37.9 us -> 4.97 us  [flip(): lax.ppermute(x, axis, [(i, i ^ bit) for i in range(lax.axis_size(axis))])]
    all_to_all x1, waiting for transfers between devices: 0.01 us -> 30.9 us  [local(): parts = lax.all_to_all(blocks, 'tp', 0, 0)]
    all_to_all x1 -> x0, blocking collectives: 12.8 us -> none  [carried_in(): pieces = lax.all_to_all(state.reshape(count, rows, HDIM), 'seq', 0, 0)]
    pallas_call x16 -> x17, Pallas kernels: 117 us -> 124 us  [call(): pl.pallas_call(body, grid_spec=pltpu.PrefetchScalarGridSpec(num_scalar_pr...]
    all_to_all x1 -> x2, starting transfers between devices: 5.8 us -> 12.5 us  [carried_in(): pieces = lax.all_to_all(state.reshape(count, rows, HDIM), 'seq', 0, 0)]
    unnamed x26 -> x28, local copies, waits for them, and re-layouts: 6.48 us -> 7.22 us
  transfers between devices with their start and end apart: 11 -> 12, of which waited for: 5 -> 5; matrix products, arithmetic and copies ran while one was open for 1% -> 3% of each run, Pallas kernels for 28% -> 30%
where the time goes in v4:
time: 249 us; the launch traced here: 246 us
  Pallas kernels  124 us (50%)
  waiting for transfers between devices  64.1 us (26%)
  starting transfers between devices  42.3 us (17%)
  local copies, waits for them, and re-layouts  7.79 us (3%)
  other arithmetic  6.52 us (3%)
    pallas_call x17, Pallas kernels, call(): pl.pallas_call(body, grid_spec=pltpu.PrefetchScalarGridSpec(num_scalar_pr...  124 us
    all_to_all x1, waiting for transfers between devices, local(): parts = lax.all_to_all(blocks, 'tp', 0, 0)  30.9 us
    ppermute x3, waiting for transfers between devices, to_x(): lax.ppermute(x, 'seq', [(s, s // 8 * 8 + (s % 8 + 2 * by) % 8) for s in r...  28.2 us
    all_to_all x2, starting transfers between devices, carried_in(): pieces = lax.all_to_all(state.reshape(count, rows, HDIM), 'seq', 0, 0)  12.5 us
    all_to_all x2, starting transfers between devices, carried_in(): return lax.all_to_all(sums, 'seq', 0, 0).reshape(HEADS, NF, HDIM)  11.4 us
    all_to_all x1, starting transfers between devices, local(): parts = lax.all_to_all(blocks, 'tp', 0, 0)  7.67 us
    unnamed x28, local copies, waits for them, and re-layouts  7.22 us
    reduce_sum x1, other arithmetic, local(): input_grad = jnp.sum(parts.astype(F32), axis=0).astype(BF16)  5.85 us
  transfers between devices with their start and end apart: 12, of which 5 were waited for; matrix products, arithmetic and copies ran while one was open for 3% of the time, Pallas kernels for 30%

profile of v4, /device:TPU:2, one launch (start us, length us, event | category | flops | bytes accessed | tf_op | source)
XLA Modules:
  0.0 245.6 jit_solution(794920196334292284)
XLA Ops:
  0.6 6.2 %shard_map.200 = (f32[256,640]{1,0:T(8,128)}, f32[8,640]{1,0:T(8,128)}, bf16[128,4096]{1,0:T(8,128)(2,1)}) custom-call(bf16[1024,4096]{1,0:T(8,128)(2,1)} %refs_2_.1, bf16[64,4096]{1,0:T(8,128)(2,1)} %bitcast.20, bf16[64,4096]{1,0:T(8,128)(2,1)} %bitcast.21, bf16[4096,512]{1,0:T(8,128)(2,1)} %wv_ref.5), custom_call_target="tpu_custom_call" | custom-call | flops 1342177280 | bytes 8000000 | tf_op jit(solution)/shard_map/pallas_call | solution.py:101
  6.8 1.9 collective-permute-start
  8.7 0.0 copy-start.9
  8.7 0.0 copy-start.10
  8.7 0.0 copy-start.11
  8.7 9.4 %shard_map.201.a_ref.before_ref = f32[768,640]{1,0:T(8,128)} custom-call(bf16[1024,4096]{1,0:T(8,128)(2,1)} %refs_2_.1, bf16[128,4096]{1,0:T(8,128)(2,1)} %get-tuple-element.41.wqk_ref, bf16[4096,512]{1,0:T(8,128)(2,1)} %wv_ref.5), custom_call_target="tpu_custom_call" | custom-call | flops 4026531840 | bytes 12000000 | tf_op jit(solution)/shard_map/pallas_call | solution.py:101
  18.2 0.0 copy-done.9
  18.2 0.0 copy-done.10
  18.2 0.0 copy-done.11
  18.2 0.7 pad_maximum_fusion.taps_ref.t_ref
  18.8 0.0 collective-permute-done.tail_ref
  18.8 0.6 copy-done.13
  19.4 7.9 %shard_map.202 = (bf16[1024,256]{1,0:T(8,128)(2,1)}, bf16[1024,256]{1,0:T(8,128)(2,1)}, bf16[1024,512]{1,0:T(8,128)(2,1)}, bf16[1024,512]{1,0:T(8,128)(2,1)}, f3...) custom-call(f32[768,640]{1,0:T(8,128)} %shard_map.201.a_ref.before_ref, f32[256,640]{1,0:T(8,128)} %get-tuple-element.42.b_ref, ...), custom_call_target="tpu_custom_call" | custom-call | flops 4000000000 | bytes 15000000 | tf_op jit(solution)/shard_map/pallas_call | solution.py:101
  27.4 6.8 %all-to-all-start = ((f32[16,40,128]{2,1,0:T(8,128)}), f32[16,40,128]{2,1,0:T(8,128)S(1)}, u32[]{:S(2)}, u32[]{:S(2)}) async-start(f32[16,40,128]{2,1,0:T(8,128)} %bitcast.25), calls=%async_computation | async-start | bytes 655360 | tf_op jit(solution)/shard_map/all_to_all | solution.py:259
  34.2 6.3 %shard_map.204.num_ref = f32[1024,512]{1,0:T(8,128)} custom-call(bf16[1024,256]{1,0:T(8,128)(2,1)} %get-tuple-element.44.ql_ref, bf16[1024,256]{1,0:T(8,128)(2,1)} %get-tuple-element.49.kr_ref, bf16[1024,512]{1,0:T(8,128)(2,1)} %get-tuple-element.50.vh_ref, bf16[1024,512]{1,0:T(8,128)(2,1)} %get-tuple-element.51.vl_ref), custom_call_target="tpu_custom_call" | custom-call | flops 6000000000 | bytes 6000000 | tf_op jit(solution)/shard_map/pallas_call | solution.py:101
  40.5 0.0 all-to-all-done.x_ref
  40.5 0.7 copy-done.3
  41.2 1.7 shard_map.205
  42.9 5.7 %all-to-all-start.1 = ((f32[16,40,128]{2,1,0:T(8,128)}), f32[16,40,128]{2,1,0:T(8,128)S(1)}, u32[]{:S(2)}, u32[]{:S(2)}) async-start(f32[16,40,128]{2,1,0:T(8,128)} %shard_map.205), calls=%async_computation.1 | async-start | bytes 655360 | tf_op jit(solution)/shard_map/all_to_all | solution.py:264
  48.6 6.7 %shard_map.203 = (bf16[1024,1024]{1,0:T(8,128)(2,1)}, bf16[1024,1024]{1,0:T(8,128)(2,1)}, bf16[4,160,1024]{2,1,0:T(8,128)(2,1)}, bf16[4,160,1024]{2,1,0:T(8,128)(2,1)}) custom-call(bf16[1024,256]{1,0:T(8,128)(2,1)} %get-tuple-element.44.ql_ref, bf16[4,256,512]{2,1,0:T(8,128)(2,1)} %constant.95.clone.pick_ref, bf16[4,512,256]{2,1,0:T(8,128)(2,1)} %constant.97.clone.pickt_ref, ...), custom_call_target="tpu_custom_call" | custom-call | flops 4000000000 | bytes 10000000 | tf_op jit(solution)/shard_map/pallas_call | solution.py:101
  55.3 0.0 all-to-all-done.1
  55.3 0.0 copy-start.8
  55.3 0.7 copy-done.8
  56.0 11.1 %shard_map.206 = (f32[1024,512]{1,0:T(8,128)}, bf16[1024,512]{1,0:T(8,128)(2,1)}, bf16[1024,512]{1,0:T(8,128)(2,1)}, f32[4,4,160,128]{3,2,1,0:T(8,128)}, f32[4,160,128]{2,1,0:T(8,128)}) custom-call(bf16[1024,1024]{1,0:T(8,128)(2,1)} %get-tuple-element.45.ph_ref, bf16[1024,1024]{1,0:T(8,128)(2,1)} %get-tuple-element.46.pl_ref, ...), custom_call_target="tpu_custom_call" | custom-call | flops 5000000000 | bytes 18000000 | tf_op jit(solution)/shard_map/pallas_call | solution.py:101
  67.2 5.7 %all-to-all-start.2 = ((f32[16,40,128]{2,1,0:T(8,128)}), f32[16,40,128]{2,1,0:T(8,128)S(1)}, u32[]{:S(2)}, u32[]{:S(2)}) async-start(f32[16,40,128]{2,1,0:T(8,128)} %bitcast.24), calls=%async_computation.2 | async-start | bytes 655360 | tf_op jit(solution)/shard_map/all_to_all | solution.py:259
  72.9 8.1 %shard_map.209 = (f32[1024,128]{1,0:T(8,128)}, f32[1024,512]{1,0:T(8,128)}) custom-call(bf16[1024,256]{1,0:T(8,128)(2,1)} %get-tuple-element.44.ql_ref, bf16[1024,256]{1,0:T(8,128)(2,1)} %get-tuple-element.49.kr_ref, bf16[1024,512]{1,0:T(8,128)(2,1)} %get-tuple-element.50.vh_ref, bf16[1024,512]{1,0:T(8,128)(2,1)} %get-tuple-element.51.vl_ref, ...), custom_call_target="tpu_custom_call" | custom-call | flops 8000000000 | bytes 8000000 | tf_op jit(solution)/shard_map/pallas_call | solution.py:101
  81.0 0.0 all-to-all-done.2.x_ref
  81.0 0.0 copy-start.2
  81.0 0.7 copy-done.2
  81.7 1.8 shard_map.207
  83.5 5.7 %all-to-all-start.3 = ((f32[16,40,128]{2,1,0:T(8,128)}), f32[16,40,128]{2,1,0:T(8,128)S(1)}, u32[]{:S(2)}, u32[]{:S(2)}) async-start(f32[16,40,128]{2,1,0:T(8,128)} %shard_map.207), calls=%async_computation.3 | async-start | bytes 655360 | tf_op jit(solution)/shard_map/all_to_all | solution.py:264
  89.2 12.6 %shard_map.208.gq_ref = f32[1024,128]{1,0:T(8,128)} custom-call(bf16[1024,256]{1,0:T(8,128)(2,1)} %get-tuple-element.44.ql_ref, bf16[1024,256]{1,0:T(8,128)(2,1)} %get-tuple-element.49.kr_ref, bf16[1024,512]{1,0:T(8,128)(2,1)} %get-tuple-element.50.vh_ref, bf16[1024,512]{1,0:T(8,128)(2,1)} %get-tuple-element.51.vl_ref, ...), custom_call_target="tpu_custom_call" | custom-call | flops 8000000000 | bytes 8000000 | tf_op jit(solution)/shard_map/pallas_call | solution.py:101
  101.8 0.0 all-to-all-done.3
  101.8 0.0 copy-start.1
  101.8 0.7 copy-done.1
  102.6 4.8 %shard_map.210 = (f32[256,640]{1,0:T(8,128)}, f32[8,640]{1,0:T(8,128)}) custom-call(bf16[1024,256]{1,0:T(8,128)(2,1)} %get-tuple-element.49.kr_ref, bf16[1024,512]{1,0:T(8,128)(2,1)} %get-tuple-element.50.vh_ref, bf16[1024,512]{1,0:T(8,128)(2,1)} %get-tuple-element.51.vl_ref, f32[4,4,160,128]{3,2,1,0:T(8,128)} %get-tuple-element.55.gs_ref, ...), custom_call_target="tpu_custom_call" | custom-call | flops 2000000000 | bytes 3000000 | tf_op jit(solution)/shard_map/pallas_call | solution.py:101
  107.4 2.0 collective-permute-start.1
  109.4 8.3 %shard_map.211 = (f32[768,640]{1,0:T(8,128)}, f32[8,640]{1,0:T(8,128)}) custom-call(bf16[1024,256]{1,0:T(8,128)(2,1)} %get-tuple-element.49.kr_ref, bf16[1024,512]{1,0:T(8,128)(2,1)} %get-tuple-element.50.vh_ref, bf16[1024,512]{1,0:T(8,128)(2,1)} %get-tuple-element.51.vl_ref, f32[4,4,160,128]{3,2,1,0:T(8,128)} %get-tuple-element.55.gs_ref, ...), custom_call_target="tpu_custom_call" | custom-call | flops 6000000000 | bytes 9000000 | tf_op jit(solution)/shard_map/pallas_call | solution.py:101
  117.7 0.0 collective-permute-done.1.h_ref
  117.7 0.0 copy-start.12
  117.7 0.6 copy-done.12
  118.3 12.0 %shard_map.212 = (bf16[8,1024,512]{2,1,0:T(8,128)(2,1)}, bf16[640,1024]{1,0:T(8,128)(2,1)}) custom-call(f32[256,640]{1,0:T(8,128)} %get-tuple-element.61.a_ref, f32[768,640]{1,0:T(8,128)} %get-tuple-element.62.b_ref, f32[8,640]{1,0:T(8,128)} %copy-done.12, f32[3,640]{1,0:T(4,128)} %pad_maximum_fusion.taps_ref.t_ref, bf16[4096,512]{1,0:T(8,128)(2,1)} %wv_ref.5, ...), custom_call_target="tpu_custom_call" | custom-call | flops 5368709120 | bytes 18000000 | tf_op jit(solution)/shard_map/pallas_call | solution.py:101
  130.2 7.7 %all-to-all-start.4 = ((bf16[8,1024,512]{2,1,0:T(8,128)(2,1)}), bf16[8,1024,512]{2,1,0:T(8,128)(2,1)}, u32[]{:S(2)}, u32[]{:S(2)}) async-start(bf16[8,1024,512]{2,1,0:T(8,128)(2,1)} %get-tuple-element.64.refs_3_), calls=%async_computation.4 | async-start | bytes 16777216 | tf_op jit(solution)/shard_map/all_to_all | solution.py:673
  137.9 0.6 stack.39.refs_0_
  138.5 12.2 %shard_map.213 = (bf16[8,640,256]{2,1,0:T(8,128)(2,1)}, bf16[8,640,256]{2,1,0:T(8,128)(2,1)}) custom-call(s32[9]{0:T(128)} %stack.39.refs_0_, bf16[640,1024]{1,0:T(8,128)(2,1)} %get-tuple-element.65.refs_1_, bf16[1024,4096]{1,0:T(8,128)(2,1)} %refs_2_.1, bf16[8,1024,512]{2,1,0:T(8,128)(2,1)} %get-tuple-element.64.refs_3_), custom_call_target="tpu_custom_call" | custom-call | flops 5368709120 | bytes 15000000 | tf_op jit(solution)/shard_map/pallas_call | solution.py:101
  150.6 0.2 collective-permute-start.2
  150.8 5.0 %collective-permute-done.2.came_ref = bf16[8,640,256]{2,1,0:T(8,128)(2,1)S(1)} collective-permute-done((bf16[8,640,256]{2,1,0:T(8,128)(2,1)}, bf16[8,640,256]{2,1,0:T(8,128)(2,1)S(1)}, u32[]{:S(2)}, u32[]{:S(2)}) %collective-permute-start.2) | collective-permute-done | bytes 2621472 | tf_op jit(solution)/shard_map/ppermute | solution.py:499
  155.8 1.5 copy-done
  157.3 7.1 %shard_map.214 = (bf16[2,640,256]{2,1,0:T(8,128)(2,1)}, bf16[2,640,256]{2,1,0:T(8,128)(2,1)}, bf16[2,640,256]{2,1,0:T(8,128)(2,1)}, bf16[2,640,256]{2,1,0:T(8,128)(2,1)}) custom-call(bf16[8,640,256]{2,1,0:T(8,128)(2,1)} %get-tuple-element.66.mine_ref, bf16[8,640,256]{2,1,0:T(8,128)(2,1)} %copy-done), custom_call_target="tpu_custom_call" | custom-call | bytes 8000000 | tf_op jit(solution)/shard_map/pallas_call | solution.py:101
  164.4 1.7 collective-permute-start.3
  166.1 1.0 collective-permute-start.4
  167.0 2.6 %collective-permute-start.5 = (bf16[2,640,256]{2,1,0:T(8,128)(2,1)}, bf16[2,640,256]{2,1,0:T(8,128)(2,1)S(1)}, u32[]{:S(2)}, u32[]{:S(2)}) collective-permute-start(bf16[2,640,256]{2,1,0:T(8,128)(2,1)} %get-tuple-element.71), channel_id=1, source_target_pairs={{0,48},{8,56},{16,0},{24,8},{32,16},{40,24},{48,32},{56,40},{64,11... | collective-permute-start | bytes 1966088 | tf_op jit(solution)/shard_map/ppermute | solution.py:581
  169.6 12.6 %collective-permute-done.3.a_ref = bf16[2,640,256]{2,1,0:T(8,128)(2,1)S(1)} collective-permute-done((bf16[2,640,256]{2,1,0:T(8,128)(2,1)}, bf16[2,640,256]{2,1,0:T(8,128)(2,1)S(1)}, u32[]{:S(2)}, u32[]{:S(2)}) %collective-permute-start.3) | collective-permute-done | bytes 655392 | tf_op jit(solution)/shard_map/ppermute | solution.py:581
  182.2 3.2 %collective-permute-done.4.b_ref = bf16[2,640,256]{2,1,0:T(8,128)(2,1)S(1)} collective-permute-done((bf16[2,640,256]{2,1,0:T(8,128)(2,1)}, bf16[2,640,256]{2,1,0:T(8,128)(2,1)S(1)}, u32[]{:S(2)}, u32[]{:S(2)}) %collective-permute-start.4) | collective-permute-done | bytes 655392 | tf_op jit(solution)/shard_map/ppermute | solution.py:581
  185.4 12.4 %collective-permute-done.5.c_ref = bf16[2,640,256]{2,1,0:T(8,128)(2,1)S(1)} collective-permute-done((bf16[2,640,256]{2,1,0:T(8,128)(2,1)}, bf16[2,640,256]{2,1,0:T(8,128)(2,1)S(1)}, u32[]{:S(2)}, u32[]{:S(2)}) %collective-permute-start.5) | collective-permute-done | bytes 655392 | tf_op jit(solution)/shard_map/ppermute | solution.py:581
  197.8 0.0 copy-done.4
  197.8 0.8 copy-done.6
  198.6 4.2 %shard_map.215 = (f32[640,256]{1,0:T(8,128)}, bf16[640,256]{1,0:T(8,128)(2,1)}) custom-call(bf16[2,640,256]{2,1,0:T(8,128)(2,1)} %get-tuple-element.68.mine_ref, bf16[2,640,256]{2,1,0:T(8,128)(2,1)} %copy-done.4, bf16[2,640,256]{2,1,0:T(8,128)(2,1)} %copy-done.5, bf16[2,640,256]{2,1,0:T(8,128)(2,1)} %copy-done.6), custom_call_target="tpu_custom_call" | custom-call | bytes 4000000 | tf_op jit(solution)/shard_map/pallas_call | solution.py:101
  202.9 1.4 collective-permute-start.6
  204.3 30.9 %all-to-all-done.4 = bf16[8,1024,512]{2,1,0:T(8,128)(2,1)} async-done(((bf16[8,1024,512]{2,1,0:T(8,128)(2,1)}), bf16[8,1024,512]{2,1,0:T(8,128)(2,1)}, u32[]{:S(2)}, u32[]{:S(2)}) %all-to-all-start.4) | async-done | bytes 8388640 | tf_op jit(solution)/shard_map/all_to_all | solution.py:673
  235.2 5.9 %reduce_sum.12.refs_2_ = bf16[1024,512]{1,0:T(8,128)(2,1)} reduce(bf16[8,1024,512]{2,1,0:T(8,128)(2,1)} %all-to-all-done.4, bf16[]{:T(256)} %constant.85.clone.1), dimensions={0}, to_apply=%region_0.0 | reduce | flops 3670016 | bytes 9437186 | tf_op jit(solution)/shard_map/reduce_sum | solution.py:674
  241.1 0.0 collective-permute-done.6.refs_1_
  241.1 0.7 copy-done.7
  241.8 3.8 %shard_map.216 = (f32[64,256]{1,0:T(8,128)}, f32[64,256]{1,0:T(8,128)}, f32[256,512]{1,0:T(8,128)}) custom-call(f32[640,256]{1,0:T(8,128)} %get-tuple-element.72.refs_0_, bf16[640,256]{1,0:T(8,128)(2,1)} %copy-done.7, bf16[1024,512]{1,0:T(8,128)(2,1)} %reduce_sum.12.refs_2_), custom_call_target="tpu_custom_call" | custom-call | bytes 2000000 | tf_op jit(solution)/shard_map/pallas_call | solution.py:101
  (8 shorter events, 0.0 us)
Async XLA Ops:
  6.8 12.1 %collective-permute-start = (f32[8,640]{1,0:T(8,128)}, f32[8,640]{1,0:T(8,128)S(1)}, u32[]{:S(2)}, u32[]{:S(2)}) collective-permute-start(f32[8,640]{1,0:T(8,128)} %get-tuple-element.43), channel_id=1, source_target_pairs={{0,8},{8,16},{16,24},{24,32},{32,40},{40,48},{48,56},{56,64},{64,7... | collective-permute-start | bytes 61448 | tf_op jit(solution)/shard_map/ppermute | solution.py:646
  8.7 9.5 %copy-start.9 = (f32[3,512]{1,0:T(4,128)S(1)}, f32[3,512]{1,0:T(4,128)}, u32[]{:S(2)}) copy-start(f32[3,512]{1,0:T(4,128)} %param.23) | copy-start | bytes 18436
  8.7 9.4 %copy-start.10 = (f32[3,64]{1,0:T(4,128)S(1)}, f32[3,64]{1,0:T(4,128)}, u32[]{:S(2)}) copy-start(f32[3,64]{1,0:T(4,128)} %param.22) | copy-start | bytes 2308
  8.7 9.4 %copy-start.11 = (f32[3,64]{1,0:T(4,128)S(1)}, f32[3,64]{1,0:T(4,128)}, u32[]{:S(2)}) copy-start(f32[3,64]{1,0:T(4,128)} %param.21) | copy-start | bytes 2308
  18.8 0.6 copy-start.13
  27.4 13.1 %all-to-all-start = ((f32[16,40,128]{2,1,0:T(8,128)}), f32[16,40,128]{2,1,0:T(8,128)S(1)}, u32[]{:S(2)}, u32[]{:S(2)}) async-start(f32[16,40,128]{2,1,0:T(8,128)} %bitcast.25), calls=%async_computation | async-start | bytes 655360 | tf_op jit(solution)/shard_map/all_to_all | solution.py:259
  40.5 0.7 copy-start.3
  42.9 12.4 %all-to-all-start.1 = ((f32[16,40,128]{2,1,0:T(8,128)}), f32[16,40,128]{2,1,0:T(8,128)S(1)}, u32[]{:S(2)}, u32[]{:S(2)}) async-start(f32[16,40,128]{2,1,0:T(8,128)} %shard_map.205), calls=%async_computation.1 | async-start | bytes 655360 | tf_op jit(solution)/shard_map/all_to_all | solution.py:264
  55.3 0.7 copy-start.8
  67.2 13.8 %all-to-all-start.2 = ((f32[16,40,128]{2,1,0:T(8,128)}), f32[16,40,128]{2,1,0:T(8,128)S(1)}, u32[]{:S(2)}, u32[]{:S(2)}) async-start(f32[16,40,128]{2,1,0:T(8,128)} %bitcast.24), calls=%async_computation.2 | async-start | bytes 655360 | tf_op jit(solution)/shard_map/all_to_all | solution.py:259
  81.0 0.7 copy-start.2
  83.5 18.3 %all-to-all-start.3 = ((f32[16,40,128]{2,1,0:T(8,128)}), f32[16,40,128]{2,1,0:T(8,128)S(1)}, u32[]{:S(2)}, u32[]{:S(2)}) async-start(f32[16,40,128]{2,1,0:T(8,128)} %shard_map.207), calls=%async_computation.3 | async-start | bytes 655360 | tf_op jit(solution)/shard_map/all_to_all | solution.py:264
  101.8 0.7 copy-start.1
  107.4 10.3 %collective-permute-start.1 = (f32[8,640]{1,0:T(8,128)}, f32[8,640]{1,0:T(8,128)S(1)}, u32[]{:S(2)}, u32[]{:S(2)}) collective-permute-start(f32[8,640]{1,0:T(8,128)} %get-tuple-element.63), channel_id=1, source_target_pairs={{8,0},{16,8},{24,16},{32,24},{40,32},{48,40},{56,48},{64,56},{72,6... | collective-permute-start | bytes 61448 | tf_op jit(solution)/shard_map/ppermute | solution.py:646
  117.7 0.6 copy-start.12
  130.2 105.0 %all-to-all-start.4 = ((bf16[8,1024,512]{2,1,0:T(8,128)(2,1)}), bf16[8,1024,512]{2,1,0:T(8,128)(2,1)}, u32[]{:S(2)}, u32[]{:S(2)}) async-start(bf16[8,1024,512]{2,1,0:T(8,128)(2,1)} %get-tuple-element.64.refs_3_), calls=%async_computation.4 | async-start | bytes 16777216 | tf_op jit(solution)/shard_map/all_to_all | solution.py:673
  150.6 5.1 %collective-permute-start.2 = (bf16[8,640,256]{2,1,0:T(8,128)(2,1)}, bf16[8,640,256]{2,1,0:T(8,128)(2,1)S(1)}, u32[]{:S(2)}, u32[]{:S(2)}) collective-permute-start(bf16[8,640,256]{2,1,0:T(8,128)(2,1)} %get-tuple-element.67), channel_id=1, source_target_pairs={{0,8},{8,0},{16,24},{24,16},{32,40},{40,32},{48,56},{56,48},{64,72... | collective-permute-start | bytes 7864328 | tf_op jit(solution)/shard_map/ppermute | solution.py:499
  155.7 1.5 copy-start
  164.4 17.8 %collective-permute-start.3 = (bf16[2,640,256]{2,1,0:T(8,128)(2,1)}, bf16[2,640,256]{2,1,0:T(8,128)(2,1)S(1)}, u32[]{:S(2)}, u32[]{:S(2)}) collective-permute-start(bf16[2,640,256]{2,1,0:T(8,128)(2,1)} %get-tuple-element.69), channel_id=1, source_target_pairs={{0,16},{8,24},{16,32},{24,40},{32,48},{40,56},{48,0},{56,8},{64,80... | collective-permute-start | bytes 1966088 | tf_op jit(solution)/shard_map/ppermute | solution.py:581
  166.1 19.3 %collective-permute-start.4 = (bf16[2,640,256]{2,1,0:T(8,128)(2,1)}, bf16[2,640,256]{2,1,0:T(8,128)(2,1)S(1)}, u32[]{:S(2)}, u32[]{:S(2)}) collective-permute-start(bf16[2,640,256]{2,1,0:T(8,128)(2,1)} %get-tuple-element.70), channel_id=1, source_target_pairs={{0,32},{8,40},{16,48},{24,56},{32,0},{40,8},{48,16},{56,24},{64,96... | collective-permute-start | bytes 1966088 | tf_op jit(solution)/shard_map/ppermute | solution.py:581
  167.0 30.7 %collective-permute-start.5 = (bf16[2,640,256]{2,1,0:T(8,128)(2,1)}, bf16[2,640,256]{2,1,0:T(8,128)(2,1)S(1)}, u32[]{:S(2)}, u32[]{:S(2)}) collective-permute-start(bf16[2,640,256]{2,1,0:T(8,128)(2,1)} %get-tuple-element.71), channel_id=1, source_target_pairs={{0,48},{8,56},{16,0},{24,8},{32,16},{40,24},{48,32},{56,40},{64,11... | collective-permute-start | bytes 1966088 | tf_op jit(solution)/shard_map/ppermute | solution.py:581
  182.2 15.6 %copy-start.4 = (bf16[2,640,256]{2,1,0:T(8,128)(2,1)}, bf16[2,640,256]{2,1,0:T(8,128)(2,1)S(1)}, u32[]{:S(2)}) copy-start(bf16[2,640,256]{2,1,0:T(8,128)(2,1)S(1)} %collective-permute-done.3.a_ref) | copy-start | bytes 1966084
  185.4 12.4 %copy-start.5 = (bf16[2,640,256]{2,1,0:T(8,128)(2,1)}, bf16[2,640,256]{2,1,0:T(8,128)(2,1)S(1)}, u32[]{:S(2)}) copy-start(bf16[2,640,256]{2,1,0:T(8,128)(2,1)S(1)} %collective-permute-done.4.b_ref) | copy-start | bytes 1966084
  197.8 0.8 copy-start.6
  202.9 38.2 %collective-permute-start.6 = (bf16[640,256]{1,0:T(8,128)(2,1)}, bf16[640,256]{1,0:T(8,128)(2,1)S(1)}, u32[]{:S(2)}, u32[]{:S(2)}) collective-permute-start(bf16[640,256]{1,0:T(8,128)(2,1)} %get-tuple-element.73), channel_id=1, source_target_pairs={{0,64},{8,72},{16,80},{24,88},{32,96},{40,104},{48,112},{56,120},{... | collective-permute-start | bytes 983048 | tf_op jit(solution)/shard_map/ppermute | solution.py:499
  241.1 0.7 copy-start.7

commit v5 on v4

--- a/solution.py
+++ b/solution.py
@@ -499,7 +499,7 @@
     return lax.ppermute(x, axis, [(i, i ^ bit) for i in range(lax.axis_size(axis))])
 
 
-def input_kernel(a_ref, b_ref, h_ref, t_ref, wv_ref, wqk_ref, o_ref, dt_ref, d_ref):
+def input_kernel(me_ref, a_ref, b_ref, h_ref, t_ref, wv_ref, wqk_ref, z_ref, keep_ref, send_ref, dt_ref, d_ref):
     @pl.when(pl.program_id(0) == 0)
     def _():
         n = a_ref.shape[0]
@@ -515,47 +515,118 @@
             dt_ref[:, start:end] = got.T
 
     d = d_ref[...]
-    for i in range(o_ref.shape[0]):
+    half = LEN // 2
+    bottom = []
+    for i in range(2):
         part = slice(512 * i, 512 * (i + 1))
-        o_ref[i] = (nt(d[:, 128:], wv_ref[part]) + nn(d[:, :128], wqk_ref[:, part])).astype(BF16)
-
-
-def input_products(a, b, halo, taps, wv, wqk):
-    parts, wide = wv.shape[0] // 512, 2
-    n, m = a.shape[0], b.shape[0]
+        got = nt(d[:, 128:], wv_ref[part]) + nn(d[:, :128], wqk_ref[:, part])
+        z_ref[0, i] = got[:half].astype(BF16)
+        bottom.append(got[half:])
+    first = me_ref[0] == 0
+    keep_ref[0] = jnp.where(first, bottom[0], bottom[1])
+    send_ref[0] = jnp.where(first, bottom[1], bottom[0]).astype(BF16)
+
+
+def input_products(side_y, a, b, halo, taps, wv, wqk):
+    n, m, half = a.shape[0], b.shape[0], LEN // 2
+    const = lambda *shape: pl.BlockSpec(shape, lambda i, me: (0,) * len(shape))
+    block = pl.BlockSpec((1, half, 512), lambda i, me: (i, 0, 0))
     return call(
         input_kernel,
-        (parts // wide,),
+        (4,),
         [
-            full(n, 640), full(m, 640), full(8, 640), full(3, 640),
-            pl.BlockSpec((512 * wide, 512), lambda i: (i, 0)), pl.BlockSpec((128, 512 * wide), lambda i: (0, i)),
+            const(n, 640), const(m, 640), const(8, 640), const(3, 640),
+            pl.BlockSpec((1024, 512), lambda i, me: (i, 0)), pl.BlockSpec((128, 1024), lambda i, me: (0, i)),
         ],
-        [pl.BlockSpec((wide, LEN, 512), lambda i: (i, 0, 0)), full(640, LEN)],
-        [arr((parts, LEN, 512), BF16), arr((640, LEN), BF16)],
-        (a, b, halo, taps, wv, wqk),
+        [pl.BlockSpec((1, 2, half, 512), lambda i, me: (i, 0, 0, 0)), block, block, const(640, LEN)],
+        [arr((4, 2, half, 512), BF16), arr((4, half, 512)), arr((4, half, 512), BF16), arr((640, LEN), BF16)],
+        (side_y, a, b, halo, taps, wv, wqk),
         [pltpu.VMEM((LEN, 640), BF16)],
+        prefetch=1,
         flops=2 * LEN * 640 * 4096,
-        moved=18e6,
-    )
-
-
-def weight_kernel(dest_ref, d_ref, x_ref, theirs_ref, ours_ref):
-    got = nn(d_ref[...], x_ref[...]).astype(BF16)
-    half = got.shape[1] // 2
-    low, high = got[:, :half], got[:, half:]
+        moved=20e6,
+    )
+
+
+def pair_kernel(keep_ref, came_ref, o_ref):
+    o_ref[...] = (keep_ref[...] + f32(came_ref[...])).astype(BF16)
+
+
+def top_kernel(me_ref, p_ref, keep_ref, send_ref):
+    total = f32(p_ref[0])
+    for i in range(1, 4):
+        total = total + f32(p_ref[i])
+    first = me_ref[0] == 0
+    keep_ref[...] = jnp.where(first, total[0], total[1])
+    send_ref[...] = jnp.where(first, total[1], total[0]).astype(BF16)
+
+
+def last_kernel(keep_ref, came_ref, p_ref, o_ref):
+    @pl.when(pl.program_id(0) < 2)
+    def _():
+        o_ref[...] = (keep_ref[...] + f32(came_ref[...])).astype(BF16)
+
+    @pl.when(pl.program_id(0) >= 2)
+    def _():
+        total = f32(p_ref[0])
+        for i in range(1, 4):
+            total = total + f32(p_ref[i])
+        o_ref[...] = total.astype(BF16)
+
+
+def along_z(x):
+    return lax.all_to_all(x, "tp", 0, 0, axis_index_groups=[[0, 2, 4, 6], [1, 3, 5, 7]])
+
+
+def reduce_input_grad(side_y, by_z, keep, send, before):
+    half, tile = LEN // 2, LEN // 4
+    came = flip(send, "tp", 1)
+    tops = along_z(by_z)
+    block = pl.BlockSpec((1, half, 512), lambda i: (i, 0, 0))
+    pairs = call(pair_kernel, (4,), [block, block], block, arr((4, half, 512), BF16), (keep, came), moved=8e6, after=(before,))
+    rows = pl.BlockSpec((tile // 2, 512), lambda i, me: (i, 0))
+    keep, send = call(
+        top_kernel,
+        (4,),
+        [pl.BlockSpec((4, 2, tile // 2, 512), lambda i, me: (0, 0, i, 0))],
+        [rows, rows],
+        [arr((half, 512)), arr((half, 512), BF16)],
+        (side_y, tops),
+        prefetch=1,
+        moved=6e6,
+    )
+    pairs = along_z(pairs)
+    came = flip(send, "tp", 1)
+    top = pl.BlockSpec((tile, 512), lambda i: (jnp.minimum(i, 1), 0))
+    return call(
+        last_kernel,
+        (4,),
+        [top, top, pl.BlockSpec((4, tile, 512), lambda i: (0, jnp.maximum(i - 2, 0), 0))],
+        pl.BlockSpec((tile, 512), lambda i: (i, 0)),
+        arr((LEN, 512), BF16),
+        (keep, came, pairs),
+        moved=5e6,
+    )
+
+
+def weight_kernel(dest_ref, d_ref, x_ref, y_ref, theirs_ref, ours_ref):
     first = dest_ref[8] == 0
-    theirs_ref[0] = jnp.where(first, high, low)
-    ours_ref[0] = jnp.where(first, low, high)
+    for r, ref in enumerate((x_ref, y_ref)):
+        got = nn(d_ref[...], ref[...]).astype(BF16)
+        half = got.shape[1] // 2
+        low, high = got[:, :half], got[:, half:]
+        theirs_ref[r] = jnp.where(first, high, low)
+        ours_ref[r] = jnp.where(first, low, high)
 
 
 def split_kernel(mine_ref, came_ref, *outs):
     step = pl.program_id(0)
-    got = f32(mine_ref[0]) + f32(came_ref[0])
+    got = (f32(mine_ref[...]) + f32(came_ref[...])).astype(BF16)
     for j in range(4):
 
-        @pl.when(step // 2 == j)
+        @pl.when(step == j)
         def _(j=j):
-            outs[j][0] = got.astype(BF16)
+            outs[j][...] = got
 
 
 def row_sum_kernel(mine_ref, a_ref, b_ref, c_ref, keep_ref, send_ref):
@@ -581,7 +652,7 @@
     return lax.ppermute(x, "seq", [(s, s // 8 * 8 + (s % 8 + 2 * by) % 8) for s in range(16)])
 
 
-def reduce_weight_grad(dt, x, before):
+def weight_parts(dt, x):
     me = lax.axis_index("seq")
     y, px, core = me // 8, me // 2 % 4, me % 2
     width = x.shape[1] // 16
@@ -589,29 +660,32 @@
     dest = jnp.stack([*chips, core]).astype(jnp.int32)
     theirs, ours = call(
         weight_kernel,
-        (8,),
-        [pl.BlockSpec((640, LEN), lambda i, dest: (0, 0)), pl.BlockSpec((LEN, 2 * width), lambda i, dest: (0, dest[i]))],
-        [pl.BlockSpec((1, 640, width), lambda i, dest: (i, 0, 0))] * 2,
+        (4,),
+        [pl.BlockSpec((640, LEN), lambda i, dest: (0, 0))]
+        + [pl.BlockSpec((LEN, 2 * width), lambda i, dest, r=r: (0, dest[2 * i + r])) for r in range(2)],
+        [pl.BlockSpec((2, 640, width), lambda i, dest: (i, 0, 0))] * 2,
         [arr((8, 640, width), BF16)] * 2,
-        (dest, dt, x),
+        (dest, dt, x, x),
         prefetch=1,
-        after=(before,),
         flops=2 * LEN * 640 * 4096,
         moved=15e6,
     )
     came = flip(theirs, "seq", 1)
-    block = pl.BlockSpec((1, 640, width), lambda i: (i, 0, 0))
-    parts = call(
+    block = pl.BlockSpec((2, 640, width), lambda i: (i, 0, 0))
+    return call(
         split_kernel,
-        (8,),
+        (4,),
         [block, block],
-        [pl.BlockSpec((1, 640, width), lambda i, j=j: (jnp.clip(i - 2 * j, 0, 1), 0, 0)) for j in range(4)],
+        [full(2, 640, width)] * 4,
         [arr((2, 640, width), BF16)] * 4,
         (ours, came),
         moved=8e6,
     )
+
+
+def reduce_weight_grad(parts):
     mine, *rest = parts
-    rest = [to_x(part, dx) for dx, part in enumerate(rest, 1)]
+    width = mine.shape[2]
     pair = pl.BlockSpec((2, 128, width), lambda i: (0, i, 0))
     one = pl.BlockSpec((128, width), lambda i: (i, 0))
     keep, send = call(
@@ -626,7 +700,7 @@
     return keep, flip(send, "seq", 8)
 
 
-def finish_weight_grad(keep, came, before):
+def finish_weight_grad(keep, came):
     width = keep.shape[1]
     one = pl.BlockSpec((128, width), lambda i: (i, 0))
     return call(
@@ -637,7 +711,6 @@
         [arr((64, width)), arr((64, width)), arr((width, 512))],
         (keep, came),
         moved=2e6,
-        after=(before,),
     )
 
 
@@ -669,10 +742,13 @@
     ga, halo = later(0, 1, *rest)
     halo = along(halo, -1)
     gb, _ = later(1, CHUNKS, *rest)
-    blocks, dt = input_products(ga, gb, halo, taps, w_value, wqk_t)
-    parts = lax.all_to_all(blocks, "tp", 0, 0)
-    input_grad = jnp.sum(parts.astype(F32), axis=0).astype(BF16)
-    grad_query, grad_key, grad_value = finish_weight_grad(*reduce_weight_grad(dt, inputs, blocks), input_grad)
+    side_y = (lax.axis_index("tp") % 2).astype(jnp.int32).reshape(1)
+    by_z, keep, send, dt = input_products(side_y, ga, gb, halo, taps, w_value, wqk_t)
+    mine, *rest = weight_parts(dt, inputs)
+    parts = [mine, *(to_x(part, dx) for dx, part in enumerate(rest, 1))]
+    own, came = reduce_weight_grad(parts)
+    input_grad = reduce_input_grad(side_y, by_z, keep, send, own)
+    grad_query, grad_key, grad_value = finish_weight_grad(own, came)
     return (outputs, input_grad, grad_query.T, grad_key.T, grad_value)
 
 

time: 249 us -> 248 us (level)
  waiting for transfers between devices: 64.1 us -> 47.8 us
  Pallas kernels: 124 us -> 134 us
  starting transfers between devices: 42.3 us -> 50.5 us
  other arithmetic: 6.52 us -> 0.67 us
  local copies, waits for them, and re-layouts: 7.79 us -> 10.6 us
    all_to_all x1 -> x2, waiting for transfers between devices: 30.9 us -> 0.01 us  [along_z(): lax.all_to_all(x, 'tp', 0, 0, axis_index_groups=[[0, 2, 4, 6], [1, 3, 5,...]
    ppermute x2 -> x4, waiting for transfers between devices: 4.97 us -> 19.9 us  [flip(): lax.ppermute(x, axis, [(i, i ^ bit) for i in range(lax.axis_size(axis))])]
    pallas_call x17 -> x20, Pallas kernels: 124 us -> 134 us  [call(): pl.pallas_call(body, grid_spec=pltpu.PrefetchScalarGridSpec(num_scalar_pr...]
    reduce_sum x1 -> x0, other arithmetic: 5.85 us -> none  [local(): input_grad = jnp.sum(parts.astype(F32), axis=0).astype(BF16)]
    ppermute x2 -> x4, starting transfers between devices: 1.58 us -> 7.23 us  [flip(): lax.ppermute(x, axis, [(i, i ^ bit) for i in range(lax.axis_size(axis))])]
    all_to_all x1 -> x2, starting transfers between devices: 7.67 us -> 10.6 us  [along_z(): lax.all_to_all(x, 'tp', 0, 0, axis_index_groups=[[0, 2, 4, 6], [1, 3, 5,...]
    unnamed x28 -> x36, local copies, waits for them, and re-layouts: 7.22 us -> 9.96 us
  transfers between devices with their start and end apart: 12 -> 15, of which waited for: 5 -> 5; matrix products, arithmetic and copies ran while one was open for 3% -> 1% of each run, Pallas kernels for 30% -> 30%
where the time goes in v5:
time: 248 us; the launch traced here: 244 us
  Pallas kernels  134 us (54%)
  starting transfers between devices  50.5 us (20%)
  waiting for transfers between devices  47.8 us (19%)
  local copies, waits for them, and re-layouts  10.6 us (4%)
    pallas_call x20, Pallas kernels, call(): pl.pallas_call(body, grid_spec=pltpu.PrefetchScalarGridSpec(num_scalar_pr...  134 us
    ppermute x3, waiting for transfers between devices, to_x(): lax.ppermute(x, 'seq', [(s, s // 8 * 8 + (s % 8 + 2 * by) % 8) for s in r...  27.9 us
    ppermute x4, waiting for transfers between devices, flip(): lax.ppermute(x, axis, [(i, i ^ bit) for i in range(lax.axis_size(axis))])  19.9 us
    all_to_all x2, starting transfers between devices, carried_in(): pieces = lax.all_to_all(state.reshape(count, rows, HDIM), 'seq', 0, 0)  12.5 us
    all_to_all x2, starting transfers between devices, carried_in(): return lax.all_to_all(sums, 'seq', 0, 0).reshape(HEADS, NF, HDIM)  11.4 us
    all_to_all x2, starting transfers between devices, along_z(): lax.all_to_all(x, 'tp', 0, 0, axis_index_groups=[[0, 2, 4, 6], [1, 3, 5,...  10.6 us
    unnamed x36, local copies, waits for them, and re-layouts  9.96 us
    ppermute x4, starting transfers between devices, flip(): lax.ppermute(x, axis, [(i, i ^ bit) for i in range(lax.axis_size(axis))])  7.23 us
  transfers between devices with their start and end apart: 15, of which 5 were waited for; matrix products, arithmetic and copies ran while one was open for 1% of the time, Pallas kernels for 30%

profile of v5, /device:TPU:2, one launch (start us, length us, event | category | flops | bytes accessed | tf_op | source)
XLA Modules:
  0.0 244.2 jit_solution(18323408686042185495)
XLA Ops:
  0.6 6.2 %shard_map.200 = (f32[256,640]{1,0:T(8,128)}, f32[8,640]{1,0:T(8,128)}, bf16[128,4096]{1,0:T(8,128)(2,1)}) custom-call(bf16[1024,4096]{1,0:T(8,128)(2,1)} %y_ref.1, bf16[64,4096]{1,0:T(8,128)(2,1)} %bitcast.21, bf16[64,4096]{1,0:T(8,128)(2,1)} %bitcast.22, bf16[4096,512]{1,0:T(8,128)(2,1)} %wv_ref.5), custom_call_target="tpu_custom_call" | custom-call | flops 1342177280 | bytes 8000000 | tf_op jit(solution)/shard_map/pallas_call | solution.py:101
  6.8 1.9 collective-permute-start
  8.7 0.0 copy-start.12
  8.7 0.0 copy-start.13
  8.7 0.0 copy-start.14
  8.7 9.4 %shard_map.201.a_ref.before_ref = f32[768,640]{1,0:T(8,128)} custom-call(bf16[1024,4096]{1,0:T(8,128)(2,1)} %y_ref.1, bf16[128,4096]{1,0:T(8,128)(2,1)} %get-tuple-element.45.wqk_ref, bf16[4096,512]{1,0:T(8,128)(2,1)} %wv_ref.5), custom_call_target="tpu_custom_call" | custom-call | flops 4026531840 | bytes 12000000 | tf_op jit(solution)/shard_map/pallas_call | solution.py:101
  18.2 0.7 pad_maximum_fusion.taps_ref.t_ref
  18.8 0.6 stack.39.dest_ref
  19.5 0.6 copy-done.16
  20.1 7.9 %shard_map.202 = (bf16[1024,256]{1,0:T(8,128)(2,1)}, bf16[1024,256]{1,0:T(8,128)(2,1)}, bf16[1024,512]{1,0:T(8,128)(2,1)}, bf16[1024,512]{1,0:T(8,128)(2,1)}, f3...) custom-call(f32[768,640]{1,0:T(8,128)} %shard_map.201.a_ref.before_ref, f32[256,640]{1,0:T(8,128)} %get-tuple-element.46.b_ref, ...), custom_call_target="tpu_custom_call" | custom-call | flops 4000000000 | bytes 15000000 | tf_op jit(solution)/shard_map/pallas_call | solution.py:101
  28.0 6.8 %all-to-all-start = ((f32[16,40,128]{2,1,0:T(8,128)}), f32[16,40,128]{2,1,0:T(8,128)S(1)}, u32[]{:S(2)}, u32[]{:S(2)}) async-start(f32[16,40,128]{2,1,0:T(8,128)} %bitcast.26), calls=%async_computation | async-start | bytes 655360 | tf_op jit(solution)/shard_map/all_to_all | solution.py:259
  34.8 6.3 %shard_map.204.num_ref = f32[1024,512]{1,0:T(8,128)} custom-call(bf16[1024,256]{1,0:T(8,128)(2,1)} %get-tuple-element.48.ql_ref, bf16[1024,256]{1,0:T(8,128)(2,1)} %get-tuple-element.53.kr_ref, bf16[1024,512]{1,0:T(8,128)(2,1)} %get-tuple-element.54.vh_ref, bf16[1024,512]{1,0:T(8,128)(2,1)} %get-tuple-element.55.vl_ref), custom_call_target="tpu_custom_call" | custom-call | flops 6000000000 | bytes 6000000 | tf_op jit(solution)/shard_map/pallas_call | solution.py:101
  41.1 0.0 all-to-all-done.x_ref
  41.1 0.7 copy-done.5
  41.8 1.7 shard_map.205
  43.5 5.7 %all-to-all-start.1 = ((f32[16,40,128]{2,1,0:T(8,128)}), f32[16,40,128]{2,1,0:T(8,128)S(1)}, u32[]{:S(2)}, u32[]{:S(2)}) async-start(f32[16,40,128]{2,1,0:T(8,128)} %shard_map.205), calls=%async_computation.1 | async-start | bytes 655360 | tf_op jit(solution)/shard_map/all_to_all | solution.py:264
  49.3 6.7 %shard_map.203 = (bf16[1024,1024]{1,0:T(8,128)(2,1)}, bf16[1024,1024]{1,0:T(8,128)(2,1)}, bf16[4,160,1024]{2,1,0:T(8,128)(2,1)}, bf16[4,160,1024]{2,1,0:T(8,128)(2,1)}) custom-call(bf16[1024,256]{1,0:T(8,128)(2,1)} %get-tuple-element.48.ql_ref, bf16[4,256,512]{2,1,0:T(8,128)(2,1)} %constant.99.clone.pick_ref, ...), custom_call_target="tpu_custom_call" | custom-call | flops 4000000000 | bytes 10000000 | tf_op jit(solution)/shard_map/pallas_call | solution.py:101
  55.9 0.0 all-to-all-done.1
  55.9 0.7 copy-done.10
  56.6 11.1 %shard_map.206 = (f32[1024,512]{1,0:T(8,128)}, bf16[1024,512]{1,0:T(8,128)(2,1)}, bf16[1024,512]{1,0:T(8,128)(2,1)}, f32[4,4,160,128]{3,2,1,0:T(8,128)}, f32[4,160,128]{2,1,0:T(8,128)}) custom-call(bf16[1024,1024]{1,0:T(8,128)(2,1)} %get-tuple-element.49.ph_ref, bf16[1024,1024]{1,0:T(8,128)(2,1)} %get-tuple-element.50.pl_ref, ...), custom_call_target="tpu_custom_call" | custom-call | flops 5000000000 | bytes 18000000 | tf_op jit(solution)/shard_map/pallas_call | solution.py:101
  67.8 5.7 %all-to-all-start.2 = ((f32[16,40,128]{2,1,0:T(8,128)}), f32[16,40,128]{2,1,0:T(8,128)S(1)}, u32[]{:S(2)}, u32[]{:S(2)}) async-start(f32[16,40,128]{2,1,0:T(8,128)} %bitcast.25), calls=%async_computation.2 | async-start | bytes 655360 | tf_op jit(solution)/shard_map/all_to_all | solution.py:259
  73.5 8.1 %shard_map.209 = (f32[1024,128]{1,0:T(8,128)}, f32[1024,512]{1,0:T(8,128)}) custom-call(bf16[1024,256]{1,0:T(8,128)(2,1)} %get-tuple-element.48.ql_ref, bf16[1024,256]{1,0:T(8,128)(2,1)} %get-tuple-element.53.kr_ref, bf16[1024,512]{1,0:T(8,128)(2,1)} %get-tuple-element.54.vh_ref, bf16[1024,512]{1,0:T(8,128)(2,1)} %get-tuple-element.55.vl_ref, ...), custom_call_target="tpu_custom_call" | custom-call | flops 8000000000 | bytes 8000000 | tf_op jit(solution)/shard_map/pallas_call | solution.py:101
  81.6 0.0 all-to-all-done.2.x_ref
  81.6 0.7 copy-done.4
  82.3 1.7 shard_map.207
  84.1 5.7 %all-to-all-start.3 = ((f32[16,40,128]{2,1,0:T(8,128)}), f32[16,40,128]{2,1,0:T(8,128)S(1)}, u32[]{:S(2)}, u32[]{:S(2)}) async-start(f32[16,40,128]{2,1,0:T(8,128)} %shard_map.207), calls=%async_computation.3 | async-start | bytes 655360 | tf_op jit(solution)/shard_map/all_to_all | solution.py:264
  89.8 12.6 %shard_map.208.gq_ref = f32[1024,128]{1,0:T(8,128)} custom-call(bf16[1024,256]{1,0:T(8,128)(2,1)} %get-tuple-element.48.ql_ref, bf16[1024,256]{1,0:T(8,128)(2,1)} %get-tuple-element.53.kr_ref, bf16[1024,512]{1,0:T(8,128)(2,1)} %get-tuple-element.54.vh_ref, bf16[1024,512]{1,0:T(8,128)(2,1)} %get-tuple-element.55.vl_ref, ...), custom_call_target="tpu_custom_call" | custom-call | flops 8000000000 | bytes 8000000 | tf_op jit(solution)/shard_map/pallas_call | solution.py:101
  102.4 0.0 all-to-all-done.3
  102.4 0.0 copy-start.3
  102.4 0.7 copy-done.3
  103.1 4.7 %shard_map.210 = (f32[256,640]{1,0:T(8,128)}, f32[8,640]{1,0:T(8,128)}) custom-call(bf16[1024,256]{1,0:T(8,128)(2,1)} %get-tuple-element.53.kr_ref, bf16[1024,512]{1,0:T(8,128)(2,1)} %get-tuple-element.54.vh_ref, bf16[1024,512]{1,0:T(8,128)(2,1)} %get-tuple-element.55.vl_ref, f32[4,4,160,128]{3,2,1,0:T(8,128)} %get-tuple-element.59.gs_ref, ...), custom_call_target="tpu_custom_call" | custom-call | flops 2000000000 | bytes 3000000 | tf_op jit(solution)/shard_map/pallas_call | solution.py:101
  107.8 2.0 collective-permute-start.1
  109.9 8.2 %shard_map.211 = (f32[768,640]{1,0:T(8,128)}, f32[8,640]{1,0:T(8,128)}) custom-call(bf16[1024,256]{1,0:T(8,128)(2,1)} %get-tuple-element.53.kr_ref, bf16[1024,512]{1,0:T(8,128)(2,1)} %get-tuple-element.54.vh_ref, bf16[1024,512]{1,0:T(8,128)(2,1)} %get-tuple-element.55.vl_ref, f32[4,4,160,128]{3,2,1,0:T(8,128)} %get-tuple-element.59.gs_ref, ...), custom_call_target="tpu_custom_call" | custom-call | flops 6000000000 | bytes 9000000 | tf_op jit(solution)/shard_map/pallas_call | solution.py:101
  118.1 0.0 copy-start.17
  118.1 0.6 copy-done.17
  118.7 12.1 %shard_map.212 = (bf16[4,2,512,512]{3,2,1,0:T(8,128)(2,1)}, f32[4,512,512]{2,1,0:T(8,128)}, bf16[4,512,512]{2,1,0:T(8,128)(2,1)}, bf16[640,1024]{1,0:T(8,128)(2,1)}) custom-call(s32[1]{0:T(128)} %bitcast.5.me_ref, f32[256,640]{1,0:T(8,128)} %get-tuple-element.65.a_ref, f32[768,640]{1,0:T(8,128)} %get-tuple-element.66.b_ref, f32[8,640]{1,0:T(8,128)} %copy-done.17, ...), custom_call_target="tpu_custom_call" | custom-call | flops 5368709120 | bytes 20000000 | tf_op jit(solution)/shard_map/pallas_call | solution.py:101
  130.8 10.5 %shard_map.214 = (bf16[8,640,256]{2,1,0:T(8,128)(2,1)}, bf16[8,640,256]{2,1,0:T(8,128)(2,1)}) custom-call(s32[9]{0:T(128)} %stack.39.dest_ref, bf16[640,1024]{1,0:T(8,128)(2,1)} %get-tuple-element.73.d_ref, bf16[1024,4096]{1,0:T(8,128)(2,1)} %y_ref.1, bf16[1024,4096]{1,0:T(8,128)(2,1)} %y_ref.1), custom_call_target="tpu_custom_call" | custom-call | flops 5368709120 | bytes 15000000 | tf_op jit(solution)/shard_map/pallas_call | solution.py:101
  141.3 0.4 collective-permute-start.4
  141.7 5.3 %all-to-all-start.4 = ((bf16[4,2,512,512]{3,2,1,0:T(8,128)(2,1)}), bf16[4,2,512,512]{3,2,1,0:T(8,128)(2,1)}, u32[]{:S(2)}, u32[]{:S(2)}) async-start(bf16[4,2,512,512]{3,2,1,0:T(8,128)(2,1)} %get-tuple-element.68), calls=%async_computation.4 | async-start | bytes 8388608 | tf_op jit(solution)/shard_map/all_to_all | solution.py:578
  147.0 2.9 %collective-permute-start.3 = (bf16[4,512,512]{2,1,0:T(8,128)(2,1)}, bf16[4,512,512]{2,1,0:T(8,128)(2,1)S(1)}, u32[]{:S(2)}, u32[]{:S(2)}) collective-permute-start(bf16[4,512,512]{2,1,0:T(8,128)(2,1)} %get-tuple-element.72), channel_id=1, source_target_pairs={{0,1},{1,0},{2,3},{3,2},{4,5},{5,4},{6,7},{7,6},{8,9},{9,8},{10,11... | collective-permute-start | bytes 6291464 | tf_op jit(solution)/shard_map/ppermute | solution.py:499
  149.9 1.5 copy-done.1
  151.4 5.2 %shard_map.215 = (bf16[2,640,256]{2,1,0:T(8,128)(2,1)}, bf16[2,640,256]{2,1,0:T(8,128)(2,1)}, bf16[2,640,256]{2,1,0:T(8,128)(2,1)}, bf16[2,640,256]{2,1,0:T(8,128)(2,1)}) custom-call(bf16[8,640,256]{2,1,0:T(8,128)(2,1)} %get-tuple-element.74.mine_ref, bf16[8,640,256]{2,1,0:T(8,128)(2,1)} %copy-done.1), custom_call_target="tpu_custom_call" | custom-call | bytes 8000000 | tf_op jit(solution)/shard_map/pallas_call | solution.py:101
  156.7 1.5 collective-permute-start.5
  158.2 0.7 collective-permute-start.6
  158.9 2.6 %collective-permute-start.7 = (bf16[2,640,256]{2,1,0:T(8,128)(2,1)}, bf16[2,640,256]{2,1,0:T(8,128)(2,1)S(1)}, u32[]{:S(2)}, u32[]{:S(2)}) collective-permute-start(bf16[2,640,256]{2,1,0:T(8,128)(2,1)} %get-tuple-element.79), channel_id=1, source_target_pairs={{0,48},{8,56},{16,0},{24,8},{32,16},{40,24},{48,32},{56,40},{64,11... | collective-permute-start | bytes 1966088 | tf_op jit(solution)/shard_map/ppermute | solution.py:652
  161.5 13.1 %collective-permute-done.5.a_ref = bf16[2,640,256]{2,1,0:T(8,128)(2,1)S(1)} collective-permute-done((bf16[2,640,256]{2,1,0:T(8,128)(2,1)}, bf16[2,640,256]{2,1,0:T(8,128)(2,1)S(1)}, u32[]{:S(2)}, u32[]{:S(2)}) %collective-permute-start.5) | collective-permute-done | bytes 655392 | tf_op jit(solution)/shard_map/ppermute | solution.py:652
  174.6 3.0 %collective-permute-done.6.b_ref = bf16[2,640,256]{2,1,0:T(8,128)(2,1)S(1)} collective-permute-done((bf16[2,640,256]{2,1,0:T(8,128)(2,1)}, bf16[2,640,256]{2,1,0:T(8,128)(2,1)S(1)}, u32[]{:S(2)}, u32[]{:S(2)}) %collective-permute-start.6) | collective-permute-done | bytes 655392 | tf_op jit(solution)/shard_map/ppermute | solution.py:652
  177.5 11.9 %collective-permute-done.7.c_ref = bf16[2,640,256]{2,1,0:T(8,128)(2,1)S(1)} collective-permute-done((bf16[2,640,256]{2,1,0:T(8,128)(2,1)}, bf16[2,640,256]{2,1,0:T(8,128)(2,1)S(1)}, u32[]{:S(2)}, u32[]{:S(2)}) %collective-permute-start.7) | collective-permute-done | bytes 655392 | tf_op jit(solution)/shard_map/ppermute | solution.py:652
  189.4 0.8 copy-done.8
  190.3 4.2 %shard_map.216 = (f32[640,256]{1,0:T(8,128)}, bf16[640,256]{1,0:T(8,128)(2,1)}) custom-call(bf16[2,640,256]{2,1,0:T(8,128)(2,1)} %get-tuple-element.76.mine_ref, bf16[2,640,256]{2,1,0:T(8,128)(2,1)} %copy-done.6, bf16[2,640,256]{2,1,0:T(8,128)(2,1)} %copy-done.7, bf16[2,640,256]{2,1,0:T(8,128)(2,1)} %copy-done.8), custom_call_target="tpu_custom_call" | custom-call | bytes 4000000 | tf_op jit(solution)/shard_map/pallas_call | solution.py:101
  194.5 1.6 collective-permute-done.3.refs_1_
  196.1 1.3 copy-done.2
  197.4 4.6 %shard_map.217 = bf16[4,512,512]{2,1,0:T(8,128)(2,1)} custom-call(f32[4,512,512]{2,1,0:T(8,128)} %get-tuple-element.71.refs_0_, bf16[4,512,512]{2,1,0:T(8,128)(2,1)} %copy-done.2, f32[640,256]{1,0:T(8,128)} %get-tuple-element.80.refs_2_.keep_ref), custom_call_target="tpu_custom_call" | custom-call | bytes 8000000 | tf_op jit(solution)/shard_map/pallas_call | solution.py:101
  202.1 5.3 %all-to-all-start.5 = ((bf16[4,512,512]{2,1,0:T(8,128)(2,1)}), bf16[4,512,512]{2,1,0:T(8,128)(2,1)S(1)}, u32[]{:S(2)}, u32[]{:S(2)}) async-start(bf16[4,512,512]{2,1,0:T(8,128)(2,1)} %shard_map.217), calls=%async_computation.5 | async-start | bytes 4194304 | tf_op jit(solution)/shard_map/all_to_all | solution.py:578
  207.3 4.3 %shard_map.213 = (f32[512,512]{1,0:T(8,128)}, bf16[512,512]{1,0:T(8,128)(2,1)}) custom-call(s32[1]{0:T(128)} %bitcast.5.me_ref, bf16[4,2,512,512]{3,2,1,0:T(8,128)(2,1)} %all-to-all-done.4.p_ref), custom_call_target="tpu_custom_call" | custom-call | bytes 6000000 | tf_op jit(solution)/shard_map/pallas_call | solution.py:101
  211.7 2.9 %collective-permute-start.2 = (bf16[512,512]{1,0:T(8,128)(2,1)}, bf16[512,512]{1,0:T(8,128)(2,1)S(1)}, u32[]{:S(2)}, u32[]{:S(2)}) collective-permute-start(bf16[512,512]{1,0:T(8,128)(2,1)} %get-tuple-element.70), channel_id=1, source_target_pairs={{0,1},{1,0},{2,3},{3,2},{4,5},{5,4},{6,7},{7,6},{8,9},{9,8},{10,11... | collective-permute-start | bytes 1572872 | tf_op jit(solution)/shard_map/ppermute | solution.py:499
  214.6 1.1 collective-permute-start.8
  215.6 18.3 %collective-permute-done.8.came_ref = bf16[640,256]{1,0:T(8,128)(2,1)S(1)} collective-permute-done((bf16[640,256]{1,0:T(8,128)(2,1)S(1)}, bf16[640,256]{1,0:T(8,128)(2,1)S(1)}, u32[]{:S(2)}, u32[]{:S(2)}) %collective-permute-start.8) | collective-permute-done | bytes 327712 | tf_op jit(solution)/shard_map/ppermute | solution.py:499
  233.9 0.7 copy-done.11
  234.6 3.8 %shard_map.219 = (f32[64,256]{1,0:T(8,128)}, f32[64,256]{1,0:T(8,128)}, f32[256,512]{1,0:T(8,128)}) custom-call(f32[640,256]{1,0:T(8,128)} %get-tuple-element.80.refs_2_.keep_ref, bf16[640,256]{1,0:T(8,128)(2,1)} %copy-done.11), custom_call_target="tpu_custom_call" | custom-call | bytes 2000000 | tf_op jit(solution)/shard_map/pallas_call | solution.py:101
  238.4 0.0 collective-permute-done.2.came_ref
  238.4 0.8 copy-done.9
  239.2 0.7 copy-done
  239.9 4.4 %shard_map.218 = bf16[1024,512]{1,0:T(8,128)(2,1)} custom-call(f32[512,512]{1,0:T(8,128)} %get-tuple-element.69.keep_ref, bf16[512,512]{1,0:T(8,128)(2,1)} %copy-done.9, bf16[4,512,512]{2,1,0:T(8,128)(2,1)} %copy-done), custom_call_target="tpu_custom_call" | custom-call | bytes 5000000 | tf_op jit(solution)/shard_map/pallas_call | solution.py:101
  (24 shorter events, 0.0 us)
Async XLA Ops:
  6.8 12.7 %collective-permute-start = (f32[8,640]{1,0:T(8,128)}, f32[8,640]{1,0:T(8,128)S(1)}, u32[]{:S(2)}, u32[]{:S(2)}) collective-permute-start(f32[8,640]{1,0:T(8,128)} %get-tuple-element.47), channel_id=1, source_target_pairs={{0,8},{8,16},{16,24},{24,32},{32,40},{40,48},{48,56},{56,64},{64,7... | collective-permute-start | bytes 61448 | tf_op jit(solution)/shard_map/ppermute | solution.py:719
  8.7 9.5 %copy-start.12 = (f32[3,512]{1,0:T(4,128)S(1)}, f32[3,512]{1,0:T(4,128)}, u32[]{:S(2)}) copy-start(f32[3,512]{1,0:T(4,128)} %param.23) | copy-start | bytes 18436
  8.7 9.4 %copy-start.13 = (f32[3,64]{1,0:T(4,128)S(1)}, f32[3,64]{1,0:T(4,128)}, u32[]{:S(2)}) copy-start(f32[3,64]{1,0:T(4,128)} %param.22) | copy-start | bytes 2308
  8.7 9.4 %copy-start.14 = (f32[3,64]{1,0:T(4,128)S(1)}, f32[3,64]{1,0:T(4,128)}, u32[]{:S(2)}) copy-start(f32[3,64]{1,0:T(4,128)} %param.21) | copy-start | bytes 2308
  19.5 0.6 copy-start.16
  28.0 13.1 %all-to-all-start = ((f32[16,40,128]{2,1,0:T(8,128)}), f32[16,40,128]{2,1,0:T(8,128)S(1)}, u32[]{:S(2)}, u32[]{:S(2)}) async-start(f32[16,40,128]{2,1,0:T(8,128)} %bitcast.26), calls=%async_computation | async-start | bytes 655360 | tf_op jit(solution)/shard_map/all_to_all | solution.py:259
  41.1 0.7 copy-start.5
  43.5 12.4 %all-to-all-start.1 = ((f32[16,40,128]{2,1,0:T(8,128)}), f32[16,40,128]{2,1,0:T(8,128)S(1)}, u32[]{:S(2)}, u32[]{:S(2)}) async-start(f32[16,40,128]{2,1,0:T(8,128)} %shard_map.205), calls=%async_computation.1 | async-start | bytes 655360 | tf_op jit(solution)/shard_map/all_to_all | solution.py:264
  55.9 0.7 copy-start.10
  67.8 13.8 %all-to-all-start.2 = ((f32[16,40,128]{2,1,0:T(8,128)}), f32[16,40,128]{2,1,0:T(8,128)S(1)}, u32[]{:S(2)}, u32[]{:S(2)}) async-start(f32[16,40,128]{2,1,0:T(8,128)} %bitcast.25), calls=%async_computation.2 | async-start | bytes 655360 | tf_op jit(solution)/shard_map/all_to_all | solution.py:259
  81.6 0.7 copy-start.4
  84.1 18.3 %all-to-all-start.3 = ((f32[16,40,128]{2,1,0:T(8,128)}), f32[16,40,128]{2,1,0:T(8,128)S(1)}, u32[]{:S(2)}, u32[]{:S(2)}) async-start(f32[16,40,128]{2,1,0:T(8,128)} %shard_map.207), calls=%async_computation.3 | async-start | bytes 655360 | tf_op jit(solution)/shard_map/all_to_all | solution.py:264
  102.4 0.7 copy-start.3
  107.8 10.3 %collective-permute-start.1 = (f32[8,640]{1,0:T(8,128)}, f32[8,640]{1,0:T(8,128)S(1)}, u32[]{:S(2)}, u32[]{:S(2)}) collective-permute-start(f32[8,640]{1,0:T(8,128)} %get-tuple-element.67), channel_id=1, source_target_pairs={{8,0},{16,8},{24,16},{32,24},{40,32},{48,40},{56,48},{64,56},{72,6... | collective-permute-start | bytes 61448 | tf_op jit(solution)/shard_map/ppermute | solution.py:719
  118.1 0.6 copy-start.17
  141.3 8.6 %collective-permute-start.4 = (bf16[8,640,256]{2,1,0:T(8,128)(2,1)}, bf16[8,640,256]{2,1,0:T(8,128)(2,1)S(1)}, u32[]{:S(2)}, u32[]{:S(2)}) collective-permute-start(bf16[8,640,256]{2,1,0:T(8,128)(2,1)} %get-tuple-element.75), channel_id=1, source_target_pairs={{0,8},{8,0},{16,24},{24,16},{32,40},{40,32},{48,56},{56,48},{64,72... | collective-permute-start | bytes 7864328 | tf_op jit(solution)/shard_map/ppermute | solution.py:499
  141.7 60.3 %all-to-all-start.4 = ((bf16[4,2,512,512]{3,2,1,0:T(8,128)(2,1)}), bf16[4,2,512,512]{3,2,1,0:T(8,128)(2,1)}, u32[]{:S(2)}, u32[]{:S(2)}) async-start(bf16[4,2,512,512]{3,2,1,0:T(8,128)(2,1)} %get-tuple-element.68), calls=%async_computation.4 | async-start | bytes 8388608 | tf_op jit(solution)/shard_map/all_to_all | solution.py:578
  147.0 49.1 %collective-permute-start.3 = (bf16[4,512,512]{2,1,0:T(8,128)(2,1)}, bf16[4,512,512]{2,1,0:T(8,128)(2,1)S(1)}, u32[]{:S(2)}, u32[]{:S(2)}) collective-permute-start(bf16[4,512,512]{2,1,0:T(8,128)(2,1)} %get-tuple-element.72), channel_id=1, source_target_pairs={{0,1},{1,0},{2,3},{3,2},{4,5},{5,4},{6,7},{7,6},{8,9},{9,8},{10,11... | collective-permute-start | bytes 6291464 | tf_op jit(solution)/shard_map/ppermute | solution.py:499
  149.9 1.5 copy-start.1
  156.7 17.9 %collective-permute-start.5 = (bf16[2,640,256]{2,1,0:T(8,128)(2,1)}, bf16[2,640,256]{2,1,0:T(8,128)(2,1)S(1)}, u32[]{:S(2)}, u32[]{:S(2)}) collective-permute-start(bf16[2,640,256]{2,1,0:T(8,128)(2,1)} %get-tuple-element.77), channel_id=1, source_target_pairs={{0,16},{8,24},{16,32},{24,40},{32,48},{40,56},{48,0},{56,8},{64,80... | collective-permute-start | bytes 1966088 | tf_op jit(solution)/shard_map/ppermute | solution.py:652
  158.2 19.4 %collective-permute-start.6 = (bf16[2,640,256]{2,1,0:T(8,128)(2,1)}, bf16[2,640,256]{2,1,0:T(8,128)(2,1)S(1)}, u32[]{:S(2)}, u32[]{:S(2)}) collective-permute-start(bf16[2,640,256]{2,1,0:T(8,128)(2,1)} %get-tuple-element.78), channel_id=1, source_target_pairs={{0,32},{8,40},{16,48},{24,56},{32,0},{40,8},{48,16},{56,24},{64,96... | collective-permute-start | bytes 1966088 | tf_op jit(solution)/shard_map/ppermute | solution.py:652
  158.9 30.6 %collective-permute-start.7 = (bf16[2,640,256]{2,1,0:T(8,128)(2,1)}, bf16[2,640,256]{2,1,0:T(8,128)(2,1)S(1)}, u32[]{:S(2)}, u32[]{:S(2)}) collective-permute-start(bf16[2,640,256]{2,1,0:T(8,128)(2,1)} %get-tuple-element.79), channel_id=1, source_target_pairs={{0,48},{8,56},{16,0},{24,8},{32,16},{40,24},{48,32},{56,40},{64,11... | collective-permute-start | bytes 1966088 | tf_op jit(solution)/shard_map/ppermute | solution.py:652
  174.6 14.9 %copy-start.6 = (bf16[2,640,256]{2,1,0:T(8,128)(2,1)}, bf16[2,640,256]{2,1,0:T(8,128)(2,1)S(1)}, u32[]{:S(2)}) copy-start(bf16[2,640,256]{2,1,0:T(8,128)(2,1)S(1)} %collective-permute-done.5.a_ref) | copy-start | bytes 1966084
  177.5 11.9 %copy-start.7 = (bf16[2,640,256]{2,1,0:T(8,128)(2,1)}, bf16[2,640,256]{2,1,0:T(8,128)(2,1)S(1)}, u32[]{:S(2)}) copy-start(bf16[2,640,256]{2,1,0:T(8,128)(2,1)S(1)} %collective-permute-done.6.b_ref) | copy-start | bytes 1966084
  189.4 0.8 copy-start.8
  196.1 1.3 copy-start.2
  202.1 36.3 %all-to-all-start.5 = ((bf16[4,512,512]{2,1,0:T(8,128)(2,1)}), bf16[4,512,512]{2,1,0:T(8,128)(2,1)S(1)}, u32[]{:S(2)}, u32[]{:S(2)}) async-start(bf16[4,512,512]{2,1,0:T(8,128)(2,1)} %shard_map.217), calls=%async_computation.5 | async-start | bytes 4194304 | tf_op jit(solution)/shard_map/all_to_all | solution.py:578
  207.3 7.2 %copy-start.15 = (bf16[640,256]{1,0:T(8,128)(2,1)S(1)}, bf16[640,256]{1,0:T(8,128)(2,1)}, u32[]{:S(2)}) copy-start(bf16[640,256]{1,0:T(8,128)(2,1)} %get-tuple-element.81) | copy-start | bytes 983044
  211.7 26.7 %collective-permute-start.2 = (bf16[512,512]{1,0:T(8,128)(2,1)}, bf16[512,512]{1,0:T(8,128)(2,1)S(1)}, u32[]{:S(2)}, u32[]{:S(2)}) collective-permute-start(bf16[512,512]{1,0:T(8,128)(2,1)} %get-tuple-element.70), channel_id=1, source_target_pairs={{0,1},{1,0},{2,3},{3,2},{4,5},{5,4},{6,7},{7,6},{8,9},{9,8},{10,11... | collective-permute-start | bytes 1572872 | tf_op jit(solution)/shard_map/ppermute | solution.py:499
  214.6 19.3 %collective-permute-start.8 = (bf16[640,256]{1,0:T(8,128)(2,1)S(1)}, bf16[640,256]{1,0:T(8,128)(2,1)S(1)}, u32[]{:S(2)}, u32[]{:S(2)}) collective-permute-start(bf16[640,256]{1,0:T(8,128)(2,1)S(1)} %copy-done.15), channel_id=1, source_target_pairs={{0,64},{8,72},{16,80},{24,88},{32,96},{40,104},{48,112},{56,120},{... | collective-permute-start | bytes 983048 | tf_op jit(solution)/shard_map/ppermute | solution.py:499
  233.9 0.7 copy-start.11
  238.4 0.8 copy-start.9
  238.4 1.5 copy-start

commit v6 on v5

--- a/solution.py
+++ b/solution.py
@@ -578,12 +578,12 @@
     return lax.all_to_all(x, "tp", 0, 0, axis_index_groups=[[0, 2, 4, 6], [1, 3, 5, 7]])
 
 
-def reduce_input_grad(side_y, by_z, keep, send, before):
+def reduce_input_grad(side_y, by_z, keep, send, first, second):
     half, tile = LEN // 2, LEN // 4
     came = flip(send, "tp", 1)
     tops = along_z(by_z)
     block = pl.BlockSpec((1, half, 512), lambda i: (i, 0, 0))
-    pairs = call(pair_kernel, (4,), [block, block], block, arr((4, half, 512), BF16), (keep, came), moved=8e6, after=(before,))
+    pairs = call(pair_kernel, (4,), [block, block], block, arr((4, half, 512), BF16), (keep, came), moved=8e6, after=first)
     rows = pl.BlockSpec((tile // 2, 512), lambda i, me: (i, 0))
     keep, send = call(
         top_kernel,
@@ -593,6 +593,7 @@
         [arr((half, 512)), arr((half, 512), BF16)],
         (side_y, tops),
         prefetch=1,
+        after=second,
         moved=6e6,
     )
     pairs = along_z(pairs)
@@ -747,7 +748,7 @@
     mine, *rest = weight_parts(dt, inputs)
     parts = [mine, *(to_x(part, dx) for dx, part in enumerate(rest, 1))]
     own, came = reduce_weight_grad(parts)
-    input_grad = reduce_input_grad(side_y, by_z, keep, send, own)
+    input_grad = reduce_input_grad(side_y, by_z, keep, send, parts[1:], ())
     grad_query, grad_key, grad_value = finish_weight_grad(own, came)
     return (outputs, input_grad, grad_query.T, grad_key.T, grad_value)
 

time: 248 us -> 249 us (level)
    ppermute x4, waiting for transfers between devices: 19.9 us -> 48.7 us  [flip(): lax.ppermute(x, axis, [(i, i ^ bit) for i in range(lax.axis_size(axis))])]
    ppermute x3, waiting for transfers between devices: 27.9 us -> 0.01 us  [to_x(): lax.ppermute(x, 'seq', [(s, s // 8 * 8 + (s % 8 + 2 * by) % 8) for s in r...]
    unnamed x36 -> x34, local copies, waits for them, and re-layouts: 9.96 us -> 9.73 us
  transfers between devices with their start and end apart: 15 -> 15, of which waited for: 5 -> 2; matrix products, arithmetic and copies ran while one was open for 1% -> 1% of each run, Pallas kernels for 30% -> 30%
where the time goes in v6:
time: 249 us; the launch traced here: 245 us
  Pallas kernels  134 us (54%)
  starting transfers between devices  50.5 us (20%)
  waiting for transfers between devices  48.7 us (20%)
  local copies, waits for them, and re-layouts  10.4 us (4%)
    pallas_call x20, Pallas kernels, call(): pl.pallas_call(body, grid_spec=pltpu.PrefetchScalarGridSpec(num_scalar_pr...  134 us
    ppermute x4, waiting for transfers between devices, flip(): lax.ppermute(x, axis, [(i, i ^ bit) for i in range(lax.axis_size(axis))])  48.7 us
    all_to_all x2, starting transfers between devices, carried_in(): pieces = lax.all_to_all(state.reshape(count, rows, HDIM), 'seq', 0, 0)  12.5 us
    all_to_all x2, starting transfers between devices, carried_in(): return lax.all_to_all(sums, 'seq', 0, 0).reshape(HEADS, NF, HDIM)  11.4 us
    all_to_all x2, starting transfers between devices, along_z(): lax.all_to_all(x, 'tp', 0, 0, axis_index_groups=[[0, 2, 4, 6], [1, 3, 5,...  10.6 us
    unnamed x34, local copies, waits for them, and re-layouts  9.73 us
    ppermute x4, starting transfers between devices, flip(): lax.ppermute(x, axis, [(i, i ^ bit) for i in range(lax.axis_size(axis))])  7.25 us
  transfers between devices with their start and end apart: 15, of which 2 were waited for; matrix products, arithmetic and copies ran while one was open for 1% of the time, Pallas kernels for 30%

profile of v6, /device:TPU:2, one launch (start us, length us, event | category | flops | bytes accessed | tf_op | source)
XLA Modules:
  0.0 244.9 jit_solution(11514605436261692581)
XLA Ops:
  0.6 6.2 %shard_map.200 = (f32[256,640]{1,0:T(8,128)}, f32[8,640]{1,0:T(8,128)}, bf16[128,4096]{1,0:T(8,128)(2,1)}) custom-call(bf16[1024,4096]{1,0:T(8,128)(2,1)} %y_ref.1, bf16[64,4096]{1,0:T(8,128)(2,1)} %bitcast.21, bf16[64,4096]{1,0:T(8,128)(2,1)} %bitcast.22, bf16[4096,512]{1,0:T(8,128)(2,1)} %wv_ref.5), custom_call_target="tpu_custom_call" | custom-call | flops 1342177280 | bytes 8000000 | tf_op jit(solution)/shard_map/pallas_call | solution.py:101
  6.8 1.9 collective-permute-start
  8.7 0.0 copy-start.12
  8.7 0.0 copy-start.13
  8.7 0.0 copy-start.14
  8.7 9.4 %shard_map.201.a_ref.before_ref = f32[768,640]{1,0:T(8,128)} custom-call(bf16[1024,4096]{1,0:T(8,128)(2,1)} %y_ref.1, bf16[128,4096]{1,0:T(8,128)(2,1)} %get-tuple-element.45.wqk_ref, bf16[4096,512]{1,0:T(8,128)(2,1)} %wv_ref.5), custom_call_target="tpu_custom_call" | custom-call | flops 4026531840 | bytes 12000000 | tf_op jit(solution)/shard_map/pallas_call | solution.py:101
  18.2 0.7 pad_maximum_fusion.taps_ref.t_ref
  18.8 0.6 stack.39.dest_ref
  19.5 0.0 collective-permute-done.tail_ref
  19.5 0.6 copy-done.15
  20.1 7.9 %shard_map.202 = (bf16[1024,256]{1,0:T(8,128)(2,1)}, bf16[1024,256]{1,0:T(8,128)(2,1)}, bf16[1024,512]{1,0:T(8,128)(2,1)}, bf16[1024,512]{1,0:T(8,128)(2,1)}, f3...) custom-call(f32[768,640]{1,0:T(8,128)} %shard_map.201.a_ref.before_ref, f32[256,640]{1,0:T(8,128)} %get-tuple-element.46.b_ref, ...), custom_call_target="tpu_custom_call" | custom-call | flops 4000000000 | bytes 15000000 | tf_op jit(solution)/shard_map/pallas_call | solution.py:101
  28.0 6.8 %all-to-all-start = ((f32[16,40,128]{2,1,0:T(8,128)}), f32[16,40,128]{2,1,0:T(8,128)S(1)}, u32[]{:S(2)}, u32[]{:S(2)}) async-start(f32[16,40,128]{2,1,0:T(8,128)} %bitcast.26), calls=%async_computation | async-start | bytes 655360 | tf_op jit(solution)/shard_map/all_to_all | solution.py:259
  34.8 6.3 %shard_map.204.num_ref = f32[1024,512]{1,0:T(8,128)} custom-call(bf16[1024,256]{1,0:T(8,128)(2,1)} %get-tuple-element.48.ql_ref, bf16[1024,256]{1,0:T(8,128)(2,1)} %get-tuple-element.53.kr_ref, bf16[1024,512]{1,0:T(8,128)(2,1)} %get-tuple-element.54.vh_ref, bf16[1024,512]{1,0:T(8,128)(2,1)} %get-tuple-element.55.vl_ref), custom_call_target="tpu_custom_call" | custom-call | flops 6000000000 | bytes 6000000 | tf_op jit(solution)/shard_map/pallas_call | solution.py:101
  41.1 0.0 all-to-all-done.x_ref
  41.1 0.7 copy-done.8
  41.8 1.7 shard_map.205
  43.5 5.7 %all-to-all-start.1 = ((f32[16,40,128]{2,1,0:T(8,128)}), f32[16,40,128]{2,1,0:T(8,128)S(1)}, u32[]{:S(2)}, u32[]{:S(2)}) async-start(f32[16,40,128]{2,1,0:T(8,128)} %shard_map.205), calls=%async_computation.1 | async-start | bytes 655360 | tf_op jit(solution)/shard_map/all_to_all | solution.py:264
  49.3 6.7 %shard_map.203 = (bf16[1024,1024]{1,0:T(8,128)(2,1)}, bf16[1024,1024]{1,0:T(8,128)(2,1)}, bf16[4,160,1024]{2,1,0:T(8,128)(2,1)}, bf16[4,160,1024]{2,1,0:T(8,128)(2,1)}) custom-call(bf16[1024,256]{1,0:T(8,128)(2,1)} %get-tuple-element.48.ql_ref, bf16[4,256,512]{2,1,0:T(8,128)(2,1)} %constant.99.clone.pick_ref, ...), custom_call_target="tpu_custom_call" | custom-call | flops 4000000000 | bytes 10000000 | tf_op jit(solution)/shard_map/pallas_call | solution.py:101
  55.9 0.0 all-to-all-done.1
  55.9 0.7 copy-done.10
  56.7 11.1 %shard_map.206 = (f32[1024,512]{1,0:T(8,128)}, bf16[1024,512]{1,0:T(8,128)(2,1)}, bf16[1024,512]{1,0:T(8,128)(2,1)}, f32[4,4,160,128]{3,2,1,0:T(8,128)}, f32[4,160,128]{2,1,0:T(8,128)}) custom-call(bf16[1024,1024]{1,0:T(8,128)(2,1)} %get-tuple-element.49.ph_ref, bf16[1024,1024]{1,0:T(8,128)(2,1)} %get-tuple-element.50.pl_ref, ...), custom_call_target="tpu_custom_call" | custom-call | flops 5000000000 | bytes 18000000 | tf_op jit(solution)/shard_map/pallas_call | solution.py:101
  67.8 5.7 %all-to-all-start.2 = ((f32[16,40,128]{2,1,0:T(8,128)}), f32[16,40,128]{2,1,0:T(8,128)S(1)}, u32[]{:S(2)}, u32[]{:S(2)}) async-start(f32[16,40,128]{2,1,0:T(8,128)} %bitcast.25), calls=%async_computation.2 | async-start | bytes 655360 | tf_op jit(solution)/shard_map/all_to_all | solution.py:259
  73.5 8.1 %shard_map.209 = (f32[1024,128]{1,0:T(8,128)}, f32[1024,512]{1,0:T(8,128)}) custom-call(bf16[1024,256]{1,0:T(8,128)(2,1)} %get-tuple-element.48.ql_ref, bf16[1024,256]{1,0:T(8,128)(2,1)} %get-tuple-element.53.kr_ref, bf16[1024,512]{1,0:T(8,128)(2,1)} %get-tuple-element.54.vh_ref, bf16[1024,512]{1,0:T(8,128)(2,1)} %get-tuple-element.55.vl_ref, ...), custom_call_target="tpu_custom_call" | custom-call | flops 8000000000 | bytes 8000000 | tf_op jit(solution)/shard_map/pallas_call | solution.py:101
  81.6 0.0 all-to-all-done.2.x_ref
  81.6 0.7 copy-done.7
  82.4 1.8 shard_map.207
  84.1 5.7 %all-to-all-start.3 = ((f32[16,40,128]{2,1,0:T(8,128)}), f32[16,40,128]{2,1,0:T(8,128)S(1)}, u32[]{:S(2)}, u32[]{:S(2)}) async-start(f32[16,40,128]{2,1,0:T(8,128)} %shard_map.207), calls=%async_computation.3 | async-start | bytes 655360 | tf_op jit(solution)/shard_map/all_to_all | solution.py:264
  89.8 12.6 %shard_map.208.gq_ref = f32[1024,128]{1,0:T(8,128)} custom-call(bf16[1024,256]{1,0:T(8,128)(2,1)} %get-tuple-element.48.ql_ref, bf16[1024,256]{1,0:T(8,128)(2,1)} %get-tuple-element.53.kr_ref, bf16[1024,512]{1,0:T(8,128)(2,1)} %get-tuple-element.54.vh_ref, bf16[1024,512]{1,0:T(8,128)(2,1)} %get-tuple-element.55.vl_ref, ...), custom_call_target="tpu_custom_call" | custom-call | flops 8000000000 | bytes 8000000 | tf_op jit(solution)/shard_map/pallas_call | solution.py:101
  102.4 0.0 copy-start.6
  102.5 0.7 copy-done.6
  103.2 4.7 %shard_map.210 = (f32[256,640]{1,0:T(8,128)}, f32[8,640]{1,0:T(8,128)}) custom-call(bf16[1024,256]{1,0:T(8,128)(2,1)} %get-tuple-element.53.kr_ref, bf16[1024,512]{1,0:T(8,128)(2,1)} %get-tuple-element.54.vh_ref, bf16[1024,512]{1,0:T(8,128)(2,1)} %get-tuple-element.55.vl_ref, f32[4,4,160,128]{3,2,1,0:T(8,128)} %get-tuple-element.59.gs_ref, ...), custom_call_target="tpu_custom_call" | custom-call | flops 2000000000 | bytes 3000000 | tf_op jit(solution)/shard_map/pallas_call | solution.py:101
  107.9 2.0 collective-permute-start.1
  109.9 8.3 %shard_map.211 = (f32[768,640]{1,0:T(8,128)}, f32[8,640]{1,0:T(8,128)}) custom-call(bf16[1024,256]{1,0:T(8,128)(2,1)} %get-tuple-element.53.kr_ref, bf16[1024,512]{1,0:T(8,128)(2,1)} %get-tuple-element.54.vh_ref, bf16[1024,512]{1,0:T(8,128)(2,1)} %get-tuple-element.55.vl_ref, f32[4,4,160,128]{3,2,1,0:T(8,128)} %get-tuple-element.59.gs_ref, ...), custom_call_target="tpu_custom_call" | custom-call | flops 6000000000 | bytes 9000000 | tf_op jit(solution)/shard_map/pallas_call | solution.py:101
  118.2 0.0 collective-permute-done.1.h_ref
  118.2 0.0 copy-start.16
  118.2 0.6 copy-done.16
  118.8 12.1 %shard_map.212 = (bf16[4,2,512,512]{3,2,1,0:T(8,128)(2,1)}, f32[4,512,512]{2,1,0:T(8,128)}, bf16[4,512,512]{2,1,0:T(8,128)(2,1)}, bf16[640,1024]{1,0:T(8,128)(2,1)}) custom-call(s32[1]{0:T(128)} %bitcast.5.me_ref, f32[256,640]{1,0:T(8,128)} %get-tuple-element.65.a_ref, f32[768,640]{1,0:T(8,128)} %get-tuple-element.66.b_ref, f32[8,640]{1,0:T(8,128)} %copy-done.16, ...), custom_call_target="tpu_custom_call" | custom-call | flops 5368709120 | bytes 20000000 | tf_op jit(solution)/shard_map/pallas_call | solution.py:101
  130.9 10.5 %shard_map.214 = (bf16[8,640,256]{2,1,0:T(8,128)(2,1)}, bf16[8,640,256]{2,1,0:T(8,128)(2,1)}) custom-call(s32[9]{0:T(128)} %stack.39.dest_ref, bf16[640,1024]{1,0:T(8,128)(2,1)} %get-tuple-element.73.d_ref, bf16[1024,4096]{1,0:T(8,128)(2,1)} %y_ref.1, bf16[1024,4096]{1,0:T(8,128)(2,1)} %y_ref.1), custom_call_target="tpu_custom_call" | custom-call | flops 5368709120 | bytes 15000000 | tf_op jit(solution)/shard_map/pallas_call | solution.py:101
  141.4 0.4 collective-permute-start.4
  141.8 5.3 %all-to-all-start.4 = ((bf16[4,2,512,512]{3,2,1,0:T(8,128)(2,1)}), bf16[4,2,512,512]{3,2,1,0:T(8,128)(2,1)}, u32[]{:S(2)}, u32[]{:S(2)}) async-start(bf16[4,2,512,512]{3,2,1,0:T(8,128)(2,1)} %get-tuple-element.68), calls=%async_computation.4 | async-start | bytes 8388608 | tf_op jit(solution)/shard_map/all_to_all | solution.py:578
  147.1 2.9 %collective-permute-start.3 = (bf16[4,512,512]{2,1,0:T(8,128)(2,1)}, bf16[4,512,512]{2,1,0:T(8,128)(2,1)S(1)}, u32[]{:S(2)}, u32[]{:S(2)}) collective-permute-start(bf16[4,512,512]{2,1,0:T(8,128)(2,1)} %get-tuple-element.72), channel_id=1, source_target_pairs={{0,1},{1,0},{2,3},{3,2},{4,5},{5,4},{6,7},{7,6},{8,9},{9,8},{10,11... | collective-permute-start | bytes 6291464 | tf_op jit(solution)/shard_map/ppermute | solution.py:499
  150.0 0.0 collective-permute-done.4.came_ref
  150.0 1.5 copy-done.4
  151.5 5.2 %shard_map.215 = (bf16[2,640,256]{2,1,0:T(8,128)(2,1)}, bf16[2,640,256]{2,1,0:T(8,128)(2,1)}, bf16[2,640,256]{2,1,0:T(8,128)(2,1)}, bf16[2,640,256]{2,1,0:T(8,128)(2,1)}) custom-call(bf16[8,640,256]{2,1,0:T(8,128)(2,1)} %get-tuple-element.74.mine_ref, bf16[8,640,256]{2,1,0:T(8,128)(2,1)} %copy-done.4), custom_call_target="tpu_custom_call" | custom-call | bytes 8000000 | tf_op jit(solution)/shard_map/pallas_call | solution.py:101
  156.8 1.5 collective-permute-start.5
  158.2 0.7 collective-permute-start.6
  159.0 2.6 %collective-permute-start.7 = (bf16[2,640,256]{2,1,0:T(8,128)(2,1)}, bf16[2,640,256]{2,1,0:T(8,128)(2,1)S(1)}, u32[]{:S(2)}, u32[]{:S(2)}) collective-permute-start(bf16[2,640,256]{2,1,0:T(8,128)(2,1)} %get-tuple-element.78), channel_id=1, source_target_pairs={{0,48},{8,56},{16,0},{24,8},{32,16},{40,24},{48,32},{56,40},{64,11... | collective-permute-start | bytes 1966088 | tf_op jit(solution)/shard_map/ppermute | solution.py:653
  161.6 34.6 %collective-permute-done.3.refs_1_ = bf16[4,512,512]{2,1,0:T(8,128)(2,1)S(1)} collective-permute-done((bf16[4,512,512]{2,1,0:T(8,128)(2,1)}, bf16[4,512,512]{2,1,0:T(8,128)(2,1)S(1)}, u32[]{:S(2)}, u32[]{:S(2)}) %collective-permute-start.3) | collective-permute-done | bytes 2097184 | tf_op jit(solution)/shard_map/ppermute | solution.py:499
  196.3 1.3 copy-done.5
  197.5 0.2 copy-done.1
  197.8 0.2 copy-done.2
  197.9 0.2 copy-done.3
  198.2 4.6 %shard_map.216 = bf16[4,512,512]{2,1,0:T(8,128)(2,1)} custom-call(f32[4,512,512]{2,1,0:T(8,128)} %get-tuple-element.71.refs_0_, bf16[4,512,512]{2,1,0:T(8,128)(2,1)} %copy-done.5, bf16[2,640,256]{2,1,0:T(8,128)(2,1)} %copy-done.1, bf16[2,640,256]{2,1,0:T(8,128)(2,1)} %copy-done.2, bf16[2,640,256]{2,1,0:T(8,128)(2,1)} %copy-done.3), custom_call_target="tpu_custom_call" | custom-call | bytes 8000000 | tf_op jit(solution)/shard_map/pallas_call | solution.py:101
  202.8 5.3 %all-to-all-start.5 = ((bf16[4,512,512]{2,1,0:T(8,128)(2,1)}), bf16[4,512,512]{2,1,0:T(8,128)(2,1)S(1)}, u32[]{:S(2)}, u32[]{:S(2)}) async-start(bf16[4,512,512]{2,1,0:T(8,128)(2,1)} %shard_map.216), calls=%async_computation.5 | async-start | bytes 4194304 | tf_op jit(solution)/shard_map/all_to_all | solution.py:578
  208.1 4.3 %shard_map.213 = (f32[512,512]{1,0:T(8,128)}, bf16[512,512]{1,0:T(8,128)(2,1)}) custom-call(s32[1]{0:T(128)} %bitcast.5.me_ref, bf16[4,2,512,512]{3,2,1,0:T(8,128)(2,1)} %all-to-all-done.4.p_ref), custom_call_target="tpu_custom_call" | custom-call | bytes 6000000 | tf_op jit(solution)/shard_map/pallas_call | solution.py:101
  212.4 2.9 %collective-permute-start.2 = (bf16[512,512]{1,0:T(8,128)(2,1)}, bf16[512,512]{1,0:T(8,128)(2,1)S(1)}, u32[]{:S(2)}, u32[]{:S(2)}) collective-permute-start(bf16[512,512]{1,0:T(8,128)(2,1)} %get-tuple-element.70), channel_id=1, source_target_pairs={{0,1},{1,0},{2,3},{3,2},{4,5},{5,4},{6,7},{7,6},{8,9},{9,8},{10,11... | collective-permute-start | bytes 1572872 | tf_op jit(solution)/shard_map/ppermute | solution.py:499
  215.3 4.2 %shard_map.218 = (f32[640,256]{1,0:T(8,128)}, bf16[640,256]{1,0:T(8,128)(2,1)}) custom-call(bf16[2,640,256]{2,1,0:T(8,128)(2,1)} %get-tuple-element.79.mine_ref, bf16[2,640,256]{2,1,0:T(8,128)(2,1)} %copy-done.1, bf16[2,640,256]{2,1,0:T(8,128)(2,1)} %copy-done.2, bf16[2,640,256]{2,1,0:T(8,128)(2,1)} %copy-done.3), custom_call_target="tpu_custom_call" | custom-call | bytes 4000000 | tf_op jit(solution)/shard_map/pallas_call | solution.py:101
  219.5 1.1 collective-permute-start.8
  220.6 14.0 %collective-permute-done.8.came_ref = bf16[640,256]{1,0:T(8,128)(2,1)S(1)} collective-permute-done((bf16[640,256]{1,0:T(8,128)(2,1)}, bf16[640,256]{1,0:T(8,128)(2,1)S(1)}, u32[]{:S(2)}, u32[]{:S(2)}) %collective-permute-start.8) | collective-permute-done | bytes 327712 | tf_op jit(solution)/shard_map/ppermute | solution.py:499
  234.6 0.7 copy-done.11
  235.3 3.8 %shard_map.219 = (f32[64,256]{1,0:T(8,128)}, f32[64,256]{1,0:T(8,128)}, f32[256,512]{1,0:T(8,128)}) custom-call(f32[640,256]{1,0:T(8,128)} %get-tuple-element.80.keep_ref, bf16[640,256]{1,0:T(8,128)(2,1)} %copy-done.11), custom_call_target="tpu_custom_call" | custom-call | bytes 2000000 | tf_op jit(solution)/shard_map/pallas_call | solution.py:101
  239.1 0.8 copy-done.9
  239.9 0.7 copy-done
  240.6 4.4 %shard_map.217 = bf16[1024,512]{1,0:T(8,128)(2,1)} custom-call(f32[512,512]{1,0:T(8,128)} %get-tuple-element.69.keep_ref, bf16[512,512]{1,0:T(8,128)(2,1)} %copy-done.9, bf16[4,512,512]{2,1,0:T(8,128)(2,1)} %copy-done), custom_call_target="tpu_custom_call" | custom-call | bytes 5000000 | tf_op jit(solution)/shard_map/pallas_call | solution.py:101
  (22 shorter events, 0.0 us)
Async XLA Ops:
  6.8 12.7 %collective-permute-start = (f32[8,640]{1,0:T(8,128)}, f32[8,640]{1,0:T(8,128)S(1)}, u32[]{:S(2)}, u32[]{:S(2)}) collective-permute-start(f32[8,640]{1,0:T(8,128)} %get-tuple-element.47), channel_id=1, source_target_pairs={{0,8},{8,16},{16,24},{24,32},{32,40},{40,48},{48,56},{56,64},{64,7... | collective-permute-start | bytes 61448 | tf_op jit(solution)/shard_map/ppermute | solution.py:720
  8.7 9.5 %copy-start.12 = (f32[3,512]{1,0:T(4,128)S(1)}, f32[3,512]{1,0:T(4,128)}, u32[]{:S(2)}) copy-start(f32[3,512]{1,0:T(4,128)} %param.23) | copy-start | bytes 18436
  8.7 9.4 %copy-start.13 = (f32[3,64]{1,0:T(4,128)S(1)}, f32[3,64]{1,0:T(4,128)}, u32[]{:S(2)}) copy-start(f32[3,64]{1,0:T(4,128)} %param.22) | copy-start | bytes 2308
  8.7 9.4 %copy-start.14 = (f32[3,64]{1,0:T(4,128)S(1)}, f32[3,64]{1,0:T(4,128)}, u32[]{:S(2)}) copy-start(f32[3,64]{1,0:T(4,128)} %param.21) | copy-start | bytes 2308
  19.5 0.6 copy-start.15
  28.0 13.1 %all-to-all-start = ((f32[16,40,128]{2,1,0:T(8,128)}), f32[16,40,128]{2,1,0:T(8,128)S(1)}, u32[]{:S(2)}, u32[]{:S(2)}) async-start(f32[16,40,128]{2,1,0:T(8,128)} %bitcast.26), calls=%async_computation | async-start | bytes 655360 | tf_op jit(solution)/shard_map/all_to_all | solution.py:259
  41.1 0.7 copy-start.8
  43.5 12.4 %all-to-all-start.1 = ((f32[16,40,128]{2,1,0:T(8,128)}), f32[16,40,128]{2,1,0:T(8,128)S(1)}, u32[]{:S(2)}, u32[]{:S(2)}) async-start(f32[16,40,128]{2,1,0:T(8,128)} %shard_map.205), calls=%async_computation.1 | async-start | bytes 655360 | tf_op jit(solution)/shard_map/all_to_all | solution.py:264
  55.9 0.7 copy-start.10
  67.8 13.8 %all-to-all-start.2 = ((f32[16,40,128]{2,1,0:T(8,128)}), f32[16,40,128]{2,1,0:T(8,128)S(1)}, u32[]{:S(2)}, u32[]{:S(2)}) async-start(f32[16,40,128]{2,1,0:T(8,128)} %bitcast.25), calls=%async_computation.2 | async-start | bytes 655360 | tf_op jit(solution)/shard_map/all_to_all | solution.py:259
  81.6 0.7 copy-start.7
  84.1 18.3 %all-to-all-start.3 = ((f32[16,40,128]{2,1,0:T(8,128)}), f32[16,40,128]{2,1,0:T(8,128)S(1)}, u32[]{:S(2)}, u32[]{:S(2)}) async-start(f32[16,40,128]{2,1,0:T(8,128)} %shard_map.207), calls=%async_computation.3 | async-start | bytes 655360 | tf_op jit(solution)/shard_map/all_to_all | solution.py:264
  102.4 0.7 copy-start.6
  107.9 10.3 %collective-permute-start.1 = (f32[8,640]{1,0:T(8,128)}, f32[8,640]{1,0:T(8,128)S(1)}, u32[]{:S(2)}, u32[]{:S(2)}) collective-permute-start(f32[8,640]{1,0:T(8,128)} %get-tuple-element.67), channel_id=1, source_target_pairs={{8,0},{16,8},{24,16},{32,24},{40,32},{48,40},{56,48},{64,56},{72,6... | collective-permute-start | bytes 61448 | tf_op jit(solution)/shard_map/ppermute | solution.py:720
  118.2 0.6 copy-start.16
  141.4 8.6 %collective-permute-start.4 = (bf16[8,640,256]{2,1,0:T(8,128)(2,1)}, bf16[8,640,256]{2,1,0:T(8,128)(2,1)S(1)}, u32[]{:S(2)}, u32[]{:S(2)}) collective-permute-start(bf16[8,640,256]{2,1,0:T(8,128)(2,1)} %get-tuple-element.75), channel_id=1, source_target_pairs={{0,8},{8,0},{16,24},{24,16},{32,40},{40,32},{48,56},{56,48},{64,72... | collective-permute-start | bytes 7864328 | tf_op jit(solution)/shard_map/ppermute | solution.py:499
  141.8 61.0 %all-to-all-start.4 = ((bf16[4,2,512,512]{3,2,1,0:T(8,128)(2,1)}), bf16[4,2,512,512]{3,2,1,0:T(8,128)(2,1)}, u32[]{:S(2)}, u32[]{:S(2)}) async-start(bf16[4,2,512,512]{3,2,1,0:T(8,128)(2,1)} %get-tuple-element.68), calls=%async_computation.4 | async-start | bytes 8388608 | tf_op jit(solution)/shard_map/all_to_all | solution.py:578
  147.1 49.1 %collective-permute-start.3 = (bf16[4,512,512]{2,1,0:T(8,128)(2,1)}, bf16[4,512,512]{2,1,0:T(8,128)(2,1)S(1)}, u32[]{:S(2)}, u32[]{:S(2)}) collective-permute-start(bf16[4,512,512]{2,1,0:T(8,128)(2,1)} %get-tuple-element.72), channel_id=1, source_target_pairs={{0,1},{1,0},{2,3},{3,2},{4,5},{5,4},{6,7},{7,6},{8,9},{9,8},{10,11... | collective-permute-start | bytes 6291464 | tf_op jit(solution)/shard_map/ppermute | solution.py:499
  150.0 1.5 copy-start.4
  156.8 39.4 %collective-permute-start.5 = (bf16[2,640,256]{2,1,0:T(8,128)(2,1)}, bf16[2,640,256]{2,1,0:T(8,128)(2,1)S(1)}, u32[]{:S(2)}, u32[]{:S(2)}) collective-permute-start(bf16[2,640,256]{2,1,0:T(8,128)(2,1)} %get-tuple-element.76), channel_id=1, source_target_pairs={{0,16},{8,24},{16,32},{24,40},{32,48},{40,56},{48,0},{56,8},{64,80... | collective-permute-start | bytes 1966088 | tf_op jit(solution)/shard_map/ppermute | solution.py:653
  158.2 38.0 %collective-permute-start.6 = (bf16[2,640,256]{2,1,0:T(8,128)(2,1)}, bf16[2,640,256]{2,1,0:T(8,128)(2,1)S(1)}, u32[]{:S(2)}, u32[]{:S(2)}) collective-permute-start(bf16[2,640,256]{2,1,0:T(8,128)(2,1)} %get-tuple-element.77), channel_id=1, source_target_pairs={{0,32},{8,40},{16,48},{24,56},{32,0},{40,8},{48,16},{56,24},{64,96... | collective-permute-start | bytes 1966088 | tf_op jit(solution)/shard_map/ppermute | solution.py:653
  159.0 37.3 %collective-permute-start.7 = (bf16[2,640,256]{2,1,0:T(8,128)(2,1)}, bf16[2,640,256]{2,1,0:T(8,128)(2,1)S(1)}, u32[]{:S(2)}, u32[]{:S(2)}) collective-permute-start(bf16[2,640,256]{2,1,0:T(8,128)(2,1)} %get-tuple-element.78), channel_id=1, source_target_pairs={{0,48},{8,56},{16,0},{24,8},{32,16},{40,24},{48,32},{56,40},{64,11... | collective-permute-start | bytes 1966088 | tf_op jit(solution)/shard_map/ppermute | solution.py:653
  196.2 1.3 copy-start.5
  196.2 1.5 copy-start.1
  196.2 1.7 copy-start.2
  196.2 1.9 copy-start.3
  202.8 36.3 %all-to-all-start.5 = ((bf16[4,512,512]{2,1,0:T(8,128)(2,1)}), bf16[4,512,512]{2,1,0:T(8,128)(2,1)S(1)}, u32[]{:S(2)}, u32[]{:S(2)}) async-start(bf16[4,512,512]{2,1,0:T(8,128)(2,1)} %shard_map.216), calls=%async_computation.5 | async-start | bytes 4194304 | tf_op jit(solution)/shard_map/all_to_all | solution.py:578
  212.4 26.7 %collective-permute-start.2 = (bf16[512,512]{1,0:T(8,128)(2,1)}, bf16[512,512]{1,0:T(8,128)(2,1)S(1)}, u32[]{:S(2)}, u32[]{:S(2)}) collective-permute-start(bf16[512,512]{1,0:T(8,128)(2,1)} %get-tuple-element.70), channel_id=1, source_target_pairs={{0,1},{1,0},{2,3},{3,2},{4,5},{5,4},{6,7},{7,6},{8,9},{9,8},{10,11... | collective-permute-start | bytes 1572872 | tf_op jit(solution)/shard_map/ppermute | solution.py:499
  219.5 15.1 %collective-permute-start.8 = (bf16[640,256]{1,0:T(8,128)(2,1)}, bf16[640,256]{1,0:T(8,128)(2,1)S(1)}, u32[]{:S(2)}, u32[]{:S(2)}) collective-permute-start(bf16[640,256]{1,0:T(8,128)(2,1)} %get-tuple-element.81), channel_id=1, source_target_pairs={{0,64},{8,72},{16,80},{24,88},{32,96},{40,104},{48,112},{56,120},{... | collective-permute-start | bytes 983048 | tf_op jit(solution)/shard_map/ppermute | solution.py:499
  234.6 0.7 copy-start.11
  239.1 0.8 copy-start.9
  239.1 1.5 copy-start

commit v7 on v6

--- a/solution.py
+++ b/solution.py
@@ -118,21 +118,39 @@
 
 
 def end_kernel(x_ref, wq_ref, wk_ref, wv_ref, o_ref, tail_ref, wqk_ref):
+    step = pl.program_id(0)
     wqk_ref[0:64] = wq_ref[...]
     wqk_ref[64:128] = wk_ref[...]
     x = x_ref[...]
-    o_ref[:, :128] = nt(x, wqk_ref[...])
-    o_ref[:, 128:] = nn(x, wv_ref[...])
+    qk, v = nt(x, wqk_ref[...]), nn(x, wv_ref[...])
+
+    @pl.when(step == 0)
+    def _():
+        o_ref[:, :128] = qk
+        o_ref[:, 128:] = v
+
+    @pl.when(step > 0)
+    def _():
+        o_ref[:, :128] += qk
+        o_ref[:, 128:] += v
+
     tail_ref[...] = o_ref[CHUNK - 8 :]
 
 
 def project_end(x, wq_t, wk_t, wv):
     depth = x.shape[1]
+    part = depth // 4
+    at = lambda k: (0, k)
     return call(
         end_kernel,
-        (1,),
-        [pl.BlockSpec((CHUNK, depth), lambda c: (CHUNKS - 1, 0)), full(64, depth), full(64, depth), full(depth, 512)],
-        [full(CHUNK, 640), full(8, 640), full(128, depth)],
+        (4,),
+        [
+            pl.BlockSpec((CHUNK, part), lambda k: (CHUNKS - 1, k)),
+            pl.BlockSpec((64, part), at),
+            pl.BlockSpec((64, part), at),
+            pl.BlockSpec((part, 512), lambda k: (k, 0)),
+        ],
+        [full(CHUNK, 640), full(8, 640), pl.BlockSpec((128, part), at)],
         [arr((CHUNK, 640)), arr((8, 640)), arr((128, depth), BF16)],
         (x, wq_t, wk_t, wv),
         flops=2 * CHUNK * depth * 640,
@@ -701,7 +719,7 @@
     return keep, flip(send, "seq", 8)
 
 
-def finish_weight_grad(keep, came):
+def finish_weight_grad(keep, came, before):
     width = keep.shape[1]
     one = pl.BlockSpec((128, width), lambda i: (i, 0))
     return call(
@@ -712,6 +730,7 @@
         [arr((64, width)), arr((64, width)), arr((width, 512))],
         (keep, came),
         moved=2e6,
+        after=(before,),
     )
 
 
@@ -749,7 +768,7 @@
     parts = [mine, *(to_x(part, dx) for dx, part in enumerate(rest, 1))]
     own, came = reduce_weight_grad(parts)
     input_grad = reduce_input_grad(side_y, by_z, keep, send, parts[1:], ())
-    grad_query, grad_key, grad_value = finish_weight_grad(own, came)
+    grad_query, grad_key, grad_value = finish_weight_grad(own, came, input_grad)
     return (outputs, input_grad, grad_query.T, grad_key.T, grad_value)
 
 

time: 249 us -> 249 us (level)
    ppermute x4, waiting for transfers between devices: 48.7 us -> 43 us  [flip(): lax.ppermute(x, axis, [(i, i ^ bit) for i in range(lax.axis_size(axis))])]
    all_to_all x2, waiting for transfers between devices: 0.01 us -> 4.91 us  [along_z(): lax.all_to_all(x, 'tp', 0, 0, axis_index_groups=[[0, 2, 4, 6], [1, 3, 5,...]
  transfers between devices with their start and end apart: 15 -> 15, of which waited for: 2 -> 3; matrix products, arithmetic and copies ran while one was open for 1% -> 1% of each run, Pallas kernels for 30% -> 30%
where the time goes in v7:
time: 249 us; the launch traced here: 244 us
  Pallas kernels  134 us (54%)
  starting transfers between devices  50.5 us (20%)
  waiting for transfers between devices  47.9 us (19%)
  local copies, waits for them, and re-layouts  10.2 us (4%)
    pallas_call x20, Pallas kernels, call(): pl.pallas_call(body, grid_spec=pltpu.PrefetchScalarGridSpec(num_scalar_pr...  134 us
    ppermute x4, waiting for transfers between devices, flip(): lax.ppermute(x, axis, [(i, i ^ bit) for i in range(lax.axis_size(axis))])  43 us
    all_to_all x2, starting transfers between devices, carried_in(): pieces = lax.all_to_all(state.reshape(count, rows, HDIM), 'seq', 0, 0)  12.5 us
    all_to_all x2, starting transfers between devices, carried_in(): return lax.all_to_all(sums, 'seq', 0, 0).reshape(HEADS, NF, HDIM)  11.4 us
    all_to_all x2, starting transfers between devices, along_z(): lax.all_to_all(x, 'tp', 0, 0, axis_index_groups=[[0, 2, 4, 6], [1, 3, 5,...  10.6 us
    unnamed x34, local copies, waits for them, and re-layouts  9.61 us
    ppermute x4, starting transfers between devices, flip(): lax.ppermute(x, axis, [(i, i ^ bit) for i in range(lax.axis_size(axis))])  7.3 us
  transfers between devices with their start and end apart: 15, of which 3 were waited for; matrix products, arithmetic and copies ran while one was open for 1% of the time, Pallas kernels for 30%

profile of v7, /device:TPU:2, one launch (start us, length us, event | category | flops | bytes accessed | tf_op | source)
XLA Modules:
  0.0 244.0 jit_solution(16340478864873471576)
XLA Ops:
  0.6 6.1 %shard_map.200 = (f32[256,640]{1,0:T(8,128)}, f32[8,640]{1,0:T(8,128)}, bf16[128,4096]{1,0:T(8,128)(2,1)}) custom-call(bf16[1024,4096]{1,0:T(8,128)(2,1)} %y_ref.1, bf16[64,4096]{1,0:T(8,128)(2,1)} %bitcast.21, bf16[64,4096]{1,0:T(8,128)(2,1)} %bitcast.22, bf16[4096,512]{1,0:T(8,128)(2,1)} %wv_ref.5), custom_call_target="tpu_custom_call" | custom-call | flops 1342177280 | bytes 8000000 | tf_op jit(solution)/shard_map/pallas_call | solution.py:101
  6.8 1.9 collective-permute-start
  8.7 0.0 copy-start.12
  8.7 0.0 copy-start.13
  8.7 0.0 copy-start.14
  8.7 9.4 %shard_map.201.a_ref.before_ref = f32[768,640]{1,0:T(8,128)} custom-call(bf16[1024,4096]{1,0:T(8,128)(2,1)} %y_ref.1, bf16[128,4096]{1,0:T(8,128)(2,1)} %get-tuple-element.45.wqk_ref, bf16[4096,512]{1,0:T(8,128)(2,1)} %wv_ref.5), custom_call_target="tpu_custom_call" | custom-call | flops 4026531840 | bytes 12000000 | tf_op jit(solution)/shard_map/pallas_call | solution.py:101
  18.1 0.7 pad_maximum_fusion.taps_ref.t_ref
  18.8 0.6 stack.39.dest_ref
  19.4 0.0 collective-permute-done.tail_ref
  19.4 0.6 copy-done.15
  20.1 7.9 %shard_map.202 = (bf16[1024,256]{1,0:T(8,128)(2,1)}, bf16[1024,256]{1,0:T(8,128)(2,1)}, bf16[1024,512]{1,0:T(8,128)(2,1)}, bf16[1024,512]{1,0:T(8,128)(2,1)}, f3...) custom-call(f32[768,640]{1,0:T(8,128)} %shard_map.201.a_ref.before_ref, f32[256,640]{1,0:T(8,128)} %get-tuple-element.46.b_ref, ...), custom_call_target="tpu_custom_call" | custom-call | flops 4000000000 | bytes 15000000 | tf_op jit(solution)/shard_map/pallas_call | solution.py:101
  28.0 6.8 %all-to-all-start = ((f32[16,40,128]{2,1,0:T(8,128)}), f32[16,40,128]{2,1,0:T(8,128)S(1)}, u32[]{:S(2)}, u32[]{:S(2)}) async-start(f32[16,40,128]{2,1,0:T(8,128)} %bitcast.26), calls=%async_computation | async-start | bytes 655360 | tf_op jit(solution)/shard_map/all_to_all | solution.py:277
  34.7 6.3 %shard_map.204.num_ref = f32[1024,512]{1,0:T(8,128)} custom-call(bf16[1024,256]{1,0:T(8,128)(2,1)} %get-tuple-element.48.ql_ref, bf16[1024,256]{1,0:T(8,128)(2,1)} %get-tuple-element.53.kr_ref, bf16[1024,512]{1,0:T(8,128)(2,1)} %get-tuple-element.54.vh_ref, bf16[1024,512]{1,0:T(8,128)(2,1)} %get-tuple-element.55.vl_ref), custom_call_target="tpu_custom_call" | custom-call | flops 6000000000 | bytes 6000000 | tf_op jit(solution)/shard_map/pallas_call | solution.py:101
  41.0 0.0 all-to-all-done.x_ref
  41.1 0.7 copy-done.8
  41.8 1.7 shard_map.205
  43.5 5.7 %all-to-all-start.1 = ((f32[16,40,128]{2,1,0:T(8,128)}), f32[16,40,128]{2,1,0:T(8,128)S(1)}, u32[]{:S(2)}, u32[]{:S(2)}) async-start(f32[16,40,128]{2,1,0:T(8,128)} %shard_map.205), calls=%async_computation.1 | async-start | bytes 655360 | tf_op jit(solution)/shard_map/all_to_all | solution.py:282
  49.2 6.7 %shard_map.203 = (bf16[1024,1024]{1,0:T(8,128)(2,1)}, bf16[1024,1024]{1,0:T(8,128)(2,1)}, bf16[4,160,1024]{2,1,0:T(8,128)(2,1)}, bf16[4,160,1024]{2,1,0:T(8,128)(2,1)}) custom-call(bf16[1024,256]{1,0:T(8,128)(2,1)} %get-tuple-element.48.ql_ref, bf16[4,256,512]{2,1,0:T(8,128)(2,1)} %constant.99.clone.pick_ref, ...), custom_call_target="tpu_custom_call" | custom-call | flops 4000000000 | bytes 10000000 | tf_op jit(solution)/shard_map/pallas_call | solution.py:101
  55.9 0.0 all-to-all-done.1
  55.9 0.7 copy-done.11
  56.6 11.1 %shard_map.206 = (f32[1024,512]{1,0:T(8,128)}, bf16[1024,512]{1,0:T(8,128)(2,1)}, bf16[1024,512]{1,0:T(8,128)(2,1)}, f32[4,4,160,128]{3,2,1,0:T(8,128)}, f32[4,160,128]{2,1,0:T(8,128)}) custom-call(bf16[1024,1024]{1,0:T(8,128)(2,1)} %get-tuple-element.49.ph_ref, bf16[1024,1024]{1,0:T(8,128)(2,1)} %get-tuple-element.50.pl_ref, ...), custom_call_target="tpu_custom_call" | custom-call | flops 5000000000 | bytes 18000000 | tf_op jit(solution)/shard_map/pallas_call | solution.py:101
  67.8 5.7 %all-to-all-start.2 = ((f32[16,40,128]{2,1,0:T(8,128)}), f32[16,40,128]{2,1,0:T(8,128)S(1)}, u32[]{:S(2)}, u32[]{:S(2)}) async-start(f32[16,40,128]{2,1,0:T(8,128)} %bitcast.25), calls=%async_computation.2 | async-start | bytes 655360 | tf_op jit(solution)/shard_map/all_to_all | solution.py:277
  73.5 8.1 %shard_map.209 = (f32[1024,128]{1,0:T(8,128)}, f32[1024,512]{1,0:T(8,128)}) custom-call(bf16[1024,256]{1,0:T(8,128)(2,1)} %get-tuple-element.48.ql_ref, bf16[1024,256]{1,0:T(8,128)(2,1)} %get-tuple-element.53.kr_ref, bf16[1024,512]{1,0:T(8,128)(2,1)} %get-tuple-element.54.vh_ref, bf16[1024,512]{1,0:T(8,128)(2,1)} %get-tuple-element.55.vl_ref, ...), custom_call_target="tpu_custom_call" | custom-call | flops 8000000000 | bytes 8000000 | tf_op jit(solution)/shard_map/pallas_call | solution.py:101
  81.6 0.0 all-to-all-done.2.x_ref
  81.6 0.7 copy-done.7
  82.3 1.8 shard_map.207
  84.1 5.7 %all-to-all-start.3 = ((f32[16,40,128]{2,1,0:T(8,128)}), f32[16,40,128]{2,1,0:T(8,128)S(1)}, u32[]{:S(2)}, u32[]{:S(2)}) async-start(f32[16,40,128]{2,1,0:T(8,128)} %shard_map.207), calls=%async_computation.3 | async-start | bytes 655360 | tf_op jit(solution)/shard_map/all_to_all | solution.py:282
  89.8 12.6 %shard_map.208.gq_ref = f32[1024,128]{1,0:T(8,128)} custom-call(bf16[1024,256]{1,0:T(8,128)(2,1)} %get-tuple-element.48.ql_ref, bf16[1024,256]{1,0:T(8,128)(2,1)} %get-tuple-element.53.kr_ref, bf16[1024,512]{1,0:T(8,128)(2,1)} %get-tuple-element.54.vh_ref, bf16[1024,512]{1,0:T(8,128)(2,1)} %get-tuple-element.55.vl_ref, ...), custom_call_target="tpu_custom_call" | custom-call | flops 8000000000 | bytes 8000000 | tf_op jit(solution)/shard_map/pallas_call | solution.py:101
  102.4 0.0 all-to-all-done.3
  102.4 0.0 copy-start.6
  102.4 0.7 copy-done.6
  103.1 4.7 %shard_map.210 = (f32[256,640]{1,0:T(8,128)}, f32[8,640]{1,0:T(8,128)}) custom-call(bf16[1024,256]{1,0:T(8,128)(2,1)} %get-tuple-element.53.kr_ref, bf16[1024,512]{1,0:T(8,128)(2,1)} %get-tuple-element.54.vh_ref, bf16[1024,512]{1,0:T(8,128)(2,1)} %get-tuple-element.55.vl_ref, f32[4,4,160,128]{3,2,1,0:T(8,128)} %get-tuple-element.59.gs_ref, ...), custom_call_target="tpu_custom_call" | custom-call | flops 2000000000 | bytes 3000000 | tf_op jit(solution)/shard_map/pallas_call | solution.py:101
  107.9 2.0 collective-permute-start.1
  109.9 8.3 %shard_map.211 = (f32[768,640]{1,0:T(8,128)}, f32[8,640]{1,0:T(8,128)}) custom-call(bf16[1024,256]{1,0:T(8,128)(2,1)} %get-tuple-element.53.kr_ref, bf16[1024,512]{1,0:T(8,128)(2,1)} %get-tuple-element.54.vh_ref, bf16[1024,512]{1,0:T(8,128)(2,1)} %get-tuple-element.55.vl_ref, f32[4,4,160,128]{3,2,1,0:T(8,128)} %get-tuple-element.59.gs_ref, ...), custom_call_target="tpu_custom_call" | custom-call | flops 6000000000 | bytes 9000000 | tf_op jit(solution)/shard_map/pallas_call | solution.py:101
  118.2 0.0 copy-start.16
  118.2 0.6 copy-done.16
  118.8 12.1 %shard_map.212 = (bf16[4,2,512,512]{3,2,1,0:T(8,128)(2,1)}, f32[4,512,512]{2,1,0:T(8,128)}, bf16[4,512,512]{2,1,0:T(8,128)(2,1)}, bf16[640,1024]{1,0:T(8,128)(2,1)}) custom-call(s32[1]{0:T(128)} %bitcast.5.me_ref, f32[256,640]{1,0:T(8,128)} %get-tuple-element.65.a_ref, f32[768,640]{1,0:T(8,128)} %get-tuple-element.66.b_ref, f32[8,640]{1,0:T(8,128)} %copy-done.16, ...), custom_call_target="tpu_custom_call" | custom-call | flops 5368709120 | bytes 20000000 | tf_op jit(solution)/shard_map/pallas_call | solution.py:101
  130.8 10.5 %shard_map.214 = (bf16[8,640,256]{2,1,0:T(8,128)(2,1)}, bf16[8,640,256]{2,1,0:T(8,128)(2,1)}) custom-call(s32[9]{0:T(128)} %stack.39.dest_ref, bf16[640,1024]{1,0:T(8,128)(2,1)} %get-tuple-element.73.d_ref, bf16[1024,4096]{1,0:T(8,128)(2,1)} %y_ref.1, bf16[1024,4096]{1,0:T(8,128)(2,1)} %y_ref.1), custom_call_target="tpu_custom_call" | custom-call | flops 5368709120 | bytes 15000000 | tf_op jit(solution)/shard_map/pallas_call | solution.py:101
  141.4 0.4 collective-permute-start.4
  141.8 5.3 %all-to-all-start.4 = ((bf16[4,2,512,512]{3,2,1,0:T(8,128)(2,1)}), bf16[4,2,512,512]{3,2,1,0:T(8,128)(2,1)}, u32[]{:S(2)}, u32[]{:S(2)}) async-start(bf16[4,2,512,512]{3,2,1,0:T(8,128)(2,1)} %get-tuple-element.68), calls=%async_computation.4 | async-start | bytes 8388608 | tf_op jit(solution)/shard_map/all_to_all | solution.py:596
  147.1 2.9 %collective-permute-start.3 = (bf16[4,512,512]{2,1,0:T(8,128)(2,1)}, bf16[4,512,512]{2,1,0:T(8,128)(2,1)S(1)}, u32[]{:S(2)}, u32[]{:S(2)}) collective-permute-start(bf16[4,512,512]{2,1,0:T(8,128)(2,1)} %get-tuple-element.72), channel_id=1, source_target_pairs={{0,1},{1,0},{2,3},{3,2},{4,5},{5,4},{6,7},{7,6},{8,9},{9,8},{10,11... | collective-permute-start | bytes 6291464 | tf_op jit(solution)/shard_map/ppermute | solution.py:517
  150.0 1.5 copy-done.4
  151.5 5.2 %shard_map.215 = (bf16[2,640,256]{2,1,0:T(8,128)(2,1)}, bf16[2,640,256]{2,1,0:T(8,128)(2,1)}, bf16[2,640,256]{2,1,0:T(8,128)(2,1)}, bf16[2,640,256]{2,1,0:T(8,128)(2,1)}) custom-call(bf16[8,640,256]{2,1,0:T(8,128)(2,1)} %get-tuple-element.74.mine_ref, bf16[8,640,256]{2,1,0:T(8,128)(2,1)} %copy-done.4), custom_call_target="tpu_custom_call" | custom-call | bytes 8000000 | tf_op jit(solution)/shard_map/pallas_call | solution.py:101
  156.8 1.5 collective-permute-start.5
  158.2 0.7 collective-permute-start.6
  158.9 2.6 %collective-permute-start.7 = (bf16[2,640,256]{2,1,0:T(8,128)(2,1)}, bf16[2,640,256]{2,1,0:T(8,128)(2,1)S(1)}, u32[]{:S(2)}, u32[]{:S(2)}) collective-permute-start(bf16[2,640,256]{2,1,0:T(8,128)(2,1)} %get-tuple-element.78), channel_id=1, source_target_pairs={{0,48},{8,56},{16,0},{24,8},{32,16},{40,24},{48,32},{56,40},{64,11... | collective-permute-start | bytes 1966088 | tf_op jit(solution)/shard_map/ppermute | solution.py:671
  161.5 34.6 %collective-permute-done.3.refs_1_ = bf16[4,512,512]{2,1,0:T(8,128)(2,1)S(1)} collective-permute-done((bf16[4,512,512]{2,1,0:T(8,128)(2,1)}, bf16[4,512,512]{2,1,0:T(8,128)(2,1)S(1)}, u32[]{:S(2)}, u32[]{:S(2)}) %collective-permute-start.3) | collective-permute-done | bytes 2097184 | tf_op jit(solution)/shard_map/ppermute | solution.py:517
  196.2 0.0 collective-permute-done.7.refs_4_.c_ref
  196.2 1.3 copy-done.5
  197.5 0.2 copy-done.1
  197.7 0.2 copy-done.2
  197.9 0.2 copy-done.3
  198.1 4.6 %shard_map.216 = bf16[4,512,512]{2,1,0:T(8,128)(2,1)} custom-call(f32[4,512,512]{2,1,0:T(8,128)} %get-tuple-element.71.refs_0_, bf16[4,512,512]{2,1,0:T(8,128)(2,1)} %copy-done.5, bf16[2,640,256]{2,1,0:T(8,128)(2,1)} %copy-done.1, bf16[2,640,256]{2,1,0:T(8,128)(2,1)} %copy-done.2, bf16[2,640,256]{2,1,0:T(8,128)(2,1)} %copy-done.3), custom_call_target="tpu_custom_call" | custom-call | bytes 8000000 | tf_op jit(solution)/shard_map/pallas_call | solution.py:101
  202.8 5.3 %all-to-all-start.5 = ((bf16[4,512,512]{2,1,0:T(8,128)(2,1)}), bf16[4,512,512]{2,1,0:T(8,128)(2,1)S(1)}, u32[]{:S(2)}, u32[]{:S(2)}) async-start(bf16[4,512,512]{2,1,0:T(8,128)(2,1)} %shard_map.216), calls=%async_computation.5 | async-start | bytes 4194304 | tf_op jit(solution)/shard_map/all_to_all | solution.py:596
  208.0 4.3 %shard_map.213 = (f32[512,512]{1,0:T(8,128)}, bf16[512,512]{1,0:T(8,128)(2,1)}) custom-call(s32[1]{0:T(128)} %bitcast.5.me_ref, bf16[4,2,512,512]{3,2,1,0:T(8,128)(2,1)} %all-to-all-done.4.p_ref), custom_call_target="tpu_custom_call" | custom-call | bytes 6000000 | tf_op jit(solution)/shard_map/pallas_call | solution.py:101
  212.3 2.9 %collective-permute-start.2 = (bf16[512,512]{1,0:T(8,128)(2,1)}, bf16[512,512]{1,0:T(8,128)(2,1)S(1)}, u32[]{:S(2)}, u32[]{:S(2)}) collective-permute-start(bf16[512,512]{1,0:T(8,128)(2,1)} %get-tuple-element.70), channel_id=1, source_target_pairs={{0,1},{1,0},{2,3},{3,2},{4,5},{5,4},{6,7},{7,6},{8,9},{9,8},{10,11... | collective-permute-start | bytes 1572872 | tf_op jit(solution)/shard_map/ppermute | solution.py:517
  215.2 4.3 %shard_map.218 = (f32[640,256]{1,0:T(8,128)}, bf16[640,256]{1,0:T(8,128)(2,1)}) custom-call(bf16[2,640,256]{2,1,0:T(8,128)(2,1)} %get-tuple-element.79.mine_ref, bf16[2,640,256]{2,1,0:T(8,128)(2,1)} %copy-done.1, bf16[2,640,256]{2,1,0:T(8,128)(2,1)} %copy-done.2, bf16[2,640,256]{2,1,0:T(8,128)(2,1)} %copy-done.3), custom_call_target="tpu_custom_call" | custom-call | bytes 4000000 | tf_op jit(solution)/shard_map/pallas_call | solution.py:101
  219.5 1.1 collective-permute-start.8
  220.5 8.3 %collective-permute-done.2.came_ref = bf16[512,512]{1,0:T(8,128)(2,1)S(1)} collective-permute-done((bf16[512,512]{1,0:T(8,128)(2,1)}, bf16[512,512]{1,0:T(8,128)(2,1)S(1)}, u32[]{:S(2)}, u32[]{:S(2)}) %collective-permute-start.2) | collective-permute-done | bytes 524320 | tf_op jit(solution)/shard_map/ppermute | solution.py:517
  228.9 4.9 %all-to-all-done.5.p_ref = bf16[4,512,512]{2,1,0:T(8,128)(2,1)S(1)} async-done(((bf16[4,512,512]{2,1,0:T(8,128)(2,1)}), bf16[4,512,512]{2,1,0:T(8,128)(2,1)S(1)}, u32[]{:S(2)}, u32[]{:S(2)}) %all-to-all-start.5) | async-done | bytes 2097184 | tf_op jit(solution)/shard_map/all_to_all | solution.py:596
  233.8 1.3 copy-done
  235.1 4.4 %shard_map.217.refs_2_ = bf16[1024,512]{1,0:T(8,128)(2,1)} custom-call(f32[512,512]{1,0:T(8,128)} %get-tuple-element.69.keep_ref, bf16[512,512]{1,0:T(8,128)(2,1)} %copy-done.9, bf16[4,512,512]{2,1,0:T(8,128)(2,1)} %copy-done), custom_call_target="tpu_custom_call" | custom-call | bytes 5000000 | tf_op jit(solution)/shard_map/pallas_call | solution.py:101
  239.5 0.7 copy-done.10
  240.2 3.8 %shard_map.219 = (f32[64,256]{1,0:T(8,128)}, f32[64,256]{1,0:T(8,128)}, f32[256,512]{1,0:T(8,128)}) custom-call(f32[640,256]{1,0:T(8,128)} %get-tuple-element.80.refs_0_, bf16[640,256]{1,0:T(8,128)(2,1)} %copy-done.10, bf16[1024,512]{1,0:T(8,128)(2,1)} %shard_map.217.refs_2_), custom_call_target="tpu_custom_call" | custom-call | bytes 2000000 | tf_op jit(solution)/shard_map/pallas_call | solution.py:101
  (22 shorter events, 0.0 us)
Async XLA Ops:
  6.8 12.7 %collective-permute-start = (f32[8,640]{1,0:T(8,128)}, f32[8,640]{1,0:T(8,128)S(1)}, u32[]{:S(2)}, u32[]{:S(2)}) collective-permute-start(f32[8,640]{1,0:T(8,128)} %get-tuple-element.47), channel_id=1, source_target_pairs={{0,8},{8,16},{16,24},{24,32},{32,40},{40,48},{48,56},{56,64},{64,7... | collective-permute-start | bytes 61448 | tf_op jit(solution)/shard_map/ppermute | solution.py:739
  8.7 9.5 %copy-start.12 = (f32[3,512]{1,0:T(4,128)S(1)}, f32[3,512]{1,0:T(4,128)}, u32[]{:S(2)}) copy-start(f32[3,512]{1,0:T(4,128)} %param.23) | copy-start | bytes 18436
  8.7 9.4 %copy-start.13 = (f32[3,64]{1,0:T(4,128)S(1)}, f32[3,64]{1,0:T(4,128)}, u32[]{:S(2)}) copy-start(f32[3,64]{1,0:T(4,128)} %param.22) | copy-start | bytes 2308
  8.7 9.4 %copy-start.14 = (f32[3,64]{1,0:T(4,128)S(1)}, f32[3,64]{1,0:T(4,128)}, u32[]{:S(2)}) copy-start(f32[3,64]{1,0:T(4,128)} %param.21) | copy-start | bytes 2308
  19.4 0.6 copy-start.15
  28.0 13.1 %all-to-all-start = ((f32[16,40,128]{2,1,0:T(8,128)}), f32[16,40,128]{2,1,0:T(8,128)S(1)}, u32[]{:S(2)}, u32[]{:S(2)}) async-start(f32[16,40,128]{2,1,0:T(8,128)} %bitcast.26), calls=%async_computation | async-start | bytes 655360 | tf_op jit(solution)/shard_map/all_to_all | solution.py:277
  41.0 0.7 copy-start.8
  43.5 12.4 %all-to-all-start.1 = ((f32[16,40,128]{2,1,0:T(8,128)}), f32[16,40,128]{2,1,0:T(8,128)S(1)}, u32[]{:S(2)}, u32[]{:S(2)}) async-start(f32[16,40,128]{2,1,0:T(8,128)} %shard_map.205), calls=%async_computation.1 | async-start | bytes 655360 | tf_op jit(solution)/shard_map/all_to_all | solution.py:282
  55.9 0.7 copy-start.11
  67.8 13.8 %all-to-all-start.2 = ((f32[16,40,128]{2,1,0:T(8,128)}), f32[16,40,128]{2,1,0:T(8,128)S(1)}, u32[]{:S(2)}, u32[]{:S(2)}) async-start(f32[16,40,128]{2,1,0:T(8,128)} %bitcast.25), calls=%async_computation.2 | async-start | bytes 655360 | tf_op jit(solution)/shard_map/all_to_all | solution.py:277
  81.6 0.7 copy-start.7
  84.1 18.3 %all-to-all-start.3 = ((f32[16,40,128]{2,1,0:T(8,128)}), f32[16,40,128]{2,1,0:T(8,128)S(1)}, u32[]{:S(2)}, u32[]{:S(2)}) async-start(f32[16,40,128]{2,1,0:T(8,128)} %shard_map.207), calls=%async_computation.3 | async-start | bytes 655360 | tf_op jit(solution)/shard_map/all_to_all | solution.py:282
  102.4 0.7 copy-start.6
  107.9 10.3 %collective-permute-start.1 = (f32[8,640]{1,0:T(8,128)}, f32[8,640]{1,0:T(8,128)S(1)}, u32[]{:S(2)}, u32[]{:S(2)}) collective-permute-start(f32[8,640]{1,0:T(8,128)} %get-tuple-element.67), channel_id=1, source_target_pairs={{8,0},{16,8},{24,16},{32,24},{40,32},{48,40},{56,48},{64,56},{72,6... | collective-permute-start | bytes 61448 | tf_op jit(solution)/shard_map/ppermute | solution.py:739
  118.2 0.6 copy-start.16
  141.4 8.6 %collective-permute-start.4 = (bf16[8,640,256]{2,1,0:T(8,128)(2,1)}, bf16[8,640,256]{2,1,0:T(8,128)(2,1)S(1)}, u32[]{:S(2)}, u32[]{:S(2)}) collective-permute-start(bf16[8,640,256]{2,1,0:T(8,128)(2,1)} %get-tuple-element.75), channel_id=1, source_target_pairs={{0,8},{8,0},{16,24},{24,16},{32,40},{40,32},{48,56},{56,48},{64,72... | collective-permute-start | bytes 7864328 | tf_op jit(solution)/shard_map/ppermute | solution.py:517
  141.8 61.0 %all-to-all-start.4 = ((bf16[4,2,512,512]{3,2,1,0:T(8,128)(2,1)}), bf16[4,2,512,512]{3,2,1,0:T(8,128)(2,1)}, u32[]{:S(2)}, u32[]{:S(2)}) async-start(bf16[4,2,512,512]{3,2,1,0:T(8,128)(2,1)} %get-tuple-element.68), calls=%async_computation.4 | async-start | bytes 8388608 | tf_op jit(solution)/shard_map/all_to_all | solution.py:596
  147.1 49.1 %collective-permute-start.3 = (bf16[4,512,512]{2,1,0:T(8,128)(2,1)}, bf16[4,512,512]{2,1,0:T(8,128)(2,1)S(1)}, u32[]{:S(2)}, u32[]{:S(2)}) collective-permute-start(bf16[4,512,512]{2,1,0:T(8,128)(2,1)} %get-tuple-element.72), channel_id=1, source_target_pairs={{0,1},{1,0},{2,3},{3,2},{4,5},{5,4},{6,7},{7,6},{8,9},{9,8},{10,11... | collective-permute-start | bytes 6291464 | tf_op jit(solution)/shard_map/ppermute | solution.py:517
  150.0 1.5 copy-start.4
  156.8 39.4 %collective-permute-start.5 = (bf16[2,640,256]{2,1,0:T(8,128)(2,1)}, bf16[2,640,256]{2,1,0:T(8,128)(2,1)S(1)}, u32[]{:S(2)}, u32[]{:S(2)}) collective-permute-start(bf16[2,640,256]{2,1,0:T(8,128)(2,1)} %get-tuple-element.76), channel_id=1, source_target_pairs={{0,16},{8,24},{16,32},{24,40},{32,48},{40,56},{48,0},{56,8},{64,80... | collective-permute-start | bytes 1966088 | tf_op jit(solution)/shard_map/ppermute | solution.py:671
  158.2 38.0 %collective-permute-start.6 = (bf16[2,640,256]{2,1,0:T(8,128)(2,1)}, bf16[2,640,256]{2,1,0:T(8,128)(2,1)S(1)}, u32[]{:S(2)}, u32[]{:S(2)}) collective-permute-start(bf16[2,640,256]{2,1,0:T(8,128)(2,1)} %get-tuple-element.77), channel_id=1, source_target_pairs={{0,32},{8,40},{16,48},{24,56},{32,0},{40,8},{48,16},{56,24},{64,96... | collective-permute-start | bytes 1966088 | tf_op jit(solution)/shard_map/ppermute | solution.py:671
  158.9 37.3 %collective-permute-start.7 = (bf16[2,640,256]{2,1,0:T(8,128)(2,1)}, bf16[2,640,256]{2,1,0:T(8,128)(2,1)S(1)}, u32[]{:S(2)}, u32[]{:S(2)}) collective-permute-start(bf16[2,640,256]{2,1,0:T(8,128)(2,1)} %get-tuple-element.78), channel_id=1, source_target_pairs={{0,48},{8,56},{16,0},{24,8},{32,16},{40,24},{48,32},{56,40},{64,11... | collective-permute-start | bytes 1966088 | tf_op jit(solution)/shard_map/ppermute | solution.py:671
  196.2 1.3 copy-start.5
  196.2 1.5 copy-start.1
  196.2 1.7 copy-start.2
  196.2 1.9 copy-start.3
  202.8 31.0 %all-to-all-start.5 = ((bf16[4,512,512]{2,1,0:T(8,128)(2,1)}), bf16[4,512,512]{2,1,0:T(8,128)(2,1)S(1)}, u32[]{:S(2)}, u32[]{:S(2)}) async-start(bf16[4,512,512]{2,1,0:T(8,128)(2,1)} %shard_map.216), calls=%async_computation.5 | async-start | bytes 4194304 | tf_op jit(solution)/shard_map/all_to_all | solution.py:596
  212.3 16.6 %collective-permute-start.2 = (bf16[512,512]{1,0:T(8,128)(2,1)}, bf16[512,512]{1,0:T(8,128)(2,1)S(1)}, u32[]{:S(2)}, u32[]{:S(2)}) collective-permute-start(bf16[512,512]{1,0:T(8,128)(2,1)} %get-tuple-element.70), channel_id=1, source_target_pairs={{0,1},{1,0},{2,3},{3,2},{4,5},{5,4},{6,7},{7,6},{8,9},{9,8},{10,11... | collective-permute-start | bytes 1572872 | tf_op jit(solution)/shard_map/ppermute | solution.py:517
  219.5 20.0 %collective-permute-start.8 = (bf16[640,256]{1,0:T(8,128)(2,1)}, bf16[640,256]{1,0:T(8,128)(2,1)S(1)}, u32[]{:S(2)}, u32[]{:S(2)}) collective-permute-start(bf16[640,256]{1,0:T(8,128)(2,1)} %get-tuple-element.81), channel_id=1, source_target_pairs={{0,64},{8,72},{16,80},{24,88},{32,96},{40,104},{48,112},{56,120},{... | collective-permute-start | bytes 983048 | tf_op jit(solution)/shard_map/ppermute | solution.py:517
  228.9 4.9 %copy-start.9 = (bf16[512,512]{1,0:T(8,128)(2,1)}, bf16[512,512]{1,0:T(8,128)(2,1)S(1)}, u32[]{:S(2)}) copy-start(bf16[512,512]{1,0:T(8,128)(2,1)S(1)} %collective-permute-done.2.came_ref) | copy-start | bytes 1572868
  233.8 1.3 copy-start
  239.5 0.7 copy-start.10

commit v8 on v7

--- a/solution.py
+++ b/solution.py
@@ -596,12 +596,12 @@
     return lax.all_to_all(x, "tp", 0, 0, axis_index_groups=[[0, 2, 4, 6], [1, 3, 5, 7]])
 
 
-def reduce_input_grad(side_y, by_z, keep, send, first, second):
+def reduce_input_grad(side_y, by_z, keep, send, first, last):
     half, tile = LEN // 2, LEN // 4
     came = flip(send, "tp", 1)
     tops = along_z(by_z)
     block = pl.BlockSpec((1, half, 512), lambda i: (i, 0, 0))
-    pairs = call(pair_kernel, (4,), [block, block], block, arr((4, half, 512), BF16), (keep, came), moved=8e6, after=first)
+    mine = keep
     rows = pl.BlockSpec((tile // 2, 512), lambda i, me: (i, 0))
     keep, send = call(
         top_kernel,
@@ -611,8 +611,17 @@
         [arr((half, 512)), arr((half, 512), BF16)],
         (side_y, tops),
         prefetch=1,
-        after=second,
         moved=6e6,
+    )
+    pairs = call(
+        pair_kernel,
+        (4,),
+        [block, block],
+        block,
+        arr((4, half, 512), BF16),
+        (mine, came),
+        moved=8e6,
+        after=(*first, send),
     )
     pairs = along_z(pairs)
     came = flip(send, "tp", 1)
@@ -625,6 +634,7 @@
         arr((LEN, 512), BF16),
         (keep, came, pairs),
         moved=5e6,
+        after=last,
     )
 
 
@@ -719,7 +729,7 @@
     return keep, flip(send, "seq", 8)
 
 
-def finish_weight_grad(keep, came, before):
+def finish_weight_grad(keep, came):
     width = keep.shape[1]
     one = pl.BlockSpec((128, width), lambda i: (i, 0))
     return call(
@@ -730,7 +740,6 @@
         [arr((64, width)), arr((64, width)), arr((width, 512))],
         (keep, came),
         moved=2e6,
-        after=(before,),
     )
 
 
@@ -767,8 +776,8 @@
     mine, *rest = weight_parts(dt, inputs)
     parts = [mine, *(to_x(part, dx) for dx, part in enumerate(rest, 1))]
     own, came = reduce_weight_grad(parts)
-    input_grad = reduce_input_grad(side_y, by_z, keep, send, parts[1:], ())
-    grad_query, grad_key, grad_value = finish_weight_grad(own, came, input_grad)
+    grad_query, grad_key, grad_value = finish_weight_grad(own, came)
+    input_grad = reduce_input_grad(side_y, by_z, keep, send, parts[1:], (grad_query,))
     return (outputs, input_grad, grad_query.T, grad_key.T, grad_value)
 
 

time: 249 us -> 248 us (level)
    all_to_all x2, waiting for transfers between devices: 4.91 us -> 35.3 us  [along_z(): lax.all_to_all(x, 'tp', 0, 0, axis_index_groups=[[0, 2, 4, 6], [1, 3, 5,...]
    ppermute x4, waiting for transfers between devices: 43 us -> 14 us  [flip(): lax.ppermute(x, axis, [(i, i ^ bit) for i in range(lax.axis_size(axis))])]
  transfers between devices with their start and end apart: 15 -> 15, of which waited for: 3 -> 2; matrix products, arithmetic and copies ran while one was open for 1% -> 1% of each run, Pallas kernels for 30% -> 28%
where the time goes in v8:
time: 248 us; the launch traced here: 244 us
  Pallas kernels  134 us (54%)
  waiting for transfers between devices  49.4 us (20%)
  starting transfers between devices  49.1 us (20%)
  local copies, waits for them, and re-layouts  9.74 us (4%)
    pallas_call x20, Pallas kernels, call(): pl.pallas_call(body, grid_spec=pltpu.PrefetchScalarGridSpec(num_scalar_pr...  134 us
    all_to_all x2, waiting for transfers between devices, along_z(): lax.all_to_all(x, 'tp', 0, 0, axis_index_groups=[[0, 2, 4, 6], [1, 3, 5,...  35.3 us
    ppermute x4, waiting for transfers between devices, flip(): lax.ppermute(x, axis, [(i, i ^ bit) for i in range(lax.axis_size(axis))])  14 us
    all_to_all x2, starting transfers between devices, carried_in(): pieces = lax.all_to_all(state.reshape(count, rows, HDIM), 'seq', 0, 0)  12.5 us
    all_to_all x2, starting transfers between devices, carried_in(): return lax.all_to_all(sums, 'seq', 0, 0).reshape(HEADS, NF, HDIM)  11.4 us
    unnamed x34, local copies, waits for them, and re-layouts  9.12 us
    all_to_all x2, starting transfers between devices, along_z(): lax.all_to_all(x, 'tp', 0, 0, axis_index_groups=[[0, 2, 4, 6], [1, 3, 5,...  9.05 us
    ppermute x4, starting transfers between devices, flip(): lax.ppermute(x, axis, [(i, i ^ bit) for i in range(lax.axis_size(axis))])  7.36 us
  transfers between devices with their start and end apart: 15, of which 2 were waited for; matrix products, arithmetic and copies ran while one was open for 1% of the time, Pallas kernels for 28%

profile of v8, /device:TPU:2, one launch (start us, length us, event | category | flops | bytes accessed | tf_op | source)
XLA Modules:
  0.0 243.8 jit_solution(14692287926994442741)
XLA Ops:
  0.6 6.1 %shard_map.200 = (f32[256,640]{1,0:T(8,128)}, f32[8,640]{1,0:T(8,128)}, bf16[128,4096]{1,0:T(8,128)(2,1)}) custom-call(bf16[1024,4096]{1,0:T(8,128)(2,1)} %y_ref.1, bf16[64,4096]{1,0:T(8,128)(2,1)} %bitcast.21, bf16[64,4096]{1,0:T(8,128)(2,1)} %bitcast.22, bf16[4096,512]{1,0:T(8,128)(2,1)} %wv_ref.5), custom_call_target="tpu_custom_call" | custom-call | flops 1342177280 | bytes 8000000 | tf_op jit(solution)/shard_map/pallas_call | solution.py:101
  6.8 1.9 collective-permute-start
  8.7 0.0 copy-start.12
  8.7 0.0 copy-start.13
  8.7 0.0 copy-start.14
  8.7 9.4 %shard_map.201.a_ref.before_ref = f32[768,640]{1,0:T(8,128)} custom-call(bf16[1024,4096]{1,0:T(8,128)(2,1)} %y_ref.1, bf16[128,4096]{1,0:T(8,128)(2,1)} %get-tuple-element.45.wqk_ref, bf16[4096,512]{1,0:T(8,128)(2,1)} %wv_ref.5), custom_call_target="tpu_custom_call" | custom-call | flops 4026531840 | bytes 12000000 | tf_op jit(solution)/shard_map/pallas_call | solution.py:101
  18.1 0.7 pad_maximum_fusion.taps_ref.t_ref
  18.8 0.6 stack.39.dest_ref
  19.4 0.0 collective-permute-done.tail_ref
  19.4 0.6 copy-done.15
  20.1 7.9 %shard_map.202 = (bf16[1024,256]{1,0:T(8,128)(2,1)}, bf16[1024,256]{1,0:T(8,128)(2,1)}, bf16[1024,512]{1,0:T(8,128)(2,1)}, bf16[1024,512]{1,0:T(8,128)(2,1)}, f3...) custom-call(f32[768,640]{1,0:T(8,128)} %shard_map.201.a_ref.before_ref, f32[256,640]{1,0:T(8,128)} %get-tuple-element.46.b_ref, ...), custom_call_target="tpu_custom_call" | custom-call | flops 4000000000 | bytes 15000000 | tf_op jit(solution)/shard_map/pallas_call | solution.py:101
  28.0 6.8 %all-to-all-start = ((f32[16,40,128]{2,1,0:T(8,128)}), f32[16,40,128]{2,1,0:T(8,128)S(1)}, u32[]{:S(2)}, u32[]{:S(2)}) async-start(f32[16,40,128]{2,1,0:T(8,128)} %bitcast.26), calls=%async_computation | async-start | bytes 655360 | tf_op jit(solution)/shard_map/all_to_all | solution.py:277
  34.7 6.3 %shard_map.204.num_ref = f32[1024,512]{1,0:T(8,128)} custom-call(bf16[1024,256]{1,0:T(8,128)(2,1)} %get-tuple-element.48.ql_ref, bf16[1024,256]{1,0:T(8,128)(2,1)} %get-tuple-element.53.kr_ref, bf16[1024,512]{1,0:T(8,128)(2,1)} %get-tuple-element.54.vh_ref, bf16[1024,512]{1,0:T(8,128)(2,1)} %get-tuple-element.55.vl_ref), custom_call_target="tpu_custom_call" | custom-call | flops 6000000000 | bytes 6000000 | tf_op jit(solution)/shard_map/pallas_call | solution.py:101
  41.1 0.7 copy-done.7
  41.8 1.7 shard_map.205
  43.5 5.7 %all-to-all-start.1 = ((f32[16,40,128]{2,1,0:T(8,128)}), f32[16,40,128]{2,1,0:T(8,128)S(1)}, u32[]{:S(2)}, u32[]{:S(2)}) async-start(f32[16,40,128]{2,1,0:T(8,128)} %shard_map.205), calls=%async_computation.1 | async-start | bytes 655360 | tf_op jit(solution)/shard_map/all_to_all | solution.py:282
  49.2 6.7 %shard_map.203 = (bf16[1024,1024]{1,0:T(8,128)(2,1)}, bf16[1024,1024]{1,0:T(8,128)(2,1)}, bf16[4,160,1024]{2,1,0:T(8,128)(2,1)}, bf16[4,160,1024]{2,1,0:T(8,128)(2,1)}) custom-call(bf16[1024,256]{1,0:T(8,128)(2,1)} %get-tuple-element.48.ql_ref, bf16[4,256,512]{2,1,0:T(8,128)(2,1)} %constant.99.clone.pick_ref, ...), custom_call_target="tpu_custom_call" | custom-call | flops 4000000000 | bytes 10000000 | tf_op jit(solution)/shard_map/pallas_call | solution.py:101
  55.9 0.7 copy-done.10
  56.6 11.1 %shard_map.206 = (f32[1024,512]{1,0:T(8,128)}, bf16[1024,512]{1,0:T(8,128)(2,1)}, bf16[1024,512]{1,0:T(8,128)(2,1)}, f32[4,4,160,128]{3,2,1,0:T(8,128)}, f32[4,160,128]{2,1,0:T(8,128)}) custom-call(bf16[1024,1024]{1,0:T(8,128)(2,1)} %get-tuple-element.49.ph_ref, bf16[1024,1024]{1,0:T(8,128)(2,1)} %get-tuple-element.50.pl_ref, ...), custom_call_target="tpu_custom_call" | custom-call | flops 5000000000 | bytes 18000000 | tf_op jit(solution)/shard_map/pallas_call | solution.py:101
  67.8 5.7 %all-to-all-start.2 = ((f32[16,40,128]{2,1,0:T(8,128)}), f32[16,40,128]{2,1,0:T(8,128)S(1)}, u32[]{:S(2)}, u32[]{:S(2)}) async-start(f32[16,40,128]{2,1,0:T(8,128)} %bitcast.25), calls=%async_computation.2 | async-start | bytes 655360 | tf_op jit(solution)/shard_map/all_to_all | solution.py:277
  73.5 8.1 %shard_map.209 = (f32[1024,128]{1,0:T(8,128)}, f32[1024,512]{1,0:T(8,128)}) custom-call(bf16[1024,256]{1,0:T(8,128)(2,1)} %get-tuple-element.48.ql_ref, bf16[1024,256]{1,0:T(8,128)(2,1)} %get-tuple-element.53.kr_ref, bf16[1024,512]{1,0:T(8,128)(2,1)} %get-tuple-element.54.vh_ref, bf16[1024,512]{1,0:T(8,128)(2,1)} %get-tuple-element.55.vl_ref, ...), custom_call_target="tpu_custom_call" | custom-call | flops 8000000000 | bytes 8000000 | tf_op jit(solution)/shard_map/pallas_call | solution.py:101
  81.6 0.0 all-to-all-done.2.x_ref
  81.6 0.7 copy-done.6
  82.3 1.8 shard_map.207
  84.1 5.7 %all-to-all-start.3 = ((f32[16,40,128]{2,1,0:T(8,128)}), f32[16,40,128]{2,1,0:T(8,128)S(1)}, u32[]{:S(2)}, u32[]{:S(2)}) async-start(f32[16,40,128]{2,1,0:T(8,128)} %shard_map.207), calls=%async_computation.3 | async-start | bytes 655360 | tf_op jit(solution)/shard_map/all_to_all | solution.py:282
  89.8 12.6 %shard_map.208.gq_ref = f32[1024,128]{1,0:T(8,128)} custom-call(bf16[1024,256]{1,0:T(8,128)(2,1)} %get-tuple-element.48.ql_ref, bf16[1024,256]{1,0:T(8,128)(2,1)} %get-tuple-element.53.kr_ref, bf16[1024,512]{1,0:T(8,128)(2,1)} %get-tuple-element.54.vh_ref, bf16[1024,512]{1,0:T(8,128)(2,1)} %get-tuple-element.55.vl_ref, ...), custom_call_target="tpu_custom_call" | custom-call | flops 8000000000 | bytes 8000000 | tf_op jit(solution)/shard_map/pallas_call | solution.py:101
  102.4 0.0 all-to-all-done.3
  102.4 0.0 copy-start.5
  102.4 0.7 copy-done.5
  103.1 4.8 %shard_map.210 = (f32[256,640]{1,0:T(8,128)}, f32[8,640]{1,0:T(8,128)}) custom-call(bf16[1024,256]{1,0:T(8,128)(2,1)} %get-tuple-element.53.kr_ref, bf16[1024,512]{1,0:T(8,128)(2,1)} %get-tuple-element.54.vh_ref, bf16[1024,512]{1,0:T(8,128)(2,1)} %get-tuple-element.55.vl_ref, f32[4,4,160,128]{3,2,1,0:T(8,128)} %get-tuple-element.59.gs_ref, ...), custom_call_target="tpu_custom_call" | custom-call | flops 2000000000 | bytes 3000000 | tf_op jit(solution)/shard_map/pallas_call | solution.py:101
  107.9 2.0 collective-permute-start.1
  110.0 8.3 %shard_map.211 = (f32[768,640]{1,0:T(8,128)}, f32[8,640]{1,0:T(8,128)}) custom-call(bf16[1024,256]{1,0:T(8,128)(2,1)} %get-tuple-element.53.kr_ref, bf16[1024,512]{1,0:T(8,128)(2,1)} %get-tuple-element.54.vh_ref, bf16[1024,512]{1,0:T(8,128)(2,1)} %get-tuple-element.55.vl_ref, f32[4,4,160,128]{3,2,1,0:T(8,128)} %get-tuple-element.59.gs_ref, ...), custom_call_target="tpu_custom_call" | custom-call | flops 6000000000 | bytes 9000000 | tf_op jit(solution)/shard_map/pallas_call | solution.py:101
  118.2 0.0 copy-start.16
  118.3 0.6 copy-done.16
  118.8 12.1 %shard_map.212 = (bf16[4,2,512,512]{3,2,1,0:T(8,128)(2,1)}, f32[4,512,512]{2,1,0:T(8,128)}, bf16[4,512,512]{2,1,0:T(8,128)(2,1)}, bf16[640,1024]{1,0:T(8,128)(2,1)}) custom-call(s32[1]{0:T(128)} %bitcast.5.me_ref, f32[256,640]{1,0:T(8,128)} %get-tuple-element.65.a_ref, f32[768,640]{1,0:T(8,128)} %get-tuple-element.66.b_ref, f32[8,640]{1,0:T(8,128)} %copy-done.16, ...), custom_call_target="tpu_custom_call" | custom-call | flops 5368709120 | bytes 20000000 | tf_op jit(solution)/shard_map/pallas_call | solution.py:101
  131.0 10.5 %shard_map.214 = (bf16[8,640,256]{2,1,0:T(8,128)(2,1)}, bf16[8,640,256]{2,1,0:T(8,128)(2,1)}) custom-call(s32[9]{0:T(128)} %stack.39.dest_ref, bf16[640,1024]{1,0:T(8,128)(2,1)} %get-tuple-element.73.d_ref, bf16[1024,4096]{1,0:T(8,128)(2,1)} %y_ref.1, bf16[1024,4096]{1,0:T(8,128)(2,1)} %y_ref.1), custom_call_target="tpu_custom_call" | custom-call | flops 5368709120 | bytes 15000000 | tf_op jit(solution)/shard_map/pallas_call | solution.py:101
  141.5 0.4 collective-permute-start.4
  141.9 5.3 %all-to-all-start.4 = ((bf16[4,2,512,512]{3,2,1,0:T(8,128)(2,1)}), bf16[4,2,512,512]{3,2,1,0:T(8,128)(2,1)}, u32[]{:S(2)}, u32[]{:S(2)}) async-start(bf16[4,2,512,512]{3,2,1,0:T(8,128)(2,1)} %get-tuple-element.68), calls=%async_computation.4 | async-start | bytes 8388608 | tf_op jit(solution)/shard_map/all_to_all | solution.py:596
  147.2 2.9 %collective-permute-start.3 = (bf16[4,512,512]{2,1,0:T(8,128)(2,1)}, bf16[4,512,512]{2,1,0:T(8,128)(2,1)}, u32[]{:S(2)}, u32[]{:S(2)}) collective-permute-start(bf16[4,512,512]{2,1,0:T(8,128)(2,1)} %get-tuple-element.72), channel_id=1, source_target_pairs={{0,1},{1,0},{2,3},{3,2},{4,5},{5,4},{6,7},{7,6},{8,9},{9,8},{10,11... | collective-permute-start | bytes 6291464 | tf_op jit(solution)/shard_map/ppermute | solution.py:517
  150.1 1.5 copy-done.1
  151.6 5.3 %shard_map.215 = (bf16[2,640,256]{2,1,0:T(8,128)(2,1)}, bf16[2,640,256]{2,1,0:T(8,128)(2,1)}, bf16[2,640,256]{2,1,0:T(8,128)(2,1)}, bf16[2,640,256]{2,1,0:T(8,128)(2,1)}) custom-call(bf16[8,640,256]{2,1,0:T(8,128)(2,1)} %get-tuple-element.74.mine_ref, bf16[8,640,256]{2,1,0:T(8,128)(2,1)} %copy-done.1), custom_call_target="tpu_custom_call" | custom-call | bytes 8000000 | tf_op jit(solution)/shard_map/pallas_call | solution.py:101
  156.9 1.5 collective-permute-start.5
  158.4 0.7 collective-permute-start.6
  159.1 2.6 %collective-permute-start.7 = (bf16[2,640,256]{2,1,0:T(8,128)(2,1)}, bf16[2,640,256]{2,1,0:T(8,128)(2,1)S(1)}, u32[]{:S(2)}, u32[]{:S(2)}) collective-permute-start(bf16[2,640,256]{2,1,0:T(8,128)(2,1)} %get-tuple-element.78), channel_id=1, source_target_pairs={{0,48},{8,56},{16,0},{24,8},{32,16},{40,24},{48,32},{56,40},{64,11... | collective-permute-start | bytes 1966088 | tf_op jit(solution)/shard_map/ppermute | solution.py:681
  161.7 35.3 %all-to-all-done.4.p_ref = bf16[4,2,512,512]{3,2,1,0:T(8,128)(2,1)} async-done(((bf16[4,2,512,512]{3,2,1,0:T(8,128)(2,1)}), bf16[4,2,512,512]{3,2,1,0:T(8,128)(2,1)}, u32[]{:S(2)}, u32[]{:S(2)}) %all-to-all-start.4) | async-done | bytes 4194336 | tf_op jit(solution)/shard_map/all_to_all | solution.py:596
  197.0 4.3 %shard_map.213 = (f32[512,512]{1,0:T(8,128)}, bf16[512,512]{1,0:T(8,128)(2,1)}) custom-call(s32[1]{0:T(128)} %bitcast.5.me_ref, bf16[4,2,512,512]{3,2,1,0:T(8,128)(2,1)} %all-to-all-done.4.p_ref), custom_call_target="tpu_custom_call" | custom-call | bytes 6000000 | tf_op jit(solution)/shard_map/pallas_call | solution.py:101
  201.3 0.0 collective-permute-done.3.refs_1_
  201.3 0.0 collective-permute-done.5.refs_2_.a_ref
  201.3 0.0 collective-permute-done.6.refs_3_.b_ref
  201.4 0.9 copy-done.2
  202.3 0.2 copy-done.3
  202.5 0.2 copy-done.4
  202.7 4.6 %shard_map.216 = bf16[4,512,512]{2,1,0:T(8,128)(2,1)} custom-call(f32[4,512,512]{2,1,0:T(8,128)} %get-tuple-element.71.refs_0_, bf16[4,512,512]{2,1,0:T(8,128)(2,1)} %collective-permute-done.3.refs_1_, bf16[2,640,256]{2,1,0:T(8,128)(2,1)} %copy-done.2, bf16[2,640,256]{2,1,0:T(8,128)(2,1)} %copy-done.3, bf16[2,640,256]{2,1,0:T(8,128)(2,1)} %copy-done.4, ...), custom_call_target="tpu_custom_call" | custom-call | bytes 8000000 | tf_op jit(solution)/shard_map/pallas_call | solution.py:101
  207.3 3.7 %all-to-all-start.5 = ((bf16[4,512,512]{2,1,0:T(8,128)(2,1)}), bf16[4,512,512]{2,1,0:T(8,128)(2,1)S(1)}, u32[]{:S(2)}, u32[]{:S(2)}) async-start(bf16[4,512,512]{2,1,0:T(8,128)(2,1)} %shard_map.216), calls=%async_computation.5 | async-start | bytes 4194304 | tf_op jit(solution)/shard_map/all_to_all | solution.py:596
  211.1 3.0 %collective-permute-start.2 = (bf16[512,512]{1,0:T(8,128)(2,1)S(1)}, bf16[512,512]{1,0:T(8,128)(2,1)S(1)}, u32[]{:S(2)}, u32[]{:S(2)}) collective-permute-start(bf16[512,512]{1,0:T(8,128)(2,1)S(1)} %copy-done.9), channel_id=1, source_target_pairs={{0,1},{1,0},{2,3},{3,2},{4,5},{5,4},{6,7},{7,6},{8,9},{9,8},{10,11... | collective-permute-start | bytes 1572872 | tf_op jit(solution)/shard_map/ppermute | solution.py:517
  214.1 4.2 %shard_map.217 = (f32[640,256]{1,0:T(8,128)}, bf16[640,256]{1,0:T(8,128)(2,1)}) custom-call(bf16[2,640,256]{2,1,0:T(8,128)(2,1)} %get-tuple-element.79.mine_ref, bf16[2,640,256]{2,1,0:T(8,128)(2,1)} %copy-done.2, bf16[2,640,256]{2,1,0:T(8,128)(2,1)} %copy-done.3, bf16[2,640,256]{2,1,0:T(8,128)(2,1)} %copy-done.4), custom_call_target="tpu_custom_call" | custom-call | bytes 4000000 | tf_op jit(solution)/shard_map/pallas_call | solution.py:101
  218.3 1.1 collective-permute-start.8
  219.4 14.0 %collective-permute-done.8.came_ref = bf16[640,256]{1,0:T(8,128)(2,1)S(1)} collective-permute-done((bf16[640,256]{1,0:T(8,128)(2,1)}, bf16[640,256]{1,0:T(8,128)(2,1)S(1)}, u32[]{:S(2)}, u32[]{:S(2)}) %collective-permute-start.8) | collective-permute-done | bytes 327712 | tf_op jit(solution)/shard_map/ppermute | solution.py:517
  233.4 0.7 copy-done.11
  234.1 3.8 %shard_map.218 = (f32[64,256]{1,0:T(8,128)}, f32[64,256]{1,0:T(8,128)}, f32[256,512]{1,0:T(8,128)}) custom-call(f32[640,256]{1,0:T(8,128)} %get-tuple-element.80.keep_ref, bf16[640,256]{1,0:T(8,128)(2,1)} %copy-done.11), custom_call_target="tpu_custom_call" | custom-call | bytes 2000000 | tf_op jit(solution)/shard_map/pallas_call | solution.py:101
  237.9 0.0 all-to-all-done.5.refs_2_
  237.9 0.8 copy-done.8
  238.7 0.7 copy-done
  239.4 4.4 %shard_map.219 = bf16[1024,512]{1,0:T(8,128)(2,1)} custom-call(f32[512,512]{1,0:T(8,128)} %get-tuple-element.69.refs_0_, bf16[512,512]{1,0:T(8,128)(2,1)} %copy-done.8, bf16[4,512,512]{2,1,0:T(8,128)(2,1)} %copy-done, f32[64,256]{1,0:T(8,128)} %get-tuple-element.82.refs_3_), custom_call_target="tpu_custom_call" | custom-call | bytes 5000000 | tf_op jit(solution)/shard_map/pallas_call | solution.py:101
  (22 shorter events, 0.0 us)
Async XLA Ops:
  6.8 12.7 %collective-permute-start = (f32[8,640]{1,0:T(8,128)}, f32[8,640]{1,0:T(8,128)S(1)}, u32[]{:S(2)}, u32[]{:S(2)}) collective-permute-start(f32[8,640]{1,0:T(8,128)} %get-tuple-element.47), channel_id=1, source_target_pairs={{0,8},{8,16},{16,24},{24,32},{32,40},{40,48},{48,56},{56,64},{64,7... | collective-permute-start | bytes 61448 | tf_op jit(solution)/shard_map/ppermute | solution.py:748
  8.7 9.5 %copy-start.12 = (f32[3,512]{1,0:T(4,128)S(1)}, f32[3,512]{1,0:T(4,128)}, u32[]{:S(2)}) copy-start(f32[3,512]{1,0:T(4,128)} %param.23) | copy-start | bytes 18436
  8.7 9.4 %copy-start.13 = (f32[3,64]{1,0:T(4,128)S(1)}, f32[3,64]{1,0:T(4,128)}, u32[]{:S(2)}) copy-start(f32[3,64]{1,0:T(4,128)} %param.22) | copy-start | bytes 2308
  8.7 9.4 %copy-start.14 = (f32[3,64]{1,0:T(4,128)S(1)}, f32[3,64]{1,0:T(4,128)}, u32[]{:S(2)}) copy-start(f32[3,64]{1,0:T(4,128)} %param.21) | copy-start | bytes 2308
  19.4 0.6 copy-start.15
  28.0 13.1 %all-to-all-start = ((f32[16,40,128]{2,1,0:T(8,128)}), f32[16,40,128]{2,1,0:T(8,128)S(1)}, u32[]{:S(2)}, u32[]{:S(2)}) async-start(f32[16,40,128]{2,1,0:T(8,128)} %bitcast.26), calls=%async_computation | async-start | bytes 655360 | tf_op jit(solution)/shard_map/all_to_all | solution.py:277
  41.0 0.7 copy-start.7
  43.5 12.4 %all-to-all-start.1 = ((f32[16,40,128]{2,1,0:T(8,128)}), f32[16,40,128]{2,1,0:T(8,128)S(1)}, u32[]{:S(2)}, u32[]{:S(2)}) async-start(f32[16,40,128]{2,1,0:T(8,128)} %shard_map.205), calls=%async_computation.1 | async-start | bytes 655360 | tf_op jit(solution)/shard_map/all_to_all | solution.py:282
  55.9 0.7 copy-start.10
  67.8 13.8 %all-to-all-start.2 = ((f32[16,40,128]{2,1,0:T(8,128)}), f32[16,40,128]{2,1,0:T(8,128)S(1)}, u32[]{:S(2)}, u32[]{:S(2)}) async-start(f32[16,40,128]{2,1,0:T(8,128)} %bitcast.25), calls=%async_computation.2 | async-start | bytes 655360 | tf_op jit(solution)/shard_map/all_to_all | solution.py:277
  81.6 0.7 copy-start.6
  84.1 18.3 %all-to-all-start.3 = ((f32[16,40,128]{2,1,0:T(8,128)}), f32[16,40,128]{2,1,0:T(8,128)S(1)}, u32[]{:S(2)}, u32[]{:S(2)}) async-start(f32[16,40,128]{2,1,0:T(8,128)} %shard_map.207), calls=%async_computation.3 | async-start | bytes 655360 | tf_op jit(solution)/shard_map/all_to_all | solution.py:282
  102.4 0.7 copy-start.5
  107.9 10.3 %collective-permute-start.1 = (f32[8,640]{1,0:T(8,128)}, f32[8,640]{1,0:T(8,128)S(1)}, u32[]{:S(2)}, u32[]{:S(2)}) collective-permute-start(f32[8,640]{1,0:T(8,128)} %get-tuple-element.67), channel_id=1, source_target_pairs={{8,0},{16,8},{24,16},{32,24},{40,32},{48,40},{56,48},{64,56},{72,6... | collective-permute-start | bytes 61448 | tf_op jit(solution)/shard_map/ppermute | solution.py:748
  118.2 0.6 copy-start.16
  141.5 8.6 %collective-permute-start.4 = (bf16[8,640,256]{2,1,0:T(8,128)(2,1)}, bf16[8,640,256]{2,1,0:T(8,128)(2,1)S(1)}, u32[]{:S(2)}, u32[]{:S(2)}) collective-permute-start(bf16[8,640,256]{2,1,0:T(8,128)(2,1)} %get-tuple-element.75), channel_id=1, source_target_pairs={{0,8},{8,0},{16,24},{24,16},{32,40},{40,32},{48,56},{56,48},{64,72... | collective-permute-start | bytes 7864328 | tf_op jit(solution)/shard_map/ppermute | solution.py:517
  141.9 55.1 %all-to-all-start.4 = ((bf16[4,2,512,512]{3,2,1,0:T(8,128)(2,1)}), bf16[4,2,512,512]{3,2,1,0:T(8,128)(2,1)}, u32[]{:S(2)}, u32[]{:S(2)}) async-start(bf16[4,2,512,512]{3,2,1,0:T(8,128)(2,1)} %get-tuple-element.68), calls=%async_computation.4 | async-start | bytes 8388608 | tf_op jit(solution)/shard_map/all_to_all | solution.py:596
  147.2 54.1 %collective-permute-start.3 = (bf16[4,512,512]{2,1,0:T(8,128)(2,1)}, bf16[4,512,512]{2,1,0:T(8,128)(2,1)}, u32[]{:S(2)}, u32[]{:S(2)}) collective-permute-start(bf16[4,512,512]{2,1,0:T(8,128)(2,1)} %get-tuple-element.72), channel_id=1, source_target_pairs={{0,1},{1,0},{2,3},{3,2},{4,5},{5,4},{6,7},{7,6},{8,9},{9,8},{10,11... | collective-permute-start | bytes 6291464 | tf_op jit(solution)/shard_map/ppermute | solution.py:517
  150.1 1.5 copy-start.1
  156.9 44.4 %collective-permute-start.5 = (bf16[2,640,256]{2,1,0:T(8,128)(2,1)}, bf16[2,640,256]{2,1,0:T(8,128)(2,1)S(1)}, u32[]{:S(2)}, u32[]{:S(2)}) collective-permute-start(bf16[2,640,256]{2,1,0:T(8,128)(2,1)} %get-tuple-element.76), channel_id=1, source_target_pairs={{0,16},{8,24},{16,32},{24,40},{32,48},{40,56},{48,0},{56,8},{64,80... | collective-permute-start | bytes 1966088 | tf_op jit(solution)/shard_map/ppermute | solution.py:681
  158.4 43.0 %collective-permute-start.6 = (bf16[2,640,256]{2,1,0:T(8,128)(2,1)}, bf16[2,640,256]{2,1,0:T(8,128)(2,1)S(1)}, u32[]{:S(2)}, u32[]{:S(2)}) collective-permute-start(bf16[2,640,256]{2,1,0:T(8,128)(2,1)} %get-tuple-element.77), channel_id=1, source_target_pairs={{0,32},{8,40},{16,48},{24,56},{32,0},{40,8},{48,16},{56,24},{64,96... | collective-permute-start | bytes 1966088 | tf_op jit(solution)/shard_map/ppermute | solution.py:681
  159.1 42.3 %collective-permute-start.7 = (bf16[2,640,256]{2,1,0:T(8,128)(2,1)}, bf16[2,640,256]{2,1,0:T(8,128)(2,1)S(1)}, u32[]{:S(2)}, u32[]{:S(2)}) collective-permute-start(bf16[2,640,256]{2,1,0:T(8,128)(2,1)} %get-tuple-element.78), channel_id=1, source_target_pairs={{0,48},{8,56},{16,0},{24,8},{32,16},{40,24},{48,32},{56,40},{64,11... | collective-permute-start | bytes 1966088 | tf_op jit(solution)/shard_map/ppermute | solution.py:681
  201.3 0.9 copy-start.2
  201.3 1.1 copy-start.3
  201.4 1.3 copy-start.4
  207.3 3.8 %copy-start.9 = (bf16[512,512]{1,0:T(8,128)(2,1)S(1)}, bf16[512,512]{1,0:T(8,128)(2,1)}, u32[]{:S(2)}) copy-start(bf16[512,512]{1,0:T(8,128)(2,1)} %get-tuple-element.70.refs_5_) | copy-start | bytes 1572868
  207.3 30.6 %all-to-all-start.5 = ((bf16[4,512,512]{2,1,0:T(8,128)(2,1)}), bf16[4,512,512]{2,1,0:T(8,128)(2,1)S(1)}, u32[]{:S(2)}, u32[]{:S(2)}) async-start(bf16[4,512,512]{2,1,0:T(8,128)(2,1)} %shard_map.216), calls=%async_computation.5 | async-start | bytes 4194304 | tf_op jit(solution)/shard_map/all_to_all | solution.py:596
  211.1 26.8 %collective-permute-start.2 = (bf16[512,512]{1,0:T(8,128)(2,1)S(1)}, bf16[512,512]{1,0:T(8,128)(2,1)S(1)}, u32[]{:S(2)}, u32[]{:S(2)}) collective-permute-start(bf16[512,512]{1,0:T(8,128)(2,1)S(1)} %copy-done.9), channel_id=1, source_target_pairs={{0,1},{1,0},{2,3},{3,2},{4,5},{5,4},{6,7},{7,6},{8,9},{9,8},{10,11... | collective-permute-start | bytes 1572872 | tf_op jit(solution)/shard_map/ppermute | solution.py:517
  218.3 15.1 %collective-permute-start.8 = (bf16[640,256]{1,0:T(8,128)(2,1)}, bf16[640,256]{1,0:T(8,128)(2,1)S(1)}, u32[]{:S(2)}, u32[]{:S(2)}) collective-permute-start(bf16[640,256]{1,0:T(8,128)(2,1)} %get-tuple-element.81), channel_id=1, source_target_pairs={{0,64},{8,72},{16,80},{24,88},{32,96},{40,104},{48,112},{56,120},{... | collective-permute-start | bytes 983048 | tf_op jit(solution)/shard_map/ppermute | solution.py:517
  233.4 0.7 copy-start.11
  237.9 0.8 copy-start.8
  237.9 1.5 copy-start
